TPU v7x, 32 devices: a whole 2x2x4 slice. The times are simulated.
32 devices in a mesh: group: 4 (over z), table: 8 (over y, x, core).
Axes of the slice: x: 2, y: 2, z: 4, core: 2. Of those that a mesh axis runs over, the one named last changes fastest.
Arguments:
- table: float32 [128, 2048, 128], P('table'), may hold values from -0.36 to 0.36
- accum: float32 [128, 2048], P('table'), may hold values from 0.05 to 2
- w_hidden: bfloat16 [128, 128, 128], replicated, may hold values from -0.5 to 0.5
- w_out: float32 [128], replicated, may hold values from -1.8 to 1.8
- ids: int32 [128, 8, 4096], P('table', None, 'group'), may hold values from 0 to 2047, as said below
- labels: float32 [4096], P(('group', 'table')), may hold values from 0 to 1, as said below
- touched: int32 [128, 512], P('table'), may hold values from 0 to 2047, as said below
- row_noise: float32 [128, 512, 128], P('table'), may hold values from -1.8 to 1.8
- dense_noise: float32 [128, 128, 128], P('table', 'group'), may hold values from -3.6 to 3.6
Outputs:
- new_table: float32 [128, 2048, 128], P('table')
- new_accum: float32 [128, 2048], P('table')
- dense_grad: float32 [128, 128, 128], P('table', 'group')
Inputs may be any that keep to these rules, and one draw needn't show every extreme that they name: `touched`: for each feature, 512 different rows of that feature's table. `ids`: every id of feature f is one of the rows listed for f in touched. `labels`: each target is 0 or 1.
All inputs are finite; a program needn't handle non-finite values.
Results may differ from a plain program's by a relative error of at most 0.003.
Values may be sent and summed in bfloat16 or wider, within the bound.
No kernel may reach another device: no remote copies, remote signals or barrier semaphores. Data moves between devices by JAX's collectives and lax.ppermute only.
A program may use at most 128 MiB of HBM per device.

v0:
```python
import math

import jax
import jax.numpy as jnp
from jax import lax
from jax.sharding import PartitionSpec as P

CLIP = 1.0
LEARN = 0.05


def silu_slope(pre):
    gate = jax.nn.sigmoid(pre)
    return gate * (1.0 + pre * (1.0 - gate))


def pick_rows(source, where):
    return source[where]


def put_rows(target, where, values):
    return target.at[where].set(values)


def count_hits(ids, start, block, rows_f):
    bags = lax.dynamic_slice_in_dim(ids, start, block, 2)
    slots = lax.broadcasted_iota(jnp.int32, (1, 1, rows_f), 2)
    total = jnp.zeros((ids.shape[0], block, rows_f), jnp.bfloat16)
    for position in range(ids.shape[1]):
        total = total + (bags[:, position, :, None] == slots).astype(jnp.bfloat16)
    return total


def body(table, accum, w_hidden, w_out, ids, labels, touched, row_noise, dense_noise):
    f_dev, rows_f, width = table.shape
    b_group = ids.shape[2]
    b_dev = labels.shape[0]
    features = w_hidden.shape[0]
    hidden = w_hidden.shape[2]
    block = math.gcd(b_group, 512)
    block_count = b_group // block
    offset = lax.axis_index("table") * b_dev
    table_low = table.astype(jnp.bfloat16)

    def pool_block(number):
        counts = count_hits(ids, number * block, block, rows_f)
        return jnp.einsum("fbr,fre->bfe", counts, table_low, preferred_element_type=jnp.float32)

    pooled = lax.map(pool_block, jnp.arange(block_count, dtype=jnp.int32))
    pooled = pooled.reshape(b_group, f_dev, width).astype(jnp.bfloat16)
    repeats = jnp.sum((ids[:, :, None, :] == ids[:, None, :, :]).astype(jnp.float32), axis=(1, 2))
    gathered = lax.all_to_all(pooled, "table", split_axis=0, concat_axis=1, tiled=True)
    flat = gathered.reshape(b_dev, features * width)
    w_flat = w_hidden.reshape(features * width, hidden)
    pre = jnp.dot(flat, w_flat, preferred_element_type=jnp.float32)
    logit = jnp.sum(jax.nn.silu(pre) * w_out, axis=1)
    prob = jax.nn.sigmoid(logit)
    delta = silu_slope(pre) * w_out * (prob - labels)[:, None]
    delta_low = delta.astype(jnp.bfloat16)
    grad_pool = lax.dot_general(
        delta_low, w_flat, (((1,), (1,)), ((), ())), preferred_element_type=jnp.float32
    )
    grad_pool = grad_pool.astype(jnp.bfloat16).reshape(b_dev, features, width)
    dense_sq = jnp.sum(jnp.square(flat.astype(jnp.float32)), axis=1) * jnp.sum(
        delta * delta, axis=1
    )
    returned = lax.all_to_all(grad_pool, "table", split_axis=1, concat_axis=0, tiled=True)
    grad_sq = jnp.sum(jnp.square(returned.astype(jnp.float32)), axis=2)
    embed_part = jnp.sum(repeats.T * grad_sq, axis=1)
    dense_part = lax.dynamic_update_slice_in_dim(
        jnp.zeros((b_group,), jnp.float32), dense_sq, offset, 0
    )
    totals = lax.psum(embed_part + dense_part, "table")
    factor_all = CLIP / jnp.maximum(jnp.sqrt(totals), CLIP)
    factor_own = lax.dynamic_slice_in_dim(factor_all, offset, b_dev, 0)
    arrived = (factor_all[:, None, None] * returned.astype(jnp.float32)).astype(jnp.bfloat16)
    clip_rows = (factor_own[:, None] * delta).astype(jnp.bfloat16)
    group_sum = lax.psum_scatter(
        jnp.einsum("bfe,bh->feh", gathered, clip_rows, preferred_element_type=jnp.float32).astype(
            jnp.bfloat16
        ),
        "table",
        scatter_dimension=0,
        tiled=True,
    )
    dense_sum = lax.psum_scatter(group_sum, "group", scatter_dimension=1, tiled=True).astype(
        jnp.float32
    )
    dense_grad = dense_sum + dense_noise

    def add_block(number, total):
        counts = count_hits(ids, number * block, block, rows_f)
        rows_now = lax.dynamic_slice_in_dim(arrived, number * block, block, 0)
        return total + jnp.einsum(
            "fbr,bfe->fre", counts, rows_now, preferred_element_type=jnp.float32
        )

    grads = lax.fori_loop(0, block_count, add_block, jnp.zeros((f_dev, rows_f, width), jnp.float32))
    summed = lax.psum(grads.astype(jnp.bfloat16), "group").astype(jnp.float32)
    listed = jax.vmap(pick_rows)(summed, touched)
    listed = listed + row_noise
    new_acc = jax.vmap(pick_rows)(accum, touched) + jnp.mean(listed * listed, axis=2)
    new_rows = jax.vmap(pick_rows)(table, touched) - LEARN * listed / jnp.sqrt(new_acc)[:, :, None]
    new_table = jax.vmap(put_rows)(table, touched, new_rows)
    new_accum = jax.vmap(put_rows)(accum, touched, new_acc)
    return (new_table, new_accum, dense_grad)


def solution(mesh):
    in_specs = (
        P("table", None, None),
        P("table", None),
        P(),
        P(),
        P("table", None, "group"),
        P(("group", "table")),
        P("table", None),
        P("table", None, None),
        P("table", "group", None),
    )
    out_specs = (P("table", None, None), P("table", None), P("table", "group", None))
    return jax.shard_map(body, mesh=mesh, in_specs=in_specs, out_specs=out_specs, check_vma=False)
```

profile of v0, /device:TPU:0, one launch (start us, length us, event | category | flops | bytes accessed | tf_op | source)
XLA Modules:
  0.0 1021.1 jit_solution(562513984759428996)
XLA Ops:
  7.2 11.4 %copy.94 = f32[16,2048,128]{2,1,0:T(8,128)} copy(f32[16,2048,128]{2,1,0:T(8,128)} %param.13) | data formatting | bytes 33554432
  18.6 9.0 convert_element_type.139
  27.9 150.4 %while.24 = (s32[]{:T(128)}, bf16[2,512,16,128]{3,2,1,0:T(8,128)(2,1)}, s32[2]{0:T(128)S(1)}, s32[16,8,1024]{2,0,1:T(8,128)S(1)}, bf16[16,2048,128]{2,1,0:T(8,12...) while((s32[]{:T(128)}, ...), condition=%wide.region_2.3_spmd, body=%wide.region_1.2_spmd.sunk | while | flops 4831838208 | bytes 15467331 | solution.py:49
  29.2 71.2 %fusion.96 = bf16[1,512,16,128]{3,1,2,0:T(8,128)(2,1)S(1)} fusion(bf16[16,2048,128]{2,1,0:T(8,128)(2,1)} %get-tuple-element.333, s32[16,512]{1,0:T(8,128)S(1)} %get-tuple-element.277, s32[16,512]{1,0:T(8,128)S(1)} %get-tuple-element.278, s32[16,512]{1,0:T(8,128)S(1)} %get-tuple-element.279, s32[16,512]{1,0:T(8,128)S(1)} %get-tuple-element.280, ...), kind=kOutput, calls=%fused_computation.38.clone.2 | convolution fusion | flops 4831838208 | bytes 10747904 | tf_op jit(solution)/shard_map/while/body/eval_jaxpr/fbr,fre->bfe/dot_general | solution.py:47
  104.4 71.2 %fusion.96 = bf16[1,512,16,128]{3,1,2,0:T(8,128)(2,1)S(1)} fusion(bf16[16,2048,128]{2,1,0:T(8,128)(2,1)} %get-tuple-element.333, s32[16,512]{1,0:T(8,128)S(1)} %get-tuple-element.277, s32[16,512]{1,0:T(8,128)S(1)} %get-tuple-element.278, s32[16,512]{1,0:T(8,128)S(1)} %get-tuple-element.279, s32[16,512]{1,0:T(8,128)S(1)} %get-tuple-element.280, ...), kind=kOutput, calls=%fused_computation.38.clone.2 | convolution fusion | flops 4831838208 | bytes 10747904 | tf_op jit(solution)/shard_map/while/body/eval_jaxpr/fbr,fre->bfe/dot_general | solution.py:47
  178.3 54.5 %all_to_all.27 = bf16[1024,16,128]{2,1,0:T(8,128)(2,1)} all-to-all(bf16[1024,16,128]{2,1,0:T(8,128)(2,1)} %bitcast.15), channel_id=1, replica_groups=mesh['group'=4,'table'=8] {'table'}, dimensions={0} | all-to-all | bytes 8388608 | tf_op jit(solution)/shard_map/all_to_all | solution.py:52
  232.8 6.8 copy.43
  239.6 5.0 multiply_reduce_fusion.5
  258.1 44.8 %all-to-all-done.1 = bf16[128,128,128]{2,0,1:T(8,128)(2,1)} async-done(((bf16[128,128,128]{2,0,1:T(8,128)(2,1)}), bf16[128,128,128]{2,0,1:T(8,128)(2,1)}, u32[]{:S(2)}, u32[]{:S(2)}) %all-to-all-start.1) | async-done | bytes 4194336 | tf_op jit(solution)/shard_map/all_to_all | solution.py:67
  307.5 11.8 %psum.14 = f32[1024]{0:T(1024)S(1)} all-reduce(f32[1024]{0:T(1024)S(1)} %add_dynamic-update-slice_fusion), channel_id=1, replica_groups=mesh['group'=4,'table'=8] {'table'}, use_global_device_ids=true, to_apply=%region_8.9 | all-reduce | flops 1024 | bytes 8192 | tf_op jit(solution)/shard_map/psum | solution.py:73
  319.4 5.6 convolution_convert_fusion.1
  332.4 45.1 %reduce-scatter.3.cloned.1.call-done = bf16[16,128,128]{2,1,0:T(8,128)(2,1)} async-done(((bf16[128,128,128]{2,1,0:T(8,128)(2,1)}), bf16[16,128,128]{2,1,0:T(8,128)(2,1)}) %reduce-scatter.3.cloned.1.call-update) | async-done | bytes 524304 | tf_op jit(solution)/shard_map/reduce_scatter | solution.py:78
  377.8 131.8 %while.25 = (s32[]{:T(128)}, f32[16,2048,128]{2,1,0:T(8,128)}, s32[16,8,1024]{2,0,1:T(8,128)S(1)}, bf16[1024,16,128]{2,0,1:T(8,128)(2,1)}, s32[]{:T(128)}, /*ind...) while((s32[]{:T(128)}, f32[16,2048,128]{2,1,0:T(8,128)}, ...), condition=%wide.region_10.11_spmd.clone, body=%wide.region_9.10_spmd.clone.sunk | while | flops 4840226816 | bytes 36438332 | solution.py:98
  377.8 65.5 %select_add_fusion.2 = f32[16,2048,128]{2,1,0:T(8,128)} fusion(f32[16,2048,128]{2,1,0:T(8,128)} %get-tuple-element.361, pred[]{:T(512)S(6)} %compare.9, s32[16,512]{1,0:T(8,128)S(1)} %get-tuple-element.289, s32[16,512]{1,0:T(8,128)S(1)} %get-tuple-element.290, s32[16,512]{1,0:T(8,128)S(1)} %get-tuple-element.291, ...), kind=kOutput, calls=%fused_computation.79.clone.1 | convolution fusion | flops 4840226816 | bytes 35913732 | tf_op jit(solution)/shard_map/while/body/eval_jaxpr/fbr,bfe->fre/dot_general | solution.py:94
  443.3 66.2 %select_add_fusion.2 = f32[16,2048,128]{2,1,0:T(8,128)} fusion(f32[16,2048,128]{2,1,0:T(8,128)} %get-tuple-element.361, pred[]{:T(512)S(6)} %compare.9, s32[16,512]{1,0:T(8,128)S(1)} %get-tuple-element.289, s32[16,512]{1,0:T(8,128)S(1)} %get-tuple-element.290, s32[16,512]{1,0:T(8,128)S(1)} %get-tuple-element.291, ...), kind=kOutput, calls=%fused_computation.79.clone.1 | convolution fusion | flops 4840226816 | bytes 35913732 | tf_op jit(solution)/shard_map/while/body/eval_jaxpr/fbr,bfe->fre/dot_general | solution.py:94
  509.5 9.0 convert_element_type.151
  519.4 126.5 %gather_fusion = f32[8192,128]{1,0:T(8,128)} fusion(f32[16,2048,128]{2,1,0:T(8,128)} %copy.94, s32[8192]{0:T(1024)S(1)} %bitcast.110), kind=kCustom, calls=%fused_computation | custom fusion | bytes 8454144 | tf_op jit(solution)/shard_map/vmap()/gather | solution.py:18
  645.9 65.0 %gather_fusion.2 = f32[8192]{0:T(1024)S(1)} fusion(f32[16,2048]{1,0:T(8,128)S(1)} %copy-done, s32[8192]{0:T(1024)S(1)} %bitcast.111), kind=kCustom, calls=%fused_computation.2 | custom fusion | bytes 131072 | tf_op jit(solution)/shard_map/vmap()/gather | solution.py:18
  712.9 96.7 %all-reduce.2.cloned.1.call-done = bf16[16,2048,128]{2,1,0:T(8,128)(2,1)} async-done(((bf16[16,2048,128]{2,1,0:T(8,128)(2,1)}), bf16[16,2048,128]{2,1,0:T(8,128)(2,1)}) %all-reduce.2.cloned.1.call-update) | async-done | bytes 8388624 | tf_op jit(solution)/shard_map/psum | solution.py:99
  809.6 10.8 %convert_element_type.152 = f32[16,2048,128]{2,1,0:T(8,128)} convert(bf16[16,2048,128]{2,1,0:T(8,128)(2,1)} %all-reduce.2.cloned.1.call-done) | non-fusion elementwise | flops 4194304 | bytes 25165824 | tf_op jit(solution)/shard_map/convert_element_type | solution.py:99
  820.4 118.5 %gather_fusion.1 = f32[8192,128]{1,0:T(8,128)} fusion(f32[16,2048,128]{2,1,0:T(8,128)} %convert_element_type.152, s32[8192]{0:T(1024)S(1)} %bitcast.112), kind=kCustom, calls=%fused_computation.1 | custom fusion | bytes 8454144 | tf_op jit(solution)/shard_map/vmap()/gather | solution.py:18
  943.6 30.5 %scatter_fusion.1 = f32[32768]{0:T(1024)S(1)} fusion(f32[32768]{0:T(1024)S(1)} %bitcast.108, s32[8192]{0:T(1024)S(1)} %bitcast.126, f32[8192]{0:T(1024)S(1)} %bitcast.129), kind=kCustom, calls=%fused_computation.4 | custom fusion | bytes 131072
  974.8 7.0 divide_subtract_fusion
  981.8 32.7 %scatter_fusion = f32[32768,128]{1,0:T(8,128)} fusion(f32[32768,128]{1,0:T(8,128)} %bitcast.113, s32[8192]{0:T(1024)S(1)} %bitcast.127, f32[8192,128]{1,0:T(8,128)} %bitcast.125), kind=kCustom, calls=%fused_computation.3 | custom fusion | bytes 12615680
  (69 shorter events, 40.8 us)
Async XLA Ops:
  18.6 9.0 copy-start.2
  178.3 61.3 %copy-start.6 = (f32[128]{0:T(128)S(1)}, f32[128]{0:T(128)}, u32[]{:S(2)}) copy-start(f32[128]{0:T(128)} %param.16) | copy-start | bytes 1540
  232.8 11.8 %copy-start.9 = (f32[128]{0:T(128)S(1)}, f32[128]{0:T(128)}, u32[]{:S(2)}) copy-start(f32[128]{0:T(128)} %param.18) | copy-start | bytes 1540
  239.6 5.0 copy-start.1
  246.0 8.0 copy-start.3
  249.2 53.7 %all-to-all-start.1 = ((bf16[128,128,128]{2,0,1:T(8,128)(2,1)}), bf16[128,128,128]{2,0,1:T(8,128)(2,1)}, u32[]{:S(2)}, u32[]{:S(2)}) async-start(bf16[128,128,128]{2,0,1:T(8,128)(2,1)} %bitcast.124), calls=%async_computation.1 | async-start | bytes 8388608 | tf_op jit(solution)/shard_map/all_to_all | solution.py:67
  253.7 123.8 %reduce-scatter.3.cloned.1.call-start = ((), (), s32[]{:S(2)}) async-start(), calls=%async_computation.5 | async-start | bytes 4718592 | tf_op jit(solution)/shard_map/reduce_scatter | solution.py:78
  324.9 386.3 %reduce-scatter.5.cloned.1.call-start = ((), (), s32[]{:S(2)}) async-start(), calls=%async_computation.6 | async-start | bytes 655360 | tf_op jit(solution)/shard_map/reduce_scatter | solution.py:86
  377.5 432.1 %all-reduce.2.cloned.1.call-start = ((), (), s32[]{:S(2)}) async-start(), calls=%async_computation.4 | async-start | bytes 16777216 | tf_op jit(solution)/shard_map/psum | solution.py:99
  518.6 0.8 copy-start.5
  519.4 126.5 %copy-start = (f32[16,2048]{1,0:T(8,128)S(1)}, f32[16,2048]{1,0:T(8,128)}, u32[]{:S(2)}) copy-start(f32[16,2048]{1,0:T(8,128)} %param.14) | copy-start | bytes 393220
  645.9 65.1 %copy-start.8 = (s32[2]{0:T(128)S(1)}, s32[2]{0:T(128)}, u32[]{:S(2)}) copy-start(s32[2]{0:T(128)} %constant.70) | copy-start | bytes 28
  645.9 65.2 %copy-start.7 = (s32[2]{0:T(128)S(1)}, s32[2]{0:T(128)}, u32[]{:S(2)}) copy-start(s32[2]{0:T(128)} %constant.73) | copy-start | bytes 28
  645.9 65.3 %copy-start.4 = (f32[16,32,128]{2,1,0:T(8,128)S(1)}, f32[16,32,128]{2,1,0:T(8,128)}, u32[]{:S(2)}) copy-start(f32[16,32,128]{2,1,0:T(8,128)} %param.21) | copy-start | bytes 786436
Sparse Core Ops, SparseCore 0:
  325.1 52.3 reduce-scatter.2
  379.9 21.5 reduce-scatter.4
  518.7 290.7 all-reduce.1
where the time goes:
time: 1020 us
  local copies, waits for them, and re-layouts  404 us (40%)
  matrix products  286 us (28%)
  waiting for transfers between devices  187 us (18%)
  blocking collectives  66.2 us (6%)
  other arithmetic  57.4 us (6%)
  between operations  14 us (1%)
    gather x4, local copies, waits for them, and re-layouts, pick_rows(): return source[where]  310 us
    dot_general x2, matrix products, pool_block(): jnp.einsum('fbr,fre->bfe', counts, table_low, preferred_element_type=jnp....  142 us
    dot_general x2, matrix products, add_block(): jnp.einsum('fbr,bfe->fre', counts, rows_now, preferred_element_type=jnp.f...  132 us
    psum x1, waiting for transfers between devices, body(): summed = lax.psum(grads.astype(jnp.bfloat16), 'group').astype(jnp.float32)  96.7 us
    unnamed x28, local copies, waits for them, and re-layouts  75.8 us
    all_to_all x1, blocking collectives, body(): lax.all_to_all(pooled, 'table', split_axis=0, concat_axis=1, tiled=True)  54.5 us
    reduce_scatter x1, waiting for transfers between devices, body(): lax.psum_scatter(jnp.einsum('bfe,bh->feh', gathered, clip_rows, preferred...  45.1 us
    all_to_all x1, waiting for transfers between devices, body(): lax.all_to_all(grad_pool, 'table', split_axis=1, concat_axis=0, tiled=True)  44.8 us
  transfers between devices with their start and end apart: 4, of which 3 were waited for; matrix products, arithmetic and copies ran while one was open for 34% of the time, Pallas kernels for 0%

commit v1 on v0

v1 whole, which is shorter than its diff:
```python
import functools

import jax
import jax.numpy as jnp
from jax import lax
from jax.experimental import pallas as pl
from jax.experimental.pallas import tpu as pltpu
from jax.sharding import PartitionSpec as P

CLIP = 1.0
LEARN = 0.05
LANES = 128
DIGITS = 4
HALF = 16
BLOCK = 1024
BATCH = 32
PAIR = 2
LISTED = 16
MIB = 1 << 20

NT = (((1,), (1,)), ((), ()))
TN = (((0,), (0,)), ((), ()))


def dot(left, right, dims=(((1,), (0,)), ((), ())), precision=None):
    return lax.dot_general(
        left, right, dims, preferred_element_type=jnp.float32, precision=precision
    )


def iota(shape, axis):
    return lax.broadcasted_iota(jnp.int32, shape, axis)


def slot_words(touched_row, rows_f):
    count = touched_row.shape[1]
    low = count // DIGITS
    tall = rows_f // LANES
    slot = iota((1, count), 1)
    rows = jnp.where((touched_row >> 7) == iota((tall, count), 0), 1.0, 0.0)
    lanes = jnp.where((touched_row & (LANES - 1)) == iota((LANES, count), 0), 1.0, 0.0)
    values = (lax.rem(slot, low), LISTED + 4 * lax.div(slot, low))
    held = jnp.concatenate([rows * value.astype(jnp.float32) for value in values], axis=0)
    parts = dot(held.astype(jnp.bfloat16), lanes.astype(jnp.bfloat16), NT).astype(jnp.int32)
    word = parts[:tall] | (parts[tall:] << 8)
    return word[: tall // 2] | (word[tall // 2 :] << HALF)


def pick_lanes(lines, row, lane):
    found = jnp.zeros(row.shape, lines[0].dtype)
    for number, line in enumerate(lines):
        got = jnp.take_along_axis(jnp.broadcast_to(line, row.shape), lane, axis=1)
        found = jnp.where(row == number, got, found)
    return found


def look_up(lines, ids, slots, where):
    word = pick_lanes(lines, (ids >> 7) & (len(lines) - 1), ids & (LANES - 1))
    upper = ids >= len(lines) * LANES
    word = jnp.where(upper, lax.shift_right_logical(word, HALF), word) & 0xFFFF
    slots[0, :, where] = word & 0xFF
    slots[1, :, where] = jnp.left_shift(jnp.ones_like(word), (word >> 8) & (LISTED - 1))


def places(low):
    shape = (low // HALF, HALF, LANES)
    return (iota(shape, 0) * HALF + iota(shape, 1)).astype(jnp.int16)


def tally(place, slots, where):
    total = jnp.zeros(place.shape, jnp.int16)
    nothing = jnp.zeros(place.shape, jnp.int16)
    wide = (HALF, LANES)
    for hot in range(slots.shape[1]):
        one_group = jnp.broadcast_to(slots[0, hot : hot + 1, where], wide).astype(jnp.int16)
        one_code = jnp.broadcast_to(slots[1, hot : hot + 1, where], wide).astype(jnp.int16)
        hit = place == jnp.broadcast_to(one_group[None], place.shape)
        total = total + jnp.where(hit, jnp.broadcast_to(one_code[None], place.shape), nothing)
    return total.reshape(-1, LANES)


def spread(codes):
    parts = []
    for digit in range(DIGITS):
        if digit < DIGITS - 1:
            part = codes & jnp.full(codes.shape, 15 << (4 * digit), jnp.int16)
        else:
            part = lax.shift_right_logical(codes, jnp.full(codes.shape, 4 * digit, jnp.int16))
        parts.append(part.astype(jnp.bfloat16))
    return jnp.concatenate(parts, axis=0)


def scale(digit):
    return float(16**digit if digit < DIGITS - 1 else 1)


def pool_kernel(own_ref, listed_ref, table_ref, touched_ref, ids_ref, w_ref, *rest):
    sent_refs, (rows_ref, words_ref, codes_ref, picked, sums, same, slots) = rest[:-7], rest[-7:]
    step = pl.program_id(0)
    rows_f, width = table_ref.shape[1:]
    hots, b_group = ids_ref.shape[1:]
    count = touched_ref.shape[1]
    low = count // DIGITS
    hidden = w_ref.shape[2]
    blocks, tall, chunk = sums.shape
    block = min(b_group, BLOCK)
    place = places(low)

    @pl.when(step == 0)
    def _():
        sums[...] = jnp.zeros_like(sums)
        same[...] = jnp.zeros_like(same)

    features = range(PAIR)
    lines = []
    for side in features:
        words = slot_words(touched_ref[pl.ds(step * PAIR + side, 1)], rows_f)
        words_ref[side] = words
        lines.append([words[number : number + 1] for number in range(words.shape[0])])
    for start in range(0, count, BATCH):
        for side in features:
            batch = range(start, start + BATCH)
            listed = [listed_ref[step * PAIR + side, slot] for slot in batch]
            rows = [table_ref[side, pl.ds(row, 1), :] for row in listed]
            for slot, row in zip(batch, rows):
                picked[side, slot : slot + 1, :] = row
    rows_t, w_t = [], []
    for side in features:
        whole = picked[side].astype(jnp.bfloat16).T
        rows_ref[side] = whole
        parts = [
            whole[:, digit * low : (digit + 1) * low] * jnp.bfloat16(1 / scale(digit))
            for digit in range(DIGITS)
        ]
        rows_t.append(jnp.concatenate(parts, axis=1))
        w_t.append(w_ref[side].T)

    def one_block(number):
        for inner in range(0, block, chunk):
            for side in features:
                where = pl.ds(pl.multiple_of(number * block + inner, chunk), chunk)
                ids = ids_ref[side, :, where]
                look_up(lines[side], ids, slots.at[side], slice(inner, inner + chunk))
                pairs = jnp.zeros(ids.shape, jnp.float32)
                for turn in range(1, hots // 2 + 1):
                    weight = 2.0 if turn < hots // 2 else 1.0
                    pairs = pairs + jnp.where(ids == pltpu.roll(ids, turn, 0), weight, 0.0)
                pairs = jnp.sum(pairs, axis=0, keepdims=True) + hots
                part = number * (block // chunk) + inner // chunk
                same[part, pl.ds(step * PAIR + side, 1)] = pairs
        for inner in range(0, block, 2 * chunk):
            pre, square = 0.0, 0.0
            for side in features:
                parts = []
                for start in (inner, inner + chunk):
                    codes = tally(place, slots.at[side], slice(start, start + chunk))
                    where = pl.ds(pl.multiple_of(number * block + start, chunk), chunk)
                    codes_ref[side, :, where] = codes
                    parts.append(spread(codes))
                pooled = dot(rows_t[side], jnp.concatenate(parts, axis=1)).astype(jnp.bfloat16)
                wide = pooled.astype(jnp.float32)
                square += jnp.sum((wide * wide).reshape(width // HALF, HALF, 2 * chunk), axis=0)
                pre += dot(w_t[side], pooled)
            for turn in range(2):
                part = number * (block // chunk) + inner // chunk + turn
                lanes = slice(turn * chunk, (turn + 1) * chunk)
                sums[part, :hidden] += pre[:, lanes]
                sums[part, hidden:] += square[:, lanes]

    each(b_group // block, one_block)

    @pl.when(step == pl.num_programs(0) - 1)
    def _():
        for apart, sent_ref in enumerate(sent_refs):
            part = own_ref[0] ^ apart
            sent_ref[:tall] = sums[part].astype(jnp.bfloat16)
            sent_ref[tall:] = same[part].astype(jnp.bfloat16)


def each(times, step):
    if times == 1:
        step(0)
    else:

        @pl.loop(0, times)
        def _(number):
            step(number)


def pool(own, table, touched, ids, w_hidden, chunk):
    f_dev, rows_f, width = table.shape
    hots, b_group = ids.shape[1:]
    count = touched.shape[1]
    hidden = w_hidden.shape[2]
    blocks = b_group // chunk
    repeat_rows = -(-f_dev // HALF) * HALF
    tall = hidden + HALF
    sent = (tall + repeat_rows, chunk)

    def now(*shape):
        return pl.BlockSpec((PAIR,) + shape, lambda i, o, s: (i, 0, 0))

    low = count // DIGITS
    outs = pl.pallas_call(
        pool_kernel,
        grid_spec=pltpu.PrefetchScalarGridSpec(
            num_scalar_prefetch=2,
            grid=(f_dev // PAIR,),
            in_specs=[
                now(rows_f, width),
                pl.BlockSpec(touched.shape, lambda i, o, s: (0, 0)),
                now(hots, b_group),
                pl.BlockSpec(
                    (PAIR, width, hidden), lambda i, o, s: (o[0] * (f_dev // PAIR) + i, 0, 0)
                ),
            ],
            out_specs=[pl.BlockSpec(sent, lambda i, o, s: (0, 0))] * blocks
            + [now(width, count), now(rows_f // 256, LANES), now(low, b_group)],
            scratch_shapes=[
                pltpu.VMEM((PAIR, count, width), jnp.float32),
                pltpu.VMEM((blocks, tall, chunk), jnp.float32),
                pltpu.VMEM((blocks, repeat_rows, chunk), jnp.float32),
                pltpu.VMEM((PAIR, 2, hots, min(b_group, BLOCK)), jnp.int32),
            ],
        ),
        out_shape=[jax.ShapeDtypeStruct(sent, jnp.bfloat16)] * blocks
        + [
            jax.ShapeDtypeStruct((f_dev, width, count), jnp.bfloat16),
            jax.ShapeDtypeStruct((f_dev, rows_f // 256, LANES), jnp.int32),
            jax.ShapeDtypeStruct((f_dev, low, b_group), jnp.int16),
        ],
        compiler_params=pltpu.CompilerParams(vmem_limit_bytes=56 * MIB),
        cost_estimate=pl.CostEstimate(
            flops=2 * f_dev * count * b_group * width * 8,
            bytes_accessed=table.size * 4,
            transcendentals=0,
        ),
        name="pool",
    )(own, touched, table, touched, ids, w_hidden)
    return outs[:-3], *outs[-3:]


def code_kernel(place_ref, lower_ref, upper_ref, ids_ref, *rest):
    codes_ref, slots = rest[-2:]
    low, b_group = codes_ref.shape[2:]
    block = min(b_group, BLOCK)
    place = places(low)
    lines = [
        [words_ref[0, number : number + 1] for number in range(words_ref.shape[1])]
        for words_ref in (lower_ref, upper_ref)
    ]

    def one_block(number):
        for inner in range(0, block, LANES):
            where = pl.ds(pl.multiple_of(number * block + inner, LANES), LANES)
            packed = ids_ref[0, 0, :, where]
            for half, ids in enumerate((packed & 0xFFFF, packed >> HALF)):
                look_up(lines[half], ids, slots.at[half], slice(inner, inner + LANES))
        for inner in range(0, block, LANES):
            where = pl.ds(pl.multiple_of(number * block + inner, LANES), LANES)
            for half in range(2):
                codes_ref[half, 0, :, where] = tally(
                    place, slots.at[half], slice(inner, inner + LANES)
                )

    each(b_group // block, one_block)


def code_counts(own, words, packed, low, start, stop, before=None):
    groups, half, hots, b_group = packed.shape
    others = groups - 1
    size = (stop - start) * 2 * low * others * b_group
    kept = () if before is None else (before,)
    return pl.pallas_call(
        code_kernel,
        grid_spec=pltpu.PrefetchScalarGridSpec(
            num_scalar_prefetch=1,
            grid=(stop - start, others),
            in_specs=[
                pl.BlockSpec((1,) + words.shape[1:], lambda f, g, o: (f + start, 0, 0)),
                pl.BlockSpec((1,) + words.shape[1:], lambda f, g, o: (f + start + half, 0, 0)),
                pl.BlockSpec(
                    (1, 1, hots, b_group), lambda f, g, o: (o[0] ^ (g + 1), f + start, 0, 0)
                ),
            ]
            + [pl.BlockSpec(memory_space=pl.ANY)] * len(kept),
            out_specs=pl.BlockSpec((2, 1, low, b_group), lambda f, g, o: (0, f + start, 0, g)),
            scratch_shapes=[pltpu.VMEM((2, 2, hots, min(b_group, BLOCK)), jnp.int32)],
        ),
        out_shape=jax.ShapeDtypeStruct((2, half, low, others * b_group), jnp.int16),
        input_output_aliases={4: 0} if kept else {},
        compiler_params=pltpu.CompilerParams(vmem_limit_bytes=48 * MIB),
        cost_estimate=pl.CostEstimate(
            flops=size * 400, bytes_accessed=size * 2, transcendentals=0
        ),
        name="code",
    )(own, words, words, packed, *kept)


def clip_kernel(own_ref, w_out_ref, labels_ref, w_ref, *rest):
    sent_refs, clip_ref = rest[:-1], rest[-1]
    features, width, hidden = w_ref.shape
    share = features // len(sent_refs)
    tall = hidden + HALF
    own = own_ref[0]

    w_out = w_out_ref[...]
    red = sent_refs[0][:tall].astype(jnp.float32)
    for sent_ref in sent_refs[1:]:
        red = red + sent_ref[:tall].astype(jnp.float32)
    pre = red[:hidden]
    flat_sq = jnp.sum(red[hidden:], axis=0, keepdims=True)
    gate = jax.nn.sigmoid(pre)
    logit = jnp.sum(pre * gate * w_out, axis=0, keepdims=True)
    miss = jax.nn.sigmoid(logit) - labels_ref[...]
    delta = gate * (1.0 + pre * (1.0 - gate)) * w_out * miss
    delta_low = delta.astype(jnp.bfloat16)
    lanes = pre.shape[1]

    total = jnp.zeros((8, lanes), jnp.float32)
    for apart, sent_ref in enumerate(sent_refs):
        w_part = w_ref[pl.ds((own ^ apart) * share, share)].reshape(share * width, hidden)
        grad = dot(w_part, delta_low)
        square = jnp.sum((grad * grad).reshape(share, width // 8, 8, lanes), axis=1)
        repeats = sent_ref[tall:].astype(jnp.float32)
        for inner in range(share):
            total = total + square[inner] * repeats[inner : inner + 1]
    norm_sq = jnp.sum(total, axis=0, keepdims=True)
    norm_sq = norm_sq + flat_sq * jnp.sum(delta * delta, axis=0, keepdims=True)
    factor = CLIP / jnp.maximum(jnp.sqrt(norm_sq), CLIP)
    clip_ref[...] = (factor * delta).T.astype(jnp.bfloat16)


def clip_rows(own, sent, w_out, labels, w_hidden):
    features, width, hidden = w_hidden.shape
    b_dev = labels.shape[0]
    vmem = pl.BlockSpec(memory_space=pltpu.VMEM)
    return pl.pallas_call(
        clip_kernel,
        in_specs=[pl.BlockSpec(memory_space=pltpu.SMEM)] + [vmem] * (3 + len(sent)),
        out_specs=vmem,
        out_shape=jax.ShapeDtypeStruct((b_dev, hidden), jnp.bfloat16),
        compiler_params=pltpu.CompilerParams(vmem_limit_bytes=32 * MIB),
        cost_estimate=pl.CostEstimate(
            flops=2 * features * width * hidden * b_dev,
            bytes_accessed=w_hidden.size * 2,
            transcendentals=b_dev * hidden,
        ),
        name="clip",
    )(own, w_out.reshape(hidden, 1), labels.reshape(1, b_dev), w_hidden, *sent)


def split(array, parts):
    found = []
    for part in range(parts):
        found.append(array.astype(jnp.bfloat16))
        array = array - found[-1].astype(jnp.float32)
    return found


def update_kernel(
    place_ref,
    listed_ref,
    own_codes_ref,
    codes_ref,
    near_ref,
    far_ref,
    table_ref,
    touched_ref,
    words_ref,
    accum_ref,
    noise_ref,
    w_ref,
    rows_ref,
    dense_noise_ref,
    table_out,
    accum_out,
    dense_out,
    update,
    clips,
):
    step = pl.program_id(0)
    last = pl.num_programs(0) - 1
    low, b_group = own_codes_ref.shape[1:]
    groups = near_ref.shape[1]
    rows_f, width = table_ref.shape[1:]
    hidden = clips.shape[1]
    count = low * DIGITS
    block = min(b_group, BLOCK)
    features = range(PAIR)

    @pl.when(step == 0)
    def _():
        chips, rows = near_ref.shape[0], near_ref.shape[2]
        for core, source in enumerate((near_ref, far_ref)):
            for chip in range(chips):
                for group in range(groups):
                    start = group * b_group + (place_ref[1] ^ (2 * chip + core)) * rows
                    clips[pl.ds(pl.multiple_of(start, rows), rows)] = source[chip, group]

    def put(side, start, stop):
        feature = jnp.maximum(step - 1, 0) * PAIR + side
        for first in range(start, stop, BATCH):
            batch = range(first, first + BATCH)
            spots = [pl.ds(listed_ref[feature, slot], 1) for slot in batch]
            rows = [table_ref[side, spot, :] for spot in spots]
            steps = [update[side, slot : slot + 1, :] for slot in batch]
            for spot, row, one_step in zip(spots, rows, steps):
                table_out[side, spot, :] = row - one_step

    def add(group, number, sums):
        where = pl.ds(pl.multiple_of(number * block, block), block)
        at = pl.ds(pl.multiple_of(group * b_group + number * block, block), block)
        found = []
        for side in features:
            if group == 0:
                codes = own_codes_ref[side, :, where]
            else:
                start = pl.multiple_of((group - 1) * b_group + number * block, block)
                codes = codes_ref[0, side, :, pl.ds(start, block)]
            found.append(sums[side] + dot(spread(codes), clips[at]))
        return tuple(found)

    def finish(side, sums):
        parts = [
            sums[digit * low : (digit + 1) * low] * (1 / scale(digit)) for digit in range(DIGITS)
        ]
        both = jnp.concatenate(split(jnp.concatenate(parts, axis=0), 2), axis=1)
        dense = dot(rows_ref[side], both)
        dense_out[side] = dense[:, :hidden] + dense[:, hidden:] + dense_noise_ref[side]
        w_twice = jnp.concatenate([w_ref[side], w_ref[side]], axis=1)
        listed = dot(both, w_twice, NT) + noise_ref[side]

        square = jnp.concatenate(split(listed * listed, 2), axis=1)
        mean = dot(square, jnp.full((2 * width, LANES), 1 / width, jnp.bfloat16))
        shape = (LANES, LANES)
        eye = iota(shape, 0) == iota(shape, 1)
        sections = [slice(start, start + LANES) for start in range(0, count, LANES)]
        touched = touched_ref[pl.ds(step * PAIR + side, 1)]
        touched = jnp.concatenate([touched[:, lanes] for lanes in sections * 2], axis=0)
        lines = [accum_ref[side, number : number + 1] for number in range(rows_f // LANES)]
        old = pick_lanes(lines, touched >> 7, touched & (LANES - 1))
        ones = jnp.where(eye, 1.0, 0.0).astype(jnp.bfloat16)
        parts = split(old, 3)
        diagonal = jnp.concatenate(
            [
                jnp.concatenate(
                    [ones * jnp.broadcast_to(part[q : q + 1], shape) for part in parts], axis=1
                )
                for q in range(len(sections))
            ],
            axis=0,
        )
        total = mean + dot(diagonal, jnp.full((3 * LANES, LANES), 1, jnp.bfloat16))
        update[side] = listed * (LEARN / jnp.sqrt(total))

        extra = [
            jnp.sum(jnp.where(eye, mean[rows], 0.0), axis=0, keepdims=True) for rows in sections
        ]
        words = words_ref[side]
        for half, word in enumerate((words & 0xFFFF, lax.shift_right_logical(words, HALF))):
            gain = pick_lanes(extra, (word >> 10) & (DIGITS - 1), word & (LANES - 1))
            rows = slice(half * words.shape[0], (half + 1) * words.shape[0])
            accum_out[side, rows] = accum_ref[side, rows] + jnp.where(
                (word >> 8) >= LISTED, gain, 0.0
            )

    @pl.when(step < last)
    def _():
        table_out[...] = table_ref[...]
        sums = tuple(jnp.zeros((count, hidden), jnp.float32) for side in features)
        if b_group == block:
            share = count // groups
            for group in range(groups):
                for side in features:
                    put(side, group * share, (group + 1) * share)
                sums = add(group, 0, sums)
        else:
            for side in features:
                put(side, 0, count)
            for group in range(groups):
                sums = lax.fori_loop(0, b_group // block, functools.partial(add, group), sums)
        for side in features:
            finish(side, sums[side])

    @pl.when(step == last)
    def _():
        table_out[...] = table_ref[...]
        for side in features:
            put(side, 0, count)


def update_rows(
    place,
    own_codes,
    codes,
    near,
    far,
    table,
    touched,
    words,
    accum,
    noise,
    w_hidden,
    rows_t,
    dense_noise,
):
    f_dev, rows_f, width = table.shape
    low, b_group = own_codes.shape[1:]
    half, others = codes.shape[1], codes.shape[3]
    hidden = near.shape[-1]
    count = touched.shape[1]
    part = dense_noise.shape[1]
    tall = rows_f // LANES
    steps = f_dev // PAIR

    def current(i):
        return jnp.minimum(i, steps - 1)

    def now(*shape):
        return pl.BlockSpec((PAIR,) + shape, lambda i, p, s: (current(i), 0, 0))

    def before(*shape):
        return pl.BlockSpec((PAIR,) + shape, lambda i, p, s: (jnp.maximum(i - 1, 0), 0, 0))

    def whole(array):
        return pl.BlockSpec(array.shape, lambda i, p, s: (0,) * array.ndim)

    def code_place(i, p, s):
        return (current(i) // (half // PAIR), current(i) % (half // PAIR), 0, 0)

    new_table, new_accum, dense = pl.pallas_call(
        update_kernel,
        grid_spec=pltpu.PrefetchScalarGridSpec(
            num_scalar_prefetch=2,
            grid=(steps + 1,),
            in_specs=[
                now(low, b_group),
                pl.BlockSpec((1, PAIR, low, others), code_place),
                whole(near),
                whole(far),
                before(rows_f, width),
                whole(touched),
                now(*words.shape[1:]),
                now(tall, LANES),
                now(count, width),
                pl.BlockSpec(
                    (PAIR, width, hidden), lambda i, p, s: (p[1] * steps + current(i), 0, 0)
                ),
                pl.BlockSpec((PAIR, part, count), lambda i, p, s: (current(i), p[0], 0)),
                now(part, hidden),
            ],
            out_specs=[before(rows_f, width), now(tall, LANES), now(part, hidden)],
            scratch_shapes=[
                pltpu.VMEM((PAIR, count, width), jnp.float32),
                pltpu.VMEM((b_group + others, hidden), jnp.bfloat16),
            ],
        ),
        out_shape=[
            jax.ShapeDtypeStruct((f_dev, rows_f, width), jnp.float32),
            jax.ShapeDtypeStruct((f_dev, tall, LANES), jnp.float32),
            jax.ShapeDtypeStruct((f_dev, part, hidden), jnp.float32),
        ],
        compiler_params=pltpu.CompilerParams(vmem_limit_bytes=56 * MIB),
        cost_estimate=pl.CostEstimate(
            flops=2 * f_dev * count * (b_group + others) * hidden,
            bytes_accessed=table.size * 8 + codes.size * 2,
            transcendentals=0,
        ),
        name="update",
    )(
        place,
        touched,
        own_codes,
        codes,
        near,
        far,
        table,
        touched,
        words,
        accum.reshape(f_dev, tall, LANES),
        noise,
        w_hidden,
        rows_t,
        dense_noise,
    )
    return new_table, new_accum.reshape(f_dev, rows_f), dense


def swap(array, axis, apart):
    size = lax.axis_size(axis)
    return lax.ppermute(array, axis, [(i, i ^ apart) for i in range(size)])


def body(table, accum, w_hidden, w_out, ids, labels, touched, row_noise, dense_noise):
    f_dev = table.shape[0]
    b_dev = labels.shape[0]
    low = touched.shape[1] // DIGITS
    own = lax.axis_index("table")
    group = lax.axis_index("group")
    groups, tables = lax.axis_size("group"), lax.axis_size("table")
    place = jnp.stack([group, own]).astype(jnp.int32)
    own_index = own.astype(jnp.int32).reshape(1)
    group_index = group.astype(jnp.int32).reshape(1)

    half = f_dev // 2
    packed = ids[:half] | (ids[half:] << HALF)
    ids, packed = lax.optimization_barrier((ids, packed))
    packed = lax.all_gather(packed, "group")

    sent, rows_t, slots, own_codes = pool(own_index, table, touched, ids, w_hidden, b_dev)
    words = slots
    stops = [half * share // 8 for share in (1, 3, 5)] + [half]
    arrived = [sent[0]] + [swap(sent[d], "table", d) for d in range(1, tables)]
    codes = None
    if stops[0]:
        codes = code_counts(group_index, words, packed, low, 0, stops[0])
    arrived, codes = lax.optimization_barrier((arrived, codes))
    clips = clip_rows(own_index, arrived, w_out, labels, w_hidden)

    def go_on(number, codes, words, waits):
        if stops[number] > stops[number - 1]:
            span = (stops[number - 1], stops[number])
            codes = code_counts(group_index, words, packed, low, *span, codes)
        return lax.optimization_barrier((codes, waits))

    words, clips = lax.optimization_barrier((words, clips))
    column = [clips] + [swap(clips, "group", d) for d in range(1, groups)]
    codes, column = go_on(1, codes, words, column)
    column = jnp.stack(column)
    words, column = lax.optimization_barrier((words, column))
    near = [column] + [swap(column, "table", d) for d in range(2, tables, 2)]
    codes, near = go_on(2, codes, words, near)
    near = jnp.stack(near)
    words, near = lax.optimization_barrier((words, near))
    far = swap(near, "table", 1)
    codes, far = go_on(3, codes, words, far)
    return update_rows(
        place,
        own_codes,
        codes,
        near,
        far,
        table,
        touched,
        slots,
        accum,
        row_noise,
        w_hidden,
        rows_t,
        dense_noise,
    )


def solution(mesh):
    in_specs = (
        P("table", None, None),
        P("table", None),
        P(),
        P(),
        P("table", None, "group"),
        P(("group", "table")),
        P("table", None),
        P("table", None, None),
        P("table", "group", None),
    )
    out_specs = (P("table", None, None), P("table", None), P("table", "group", None))
    return jax.shard_map(body, mesh=mesh, in_specs=in_specs, out_specs=out_specs, check_vma=False)
```

time: 1020 us -> 132 us (0.13)
  local copies, waits for them, and re-layouts: 404 us -> 5.66 us
  matrix products: 286 us -> 0 us
  waiting for transfers between devices: 187 us -> 0.75 us
  Pallas kernels: 0 us -> 93.2 us
  blocking collectives: 66.2 us -> 0 us
  other arithmetic: 57.4 us -> 2.45 us
  starting transfers between devices: 5.09 us -> 15.8 us
    gather x4 -> x0, local copies, waits for them, and re-layouts: 310 us -> none  [pick_rows(): return source[where]]
    dot_general x7 -> x0, matrix products: 286 us -> none  [the longest x2 142 us: pool_block(): jnp.einsum('fbr,fre->bfe', counts, table_low, preferred_element_type=jnp....]
    psum x1 -> x0, waiting for transfers between devices: 96.7 us -> none  [body(): summed = lax.psum(grads.astype(jnp.bfloat16), 'group').astype(jnp.float32)]
    pallas_call x0 -> x7, Pallas kernels: none -> 93.2 us  [the longest x1 43.8 us: update_rows(): pl.pallas_call(update_kernel, grid_spec=pltpu.PrefetchScalarGridSpec(num_...]
    unnamed x28 -> x20, local copies, waits for them, and re-layouts: 75.8 us -> 5.55 us
    all_to_all x1 -> x0, blocking collectives: 54.5 us -> none  [body(): lax.all_to_all(pooled, 'table', split_axis=0, concat_axis=1, tiled=True)]
    reduce_scatter x2 -> x0, waiting for transfers between devices: 45.1 us -> none  [the longest x1 45.1 us: body(): lax.psum_scatter(jnp.einsum('bfe,bh->feh', gathered, clip_rows, preferred...]
    all_to_all x1 -> x0, waiting for transfers between devices: 44.8 us -> none  [body(): lax.all_to_all(grad_pool, 'table', split_axis=1, concat_axis=0, tiled=True)]
  transfers between devices with their start and end apart: 4 -> 15, of which waited for: 3 -> 1; matrix products, arithmetic and copies ran while one was open for 34% -> 1% of each run, Pallas kernels for 0% -> 36%
where the time goes in v1:
time: 132 us
  Pallas kernels  93.2 us (71%)
  starting transfers between devices  15.8 us (12%)
  between operations  14.2 us (11%)
  local copies, waits for them, and re-layouts  5.66 us (4%)
  other arithmetic  2.45 us (2%)
    pallas_call x1, Pallas kernels, update_rows(): pl.pallas_call(update_kernel, grid_spec=pltpu.PrefetchScalarGridSpec(num_...  43.8 us
    pallas_call x1, Pallas kernels, pool(): pl.pallas_call(pool_kernel, grid_spec=pltpu.PrefetchScalarGridSpec(num_sc...  26.3 us
    pallas_call x4, Pallas kernels, code_counts(): pl.pallas_call(code_kernel, grid_spec=pltpu.PrefetchScalarGridSpec(num_sc...  21.5 us
    ppermute x14, starting transfers between devices, swap(): return lax.ppermute(array, axis, [(i, i ^ apart) for i in range(size)])  15.7 us
    unnamed x20, local copies, waits for them, and re-layouts  5.55 us
  transfers between devices with their start and end apart: 15, of which 1 were waited for; matrix products, arithmetic and copies ran while one was open for 1% of the time, Pallas kernels for 36%

profile of v1, /device:TPU:0, one launch (start us, length us, event | category | flops | bytes accessed | tf_op | source)
XLA Modules:
  0.0 132.0 jit_solution(7385353454984909435)
XLA Ops:
  7.2 1.8 %shift-left_or_fusion = s32[8,8,1024]{2,1,0:T(8,128)} fusion(s32[16,8,1024]{2,1,0:T(8,128)} %ids_ref), kind=kLoop, calls=%fused_computation.1 | loop fusion | flops 131072 | bytes 786432 | tf_op jit(solution)/shard_map/or | solution.py:607
  9.0 26.3 %pool.1 = (bf16[160,128]{1,0:T(8,128)(2,1)}, bf16[160,128]{1,0:T(8,128)(2,1)}, bf16[160,128]{1,0:T(8,128)(2,1)}, bf16[160,128]{1,0:T(8,128)(2,1)}, bf16[160,128]...) custom-call(s32[1]{0:T(128)} %bitcast.1.own_ref, ...), custom_call_target="tpu_custom_call" | custom-call | flops 17179869184 | bytes 16777216 | tf_op jit(solution)/shard_map/pool/pallas_call | solution.py:204
  35.4 0.5 collective-permute-start
  35.9 2.6 %collective-permute-start.1 = (bf16[160,128]{1,0:T(8,128)(2,1)}, bf16[160,128]{1,0:T(8,128)(2,1)S(1)}, u32[]{:S(2)}, u32[]{:S(2)}) collective-permute-start(bf16[160,128]{1,0:T(8,128)(2,1)} %get-tuple-element.51), channel_id=1, source_target_pairs={{0,2},{1,3},{2,0},{3,1},{4,6},{5,7},{6,4},{7,5},{8,10},{9,11},{10,... | collective-permute-start | bytes 122888 | tf_op jit(solution)/shard_map/ppermute | solution.py:592
  38.5 1.8 %collective-permute-start.3 = (bf16[160,128]{1,0:T(8,128)(2,1)}, bf16[160,128]{1,0:T(8,128)(2,1)S(1)}, u32[]{:S(2)}, u32[]{:S(2)}) collective-permute-start(bf16[160,128]{1,0:T(8,128)(2,1)} %get-tuple-element.53), channel_id=1, source_target_pairs={{0,4},{1,5},{2,6},{3,7},{4,0},{5,1},{6,2},{7,3},{8,12},{9,13},{10,... | collective-permute-start | bytes 122888 | tf_op jit(solution)/shard_map/ppermute | solution.py:592
  40.3 2.6 %collective-permute-start.5 = (bf16[160,128]{1,0:T(8,128)(2,1)}, bf16[160,128]{1,0:T(8,128)(2,1)S(1)}, u32[]{:S(2)}, u32[]{:S(2)}) collective-permute-start(bf16[160,128]{1,0:T(8,128)(2,1)} %get-tuple-element.55), channel_id=1, source_target_pairs={{0,6},{1,7},{2,4},{3,5},{4,2},{5,3},{6,0},{7,1},{8,14},{9,15},{10,... | collective-permute-start | bytes 122888 | tf_op jit(solution)/shard_map/ppermute | solution.py:592
  43.2 1.4 %copy-done.1 = s32[32,8,1024]{2,1,0:T(8,128)S(1)} copy-done((s32[32,8,1024]{2,1,0:T(8,128)S(1)}, s32[32,8,1024]{2,1,0:T(8,128)}, u32[]{:S(2)}) %copy-start.1) | copy-done | bytes 1048600
  44.6 1.0 copy-done.2
  45.6 3.1 %code.4.rest_0_ = s16[2,8,128,3072]{3,2,1,0:T(8,128)(2,1)} custom-call(s32[1]{0:T(128)} %bitcast.place_ref, s32[16,8,128]{2,1,0:T(8,128)S(1)} %copy-done.2, s32[16,8,128]{2,1,0:T(8,128)S(1)} %copy-done.2, s32[4,8,8,1024]{3,2,1,0:T(8,128)S(1)} %bitcast.19), custom_call_target="tpu_custom_call" | custom-call | flops 314572800 | bytes 1572864 | tf_op jit(solution)/shard_map/code/pallas_call | solution.py:274
  48.7 1.5 %clip.1 = bf16[128,128]{1,0:T(8,128)(2,1)S(1)} custom-call(s32[1]{0:T(128)} %bitcast.1.own_ref, f32[128,1]{1,0:T(8,128)S(1)} %copy.16.w_out_ref, f32[1,128]{1,0:T(1,128)S(1)} %bitcast.24, bf16[128,128,128]{2,1,0:T(8,128)(2,1)S(1)} %copy-done, bf16[160,128]{1,0:T(8,128)(2,1)S(1)} %copy-done.3, bf16[160,128]{1,0:T(8,128)(2,1)S(1)} %collective-permute-done.rest_1_, ...), custom_call_target="tpu_custom_call" | custom-call | flops 536870912 | bytes 4194304 | tf_op jit(solution)/shard_map/clip/pallas_call | solution.py:338
  50.2 3.8 %collective-permute-start.9 = (bf16[128,128]{1,0:T(8,128)(2,1)S(1)}, bf16[128,128]{1,0:T(8,128)(2,1)S(1)}, u32[]{:S(2)}, u32[]{:S(2)}) collective-permute-start(bf16[128,128]{1,0:T(8,128)(2,1)S(1)} %clip.1), channel_id=1, source_target_pairs={{0,24},{8,16},{16,8},{24,0},{1,25},{9,17},{17,9},{25,1},{2,26},{10... | collective-permute-start | bytes 98312 | tf_op jit(solution)/shard_map/ppermute | solution.py:592
  54.0 0.7 collective-permute-start.7
  54.7 5.4 %code.5.rest_0_ = s16[2,8,128,3072]{3,2,1,0:T(8,128)(2,1)} custom-call(s32[1]{0:T(128)} %bitcast.place_ref, s32[16,8,128]{2,1,0:T(8,128)S(1)} %copy-done.2, s32[16,8,128]{2,1,0:T(8,128)S(1)} %copy-done.2, s32[4,8,8,1024]{3,2,1,0:T(8,128)S(1)} %bitcast.20, s16[2,8,128,3072]{3,2,1,0:T(8,128)(2,1)} %code.4.rest_0_), custom_call_target="tpu_custom_call", output_to_operand_aliasing={{}: (4, {})} | custom-call | flops 629145600 | bytes 3145728 | tf_op jit(solution)/shard_map/code/pallas_call | solution.py:274
  60.1 2.6 %collective-permute-start.12 = (bf16[4,128,128]{2,1,0:T(8,128)(2,1)S(1)}, bf16[4,128,128]{2,1,0:T(8,128)(2,1)S(1)}, u32[]{:S(2)}, u32[]{:S(2)}) collective-permute-start(bf16[4,128,128]{2,1,0:T(8,128)(2,1)S(1)} %pad_maximum_fusion.1), channel_id=1, source_target_pairs={{0,6},{1,7},{2,4},{3,5},{4,2},{5,3},{6,0},{7,1},{8,14},{9,15},{10,... | collective-permute-start | bytes 393224 | tf_op jit(solution)/shard_map/ppermute | solution.py:592
  62.8 0.5 collective-permute-start.11
  63.3 0.4 collective-permute-start.10
  63.7 5.4 %code.6.rest_0_ = s16[2,8,128,3072]{3,2,1,0:T(8,128)(2,1)} custom-call(s32[1]{0:T(128)} %bitcast.place_ref, s32[16,8,128]{2,1,0:T(8,128)S(1)} %copy-done.2, s32[16,8,128]{2,1,0:T(8,128)S(1)} %copy-done.2, s32[4,8,8,1024]{3,2,1,0:T(8,128)S(1)} %bitcast.21, s16[2,8,128,3072]{3,2,1,0:T(8,128)(2,1)} %code.5.rest_0_), custom_call_target="tpu_custom_call", output_to_operand_aliasing={{}: (4, {})} | custom-call | flops 629145600 | bytes 3145728 | tf_op jit(solution)/shard_map/code/pallas_call | solution.py:274
  69.1 0.7 collective-permute-done.11
  69.9 0.7 copy.17
  70.7 0.6 pad_add_fusion.place_ref
  71.3 7.7 %code.7.codes_ref = s16[2,8,128,3072]{3,2,1,0:T(8,128)(2,1)} custom-call(s32[1]{0:T(128)} %bitcast.place_ref, s32[16,8,128]{2,1,0:T(8,128)S(1)} %copy-done.2, s32[16,8,128]{2,1,0:T(8,128)S(1)} %copy-done.2, s32[4,8,8,1024]{3,2,1,0:T(8,128)S(1)} %bitcast.22, s16[2,8,128,3072]{3,2,1,0:T(8,128)(2,1)} %code.6.rest_0_), custom_call_target="tpu_custom_call", output_to_operand_aliasing={{}: (4, {})} | custom-call | flops 943718400 | bytes 4718592 | tf_op jit(solution)/shard_map/code/pallas_call | solution.py:274
  78.9 0.8 copy-done.6
  79.7 43.8 %update.1 = (f32[16,2048,128]{2,1,0:T(8,128)}, f32[16,16,128]{2,1,0:T(8,128)}, f32[16,32,128]{2,1,0:T(8,128)}) custom-call(s32[2]{0:T(128)} %pad_add_fusion.place_ref, s32[16,512]{1,0:T(8,128)} %touched_ref.3, s16[16,128,1024]{2,1,0:T(8,128)(2,1)} %get-tuple-element.47.own_codes_ref, s16[2,8,128,3072]{3,2,1,0:T(8,128)(2,1)} %code.7.codes_ref, ...), custom_call_target="tpu_custom_call" | custom-call | flops 8589934592 | bytes 46137344 | tf_op jit(solution)/shard_map/update/pallas_call | solution.py:532
  123.6 1.6 %copy.20 = f32[2,8,16,128]{3,1,2,0:T(8,128)} copy(f32[2,8,16,128]{3,2,1,0:T(8,128)} %bitcast.29) | data formatting | bytes 262144
  (39 shorter events, 0.6 us)
Async XLA Ops:
  7.2 36.0 %all-gather.3.cloned.1.call-start = ((), (), s32[]{:S(2)}) async-start(), calls=%async_computation | async-start | bytes 1310720 | tf_op jit(solution)/shard_map/all_gather | solution.py:609
  9.0 34.0 %copy-start.8 = (f32[128]{0:T(128)S(1)}, f32[128]{0:T(128)}, u32[]{:S(2)}) copy-start(f32[128]{0:T(128)} %param.12) | copy-start | bytes 1540
  35.4 13.4 %copy-start.3 = (bf16[160,128]{1,0:T(8,128)(2,1)S(1)}, bf16[160,128]{1,0:T(8,128)(2,1)}, u32[]{:S(2)}) copy-start(bf16[160,128]{1,0:T(8,128)(2,1)} %get-tuple-element.58.rest_0_) | copy-start | bytes 122884
  35.4 13.4 %copy-start.4 = (f32[128]{0:T(128)S(1)}, f32[128]{0:T(128)}, u32[]{:S(2)}) copy-start(f32[128]{0:T(128)} %param.14) | copy-start | bytes 1540
  35.4 4.9 %collective-permute-start = (bf16[160,128]{1,0:T(8,128)(2,1)}, bf16[160,128]{1,0:T(8,128)(2,1)S(1)}, u32[]{:S(2)}, u32[]{:S(2)}) collective-permute-start(bf16[160,128]{1,0:T(8,128)(2,1)} %get-tuple-element.50), channel_id=1, source_target_pairs={{0,1},{1,0},{2,3},{3,2},{4,5},{5,4},{6,7},{7,6},{8,9},{9,8},{10,11... | collective-permute-start | bytes 122888 | tf_op jit(solution)/shard_map/ppermute | solution.py:592
  35.9 7.0 %collective-permute-start.1 = (bf16[160,128]{1,0:T(8,128)(2,1)}, bf16[160,128]{1,0:T(8,128)(2,1)S(1)}, u32[]{:S(2)}, u32[]{:S(2)}) collective-permute-start(bf16[160,128]{1,0:T(8,128)(2,1)} %get-tuple-element.51), channel_id=1, source_target_pairs={{0,2},{1,3},{2,0},{3,1},{4,6},{5,7},{6,4},{7,5},{8,10},{9,11},{10,... | collective-permute-start | bytes 122888 | tf_op jit(solution)/shard_map/ppermute | solution.py:592
  38.5 10.2 %collective-permute-start.2 = (bf16[160,128]{1,0:T(8,128)(2,1)}, bf16[160,128]{1,0:T(8,128)(2,1)S(1)}, u32[]{:S(2)}, u32[]{:S(2)}) collective-permute-start(bf16[160,128]{1,0:T(8,128)(2,1)} %get-tuple-element.52), channel_id=1, source_target_pairs={{0,3},{1,2},{2,1},{3,0},{4,7},{5,6},{6,5},{7,4},{8,11},{9,10},{10,... | collective-permute-start | bytes 122888 | tf_op jit(solution)/shard_map/ppermute | solution.py:592
  38.5 10.2 %collective-permute-start.3 = (bf16[160,128]{1,0:T(8,128)(2,1)}, bf16[160,128]{1,0:T(8,128)(2,1)S(1)}, u32[]{:S(2)}, u32[]{:S(2)}) collective-permute-start(bf16[160,128]{1,0:T(8,128)(2,1)} %get-tuple-element.53), channel_id=1, source_target_pairs={{0,4},{1,5},{2,6},{3,7},{4,0},{5,1},{6,2},{7,3},{8,12},{9,13},{10,... | collective-permute-start | bytes 122888 | tf_op jit(solution)/shard_map/ppermute | solution.py:592
  40.3 8.4 %collective-permute-start.4 = (bf16[160,128]{1,0:T(8,128)(2,1)}, bf16[160,128]{1,0:T(8,128)(2,1)S(1)}, u32[]{:S(2)}, u32[]{:S(2)}) collective-permute-start(bf16[160,128]{1,0:T(8,128)(2,1)} %get-tuple-element.54), channel_id=1, source_target_pairs={{0,5},{1,4},{2,7},{3,6},{4,1},{5,0},{6,3},{7,2},{8,13},{9,12},{10,... | collective-permute-start | bytes 122888 | tf_op jit(solution)/shard_map/ppermute | solution.py:592
  40.3 8.4 %collective-permute-start.5 = (bf16[160,128]{1,0:T(8,128)(2,1)}, bf16[160,128]{1,0:T(8,128)(2,1)S(1)}, u32[]{:S(2)}, u32[]{:S(2)}) collective-permute-start(bf16[160,128]{1,0:T(8,128)(2,1)} %get-tuple-element.55), channel_id=1, source_target_pairs={{0,6},{1,7},{2,4},{3,5},{4,2},{5,3},{6,0},{7,1},{8,14},{9,15},{10,... | collective-permute-start | bytes 122888 | tf_op jit(solution)/shard_map/ppermute | solution.py:592
  42.9 5.8 %collective-permute-start.6 = (bf16[160,128]{1,0:T(8,128)(2,1)}, bf16[160,128]{1,0:T(8,128)(2,1)S(1)}, u32[]{:S(2)}, u32[]{:S(2)}) collective-permute-start(bf16[160,128]{1,0:T(8,128)(2,1)} %get-tuple-element.56), channel_id=1, source_target_pairs={{0,7},{1,6},{2,5},{3,4},{4,3},{5,2},{6,1},{7,0},{8,15},{9,14},{10,... | collective-permute-start | bytes 122888 | tf_op jit(solution)/shard_map/ppermute | solution.py:592
  43.2 5.6 %copy-start = (bf16[128,128,128]{2,1,0:T(8,128)(2,1)S(1)}, bf16[128,128,128]{2,1,0:T(8,128)(2,1)}, u32[]{:S(2)}) copy-start(bf16[128,128,128]{2,1,0:T(8,128)(2,1)} %w_ref.5) | copy-start | bytes 12582916
  43.2 1.4 %copy-start.1 = (s32[32,8,1024]{2,1,0:T(8,128)S(1)}, s32[32,8,1024]{2,1,0:T(8,128)}, u32[]{:S(2)}) copy-start(s32[32,8,1024]{2,1,0:T(8,128)} %all-gather.3.cloned.1.call-done) | copy-start | bytes 3145732
  44.6 1.0 copy-start.2
  50.2 9.9 %collective-permute-start.9 = (bf16[128,128]{1,0:T(8,128)(2,1)S(1)}, bf16[128,128]{1,0:T(8,128)(2,1)S(1)}, u32[]{:S(2)}, u32[]{:S(2)}) collective-permute-start(bf16[128,128]{1,0:T(8,128)(2,1)S(1)} %clip.1), channel_id=1, source_target_pairs={{0,24},{8,16},{16,8},{24,0},{1,25},{9,17},{17,9},{25,1},{2,26},{10... | collective-permute-start | bytes 98312 | tf_op jit(solution)/shard_map/ppermute | solution.py:592
  54.0 6.1 %collective-permute-start.8 = (bf16[128,128]{1,0:T(8,128)(2,1)S(1)}, bf16[128,128]{1,0:T(8,128)(2,1)S(1)}, u32[]{:S(2)}, u32[]{:S(2)}) collective-permute-start(bf16[128,128]{1,0:T(8,128)(2,1)S(1)} %clip.1), channel_id=1, source_target_pairs={{0,16},{8,24},{16,0},{24,8},{1,17},{9,25},{17,1},{25,9},{2,18},{10... | collective-permute-start | bytes 98312 | tf_op jit(solution)/shard_map/ppermute | solution.py:592
  54.0 6.1 %collective-permute-start.7 = (bf16[128,128]{1,0:T(8,128)(2,1)S(1)}, bf16[128,128]{1,0:T(8,128)(2,1)S(1)}, u32[]{:S(2)}, u32[]{:S(2)}) collective-permute-start(bf16[128,128]{1,0:T(8,128)(2,1)S(1)} %clip.1), channel_id=1, source_target_pairs={{0,8},{8,0},{16,24},{24,16},{1,9},{9,1},{17,25},{25,17},{2,10},{10... | collective-permute-start | bytes 98312 | tf_op jit(solution)/shard_map/ppermute | solution.py:592
  60.1 9.8 %copy-start.7 = (f32[16,2048]{1,0:T(8,128)S(1)}, f32[16,2048]{1,0:T(8,128)}, u32[]{:S(2)}) copy-start(f32[16,2048]{1,0:T(8,128)} %param.10) | copy-start | bytes 393220
  60.1 8.9 %collective-permute-start.12 = (bf16[4,128,128]{2,1,0:T(8,128)(2,1)S(1)}, bf16[4,128,128]{2,1,0:T(8,128)(2,1)S(1)}, u32[]{:S(2)}, u32[]{:S(2)}) collective-permute-start(bf16[4,128,128]{2,1,0:T(8,128)(2,1)S(1)} %pad_maximum_fusion.1), channel_id=1, source_target_pairs={{0,6},{1,7},{2,4},{3,5},{4,2},{5,3},{6,0},{7,1},{8,14},{9,15},{10,... | collective-permute-start | bytes 393224 | tf_op jit(solution)/shard_map/ppermute | solution.py:592
  62.8 7.0 %collective-permute-start.11 = (bf16[4,128,128]{2,1,0:T(8,128)(2,1)S(1)}, bf16[4,128,128]{2,1,0:T(8,128)(2,1)S(1)}, u32[]{:S(2)}, u32[]{:S(2)}) collective-permute-start(bf16[4,128,128]{2,1,0:T(8,128)(2,1)S(1)} %pad_maximum_fusion.1), channel_id=1, source_target_pairs={{0,4},{1,5},{2,6},{3,7},{4,0},{5,1},{6,2},{7,3},{8,12},{9,13},{10,... | collective-permute-start | bytes 393224 | tf_op jit(solution)/shard_map/ppermute | solution.py:592
  63.3 6.4 %collective-permute-start.10 = (bf16[4,128,128]{2,1,0:T(8,128)(2,1)S(1)}, bf16[4,128,128]{2,1,0:T(8,128)(2,1)S(1)}, u32[]{:S(2)}, u32[]{:S(2)}) collective-permute-start(bf16[4,128,128]{2,1,0:T(8,128)(2,1)S(1)} %pad_maximum_fusion.1), channel_id=1, source_target_pairs={{0,2},{1,3},{2,0},{3,1},{4,6},{5,7},{6,4},{7,5},{8,10},{9,11},{10,... | collective-permute-start | bytes 393224 | tf_op jit(solution)/shard_map/ppermute | solution.py:592
  69.8 9.1 %copy-start.5 = (bf16[4,4,128,128]{3,2,1,0:T(8,128)(2,1)}, bf16[4,4,128,128]{3,2,1,0:T(8,128)(2,1)S(1)}, u32[]{:S(2)}) copy-start(bf16[4,4,128,128]{3,2,1,0:T(8,128)(2,1)S(1)} %pad_maximum_fusion.near_ref) | copy-start | bytes 1572868
  69.8 9.1 %collective-permute-start.13 = (bf16[4,4,128,128]{3,2,1,0:T(8,128)(2,1)S(1)}, bf16[4,4,128,128]{3,2,1,0:T(8,128)(2,1)S(1)}, u32[]{:S(2)}, u32[]{:S(2)}) collective-permute-start(bf16[4,4,128,128]{3,2,1,0:T(8,128)(2,1)S(1)} %pad_maximum_fusion.near_ref), channel_id=1, source_target_pairs={{0,1},{1,0},{2,3},{3,2},{4,5},{5,4},{6,7},{7,6},{8,9},{9,8},{10,11... | collective-permute-start | bytes 1572872 | tf_op jit(solution)/shard_map/ppermute | solution.py:592
  78.9 0.8 copy-start.6
Sparse Core Ops, SparseCore 0:
  10.1 30.5 all-gather.2

commit v2 on v1

v2 whole, which is shorter than its diff:
```python
import functools

import jax
import jax.numpy as jnp
from jax import lax
from jax.experimental import pallas as pl
from jax.experimental.pallas import tpu as pltpu
from jax.sharding import PartitionSpec as P

CLIP = 1.0
LEARN = 0.05
LANES = 128
DIGITS = 4
HALF = 16
BLOCK = 1024
ROWS = 512
OWN, GROUP, BASE, FAR_BASE = range(4)
PAIR = 2
LISTED = 16
MIB = 1 << 20

NT = (((1,), (1,)), ((), ()))
TN = (((0,), (0,)), ((), ()))


def dot(left, right, dims=(((1,), (0,)), ((), ())), precision=None):
    return lax.dot_general(
        left, right, dims, preferred_element_type=jnp.float32, precision=precision
    )


def iota(shape, axis):
    return lax.broadcasted_iota(jnp.int32, shape, axis)


def slot_words(touched_row, rows_f):
    count = touched_row.shape[1]
    low = count // DIGITS
    tall = rows_f // LANES
    slot = iota((1, count), 1)
    rows = jnp.where((touched_row >> 7) == iota((tall, count), 0), 1.0, 0.0)
    lanes = jnp.where((touched_row & (LANES - 1)) == iota((LANES, count), 0), 1.0, 0.0)
    values = (lax.rem(slot, low), LISTED + 4 * lax.div(slot, low))
    held = jnp.concatenate([rows * value.astype(jnp.float32) for value in values], axis=0)
    parts = dot(held.astype(jnp.bfloat16), lanes.astype(jnp.bfloat16), NT).astype(jnp.int32)
    word = parts[:tall] | (parts[tall:] << 8)
    return word[: tall // 2] | (word[tall // 2 :] << HALF)


def pick_lanes(lines, row, lane):
    got = [
        jnp.take_along_axis(jnp.broadcast_to(line, row.shape), lane, axis=1) for line in lines
    ]
    bit = 1
    while len(got) > 1:
        odd = (row & bit) != 0
        got = [jnp.where(odd, got[i + 1], got[i]) for i in range(0, len(got), 2)]
        bit *= 2
    return got[0]


def look_up(lines, ids, slots, where):
    word = pick_lanes(lines, ids >> 7, ids & (LANES - 1))
    upper = ids >= len(lines) * LANES
    word = jnp.where(upper, lax.shift_right_logical(word, HALF), word) & 0xFFFF
    slots[0, :, where] = word & 0xFF
    slots[1, :, where] = jnp.left_shift(jnp.ones_like(word), (word >> 8) & (LISTED - 1))


def places(low):
    shape = (low // HALF, HALF, LANES)
    return (iota(shape, 0) * HALF + iota(shape, 1)).astype(jnp.int16)


def tally(place, slots, where):
    total = jnp.zeros(place.shape, jnp.int16)
    nothing = jnp.zeros(place.shape, jnp.int16)
    wide = (HALF, LANES)
    for hot in range(slots.shape[1]):
        one_group = jnp.broadcast_to(slots[0, hot : hot + 1, where], wide).astype(jnp.int16)
        one_code = jnp.broadcast_to(slots[1, hot : hot + 1, where], wide).astype(jnp.int16)
        hit = place == jnp.broadcast_to(one_group[None], place.shape)
        total = total + jnp.where(hit, jnp.broadcast_to(one_code[None], place.shape), nothing)
    return total.reshape(-1, LANES)


def spread(codes):
    parts = []
    for digit in range(DIGITS):
        if digit < DIGITS - 1:
            part = codes & jnp.full(codes.shape, 15 << (4 * digit), jnp.int16)
        else:
            part = lax.shift_right_logical(codes, jnp.full(codes.shape, 4 * digit, jnp.int16))
        parts.append(part.astype(jnp.bfloat16))
    return jnp.concatenate(parts, axis=0)


def scale(digit):
    return float(16**digit if digit < DIGITS - 1 else 1)


def pool_kernel(
    place_ref,
    table_ref,
    touched_ref,
    ids_ref,
    w_ref,
    sent_ref,
    rows_ref,
    words_ref,
    codes_ref,
    sums,
    same,
    slots,
):
    step = pl.program_id(0)
    rows_f, width = table_ref.shape[1:]
    hots, b_group = ids_ref.shape[1:]
    count = touched_ref.shape[1]
    low = count // DIGITS
    hidden = w_ref.shape[2]
    blocks, tall, chunk = sums.shape
    block = min(b_group, BLOCK)
    place = places(low)

    @pl.when(step == 0)
    def _():
        sums[...] = jnp.zeros_like(sums)
        same[...] = jnp.zeros_like(same)

    features = range(PAIR)
    lines = []
    for side in features:
        words = slot_words(touched_ref[pl.ds(step * PAIR + side, 1)], rows_f)
        words_ref[side] = words
        lines.append([words[number : number + 1] for number in range(words.shape[0])])
    lane = iota((HALF, LANES), 1)
    columns, picked = [], []
    for side in features:
        row = touched_ref[pl.ds(step * PAIR + side, 1)].astype(jnp.float32)
        column = jnp.broadcast_to(row, (LANES, count)).T.astype(jnp.int32).astype(jnp.int16)
        columns.append(column.reshape(count // HALF, HALF, LANES))
        picked.append(jnp.zeros((count, width), jnp.float32))
    one = jnp.ones(columns[0].shape, jnp.bfloat16)
    for start in range(0, rows_f, ROWS):
        for side in features:
            parts = []
            for first in range(start, start + ROWS, LANES):
                number = (lane + first).astype(jnp.int16)
                hit = columns[side] == jnp.broadcast_to(number[None], one.shape)
                parts.append(jnp.where(hit, one, jnp.zeros_like(one)).reshape(count, LANES))
            rows = table_ref[side, start : start + ROWS].astype(jnp.bfloat16)
            picked[side] = picked[side] + dot(jnp.concatenate(parts, axis=1), rows)
    rows_t, w_t = [], []
    for side in features:
        whole = picked[side].astype(jnp.bfloat16).T
        rows_ref[side] = whole
        parts = [
            whole[:, digit * low : (digit + 1) * low] * jnp.bfloat16(1 / scale(digit))
            for digit in range(DIGITS)
        ]
        rows_t.append(jnp.concatenate(parts, axis=1))
        w_t.append(w_ref[side].T)

    def one_block(number):
        for inner in range(0, block, chunk):
            for side in features:
                where = pl.ds(pl.multiple_of(number * block + inner, chunk), chunk)
                ids = ids_ref[side, :, where]
                look_up(lines[side], ids, slots.at[side], slice(inner, inner + chunk))
                pairs = jnp.zeros(ids.shape, jnp.float32)
                for turn in range(1, hots // 2 + 1):
                    weight = 2.0 if turn < hots // 2 else 1.0
                    pairs = pairs + jnp.where(ids == pltpu.roll(ids, turn, 0), weight, 0.0)
                pairs = jnp.sum(pairs, axis=0, keepdims=True) + hots
                part = number * (block // chunk) + inner // chunk
                same[part, pl.ds(step * PAIR + side, 1)] = pairs
        for inner in range(0, block, 2 * chunk):
            pre, square = 0.0, 0.0
            for side in features:
                parts = []
                for start in (inner, inner + chunk):
                    codes = tally(place, slots.at[side], slice(start, start + chunk))
                    where = pl.ds(pl.multiple_of(number * block + start, chunk), chunk)
                    codes_ref[side, :, where] = codes
                    parts.append(spread(codes))
                pooled = dot(rows_t[side], jnp.concatenate(parts, axis=1)).astype(jnp.bfloat16)
                wide = pooled.astype(jnp.float32)
                square += jnp.sum((wide * wide).reshape(width // HALF, HALF, 2 * chunk), axis=0)
                pre += dot(w_t[side], pooled)
            for turn in range(2):
                part = number * (block // chunk) + inner // chunk + turn
                lanes = slice(turn * chunk, (turn + 1) * chunk)
                sums[part, :hidden] += pre[:, lanes]
                sums[part, hidden:] += square[:, lanes]

    each(b_group // block, one_block)

    @pl.when(step == pl.num_programs(0) - 1)
    def _():
        for part in range(blocks):
            sent_ref[part, :tall] = sums[part].astype(jnp.bfloat16)
            sent_ref[part, tall:] = same[part].astype(jnp.bfloat16)


def each(times, step):
    if times == 1:
        step(0)
    else:

        @pl.loop(0, times)
        def _(number):
            step(number)


def pool(place, table, touched, ids, w_hidden, chunk):
    f_dev, rows_f, width = table.shape
    hots, b_group = ids.shape[1:]
    count = touched.shape[1]
    low = count // DIGITS
    hidden = w_hidden.shape[2]
    blocks = b_group // chunk
    repeat_rows = -(-f_dev // HALF) * HALF
    tall = hidden + HALF
    sent = (blocks, tall + repeat_rows, chunk)
    steps = f_dev // PAIR

    def now(*shape):
        return pl.BlockSpec((PAIR,) + shape, lambda i, p: (i, 0, 0))

    return pl.pallas_call(
        pool_kernel,
        grid_spec=pltpu.PrefetchScalarGridSpec(
            num_scalar_prefetch=1,
            grid=(steps,),
            in_specs=[
                now(rows_f, width),
                pl.BlockSpec(touched.shape, lambda i, p: (0, 0)),
                now(hots, b_group),
                pl.BlockSpec((PAIR, width, hidden), lambda i, p: (p[OWN] * steps + i, 0, 0)),
            ],
            out_specs=[
                pl.BlockSpec(sent, lambda i, p: (0, 0, 0)),
                now(width, count),
                now(rows_f // 256, LANES),
                now(low, b_group),
            ],
            scratch_shapes=[
                pltpu.VMEM((blocks, tall, chunk), jnp.float32),
                pltpu.VMEM((blocks, repeat_rows, chunk), jnp.float32),
                pltpu.VMEM((PAIR, 2, hots, min(b_group, BLOCK)), jnp.int32),
            ],
        ),
        out_shape=[
            jax.ShapeDtypeStruct(sent, jnp.bfloat16),
            jax.ShapeDtypeStruct((f_dev, width, count), jnp.bfloat16),
            jax.ShapeDtypeStruct((f_dev, rows_f // 256, LANES), jnp.int32),
            jax.ShapeDtypeStruct((f_dev, low, b_group), jnp.int16),
        ],
        compiler_params=pltpu.CompilerParams(vmem_limit_bytes=56 * MIB),
        cost_estimate=pl.CostEstimate(
            flops=2 * f_dev * count * b_group * width * 8,
            bytes_accessed=table.size * 4,
            transcendentals=0,
        ),
        name="pool",
    )(place, table, touched, ids, w_hidden)


def code_kernel(place_ref, words_ref, ids_ref, *rest):
    codes_ref, slots = rest[-2:]
    low, b_group = codes_ref.shape[1:]
    block = min(b_group, BLOCK)
    place = places(low)
    lines = [
        [words_ref[side, number : number + 1] for number in range(words_ref.shape[1])]
        for side in range(PAIR)
    ]

    def one_block(number):
        for inner in range(0, block, LANES):
            where = pl.ds(pl.multiple_of(number * block + inner, LANES), LANES)
            packed = ids_ref[0, 0, :, where]
            for side, ids in enumerate((packed & 0xFFFF, packed >> HALF)):
                look_up(lines[side], ids, slots.at[side], slice(inner, inner + LANES))
        for inner in range(0, block, LANES):
            where = pl.ds(pl.multiple_of(number * block + inner, LANES), LANES)
            for side in range(PAIR):
                codes_ref[side, :, where] = tally(
                    place, slots.at[side], slice(inner, inner + LANES)
                )

    each(b_group // block, one_block)


def code_counts(place, words, packed, low, start, stop, before=None):
    others, pairs, hots, b_group = packed.shape
    size = (stop - start) * PAIR * low * others * b_group
    kept = () if before is None else (before,)
    return pl.pallas_call(
        code_kernel,
        grid_spec=pltpu.PrefetchScalarGridSpec(
            num_scalar_prefetch=1,
            grid=(stop - start, others),
            in_specs=[
                pl.BlockSpec((PAIR,) + words.shape[1:], lambda f, g, p: (p[BASE] + f + start, 0, 0)),
                pl.BlockSpec((1, 1, hots, b_group), lambda f, g, p: (g, f + start, 0, 0)),
            ]
            + [pl.BlockSpec(memory_space=pl.ANY)] * len(kept),
            out_specs=pl.BlockSpec((PAIR, low, b_group), lambda f, g, p: (f + start, 0, g)),
            scratch_shapes=[pltpu.VMEM((PAIR, 2, hots, min(b_group, BLOCK)), jnp.int32)],
        ),
        out_shape=jax.ShapeDtypeStruct((pairs * PAIR, low, others * b_group), jnp.int16),
        input_output_aliases={3: 0} if kept else {},
        compiler_params=pltpu.CompilerParams(vmem_limit_bytes=48 * MIB),
        cost_estimate=pl.CostEstimate(
            flops=size * 400, bytes_accessed=size * 2, transcendentals=0
        ),
        name="code",
    )(place, words, packed, *kept)


def clip_kernel(w_out_ref, labels_ref, w_ref, sent_ref, clip_ref):
    features, width, hidden = w_ref.shape
    devices = sent_ref.shape[0]
    share = features // devices
    tall = hidden + HALF
    w_out = w_out_ref[...]
    red = sent_ref[0, :tall].astype(jnp.float32)
    for device in range(1, devices):
        red = red + sent_ref[device, :tall].astype(jnp.float32)
    pre = red[:hidden]
    flat_sq = jnp.sum(red[hidden:], axis=0, keepdims=True)
    gate = jax.nn.sigmoid(pre)
    logit = jnp.sum(pre * gate * w_out, axis=0, keepdims=True)
    miss = jax.nn.sigmoid(logit) - labels_ref[...]
    delta = gate * (1.0 + pre * (1.0 - gate)) * w_out * miss
    delta_low = delta.astype(jnp.bfloat16)
    lanes = pre.shape[1]

    total = jnp.zeros((8, lanes), jnp.float32)
    for device in range(devices):
        w_part = w_ref[device * share : (device + 1) * share].reshape(share * width, hidden)
        grad = dot(w_part, delta_low)
        square = jnp.sum((grad * grad).reshape(share, width // 8, 8, lanes), axis=1)
        repeats = sent_ref[device, tall:].astype(jnp.float32)
        for inner in range(share):
            total = total + square[inner] * repeats[inner : inner + 1]
    norm_sq = jnp.sum(total, axis=0, keepdims=True)
    norm_sq = norm_sq + flat_sq * jnp.sum(delta * delta, axis=0, keepdims=True)
    factor = CLIP / jnp.maximum(jnp.sqrt(norm_sq), CLIP)
    clip_ref[...] = (factor * delta).T.astype(jnp.bfloat16)


def clip_rows(sent, w_out, labels, w_hidden):
    features, width, hidden = w_hidden.shape
    b_dev = labels.shape[0]
    vmem = pl.BlockSpec(memory_space=pltpu.VMEM)
    return pl.pallas_call(
        clip_kernel,
        in_specs=[vmem] * 4,
        out_specs=vmem,
        out_shape=jax.ShapeDtypeStruct((b_dev, hidden), jnp.bfloat16),
        compiler_params=pltpu.CompilerParams(vmem_limit_bytes=32 * MIB),
        cost_estimate=pl.CostEstimate(
            flops=2 * features * width * hidden * b_dev,
            bytes_accessed=w_hidden.size * 2,
            transcendentals=b_dev * hidden,
        ),
        name="clip",
    )(w_out.reshape(hidden, 1), labels.reshape(1, b_dev), w_hidden, sent)


def split(array, parts):
    found = []
    for part in range(parts):
        found.append(array.astype(jnp.bfloat16))
        array = array - found[-1].astype(jnp.float32)
    return found


def sum_kernel(place_ref, own_codes_ref, codes_ref, near_ref, far_ref, sums_ref, clips):
    low, b_group = own_codes_ref.shape[1:]
    groups = near_ref.shape[1]
    hidden = clips.shape[1]
    count = low * DIGITS
    block = min(b_group, BLOCK)
    features = range(PAIR)

    @pl.when(pl.program_id(0) == 0)
    def _():
        chips, rows = near_ref.shape[0], near_ref.shape[2]
        for core, source in enumerate((near_ref, far_ref)):
            for chip in range(chips):
                for group in range(groups):
                    start = group * b_group + (place_ref[OWN] ^ (2 * chip + core)) * rows
                    clips[pl.ds(pl.multiple_of(start, rows), rows)] = source[chip, group]

    def add(group, number, sums):
        where = pl.ds(pl.multiple_of(number * block, block), block)
        at = pl.ds(pl.multiple_of(group * b_group + number * block, block), block)
        found = []
        for side in features:
            if group == 0:
                codes = own_codes_ref[side, :, where]
            else:
                start = pl.multiple_of((group - 1) * b_group + number * block, block)
                codes = codes_ref[side, :, pl.ds(start, block)]
            found.append(sums[side] + dot(spread(codes), clips[at]))
        return tuple(found)

    sums = tuple(jnp.zeros((count, hidden), jnp.float32) for side in features)
    for group in range(groups):
        if b_group == block:
            sums = add(group, 0, sums)
        else:
            sums = lax.fori_loop(0, b_group // block, functools.partial(add, group), sums)
    for side in features:
        for digit in range(DIGITS):
            rows = slice(digit * low, (digit + 1) * low)
            sums_ref[side, rows] = (sums[side][rows] * (1 / scale(digit))).astype(jnp.bfloat16)


def sum_clips(place, own_codes, codes, near, far, start, stop):
    low, b_group = own_codes.shape[1:]
    others = codes.shape[2]
    hidden = near.shape[-1]
    count = low * DIGITS
    features = (stop - start) * PAIR

    def whole(array):
        return pl.BlockSpec(array.shape, lambda i, p: (0,) * array.ndim)

    return pl.pallas_call(
        sum_kernel,
        grid_spec=pltpu.PrefetchScalarGridSpec(
            num_scalar_prefetch=1,
            grid=(stop - start,),
            in_specs=[
                pl.BlockSpec((PAIR, low, b_group), lambda i, p: (p[BASE] + start + i, 0, 0)),
                pl.BlockSpec((PAIR, low, others), lambda i, p: (start + i, 0, 0)),
                whole(near),
                whole(far),
            ],
            out_specs=pl.BlockSpec((PAIR, count, hidden), lambda i, p: (i, 0, 0)),
            scratch_shapes=[pltpu.VMEM((b_group + others, hidden), jnp.bfloat16)],
        ),
        out_shape=jax.ShapeDtypeStruct((features, count, hidden), jnp.bfloat16),
        compiler_params=pltpu.CompilerParams(vmem_limit_bytes=48 * MIB),
        cost_estimate=pl.CostEstimate(
            flops=2 * features * count * (b_group + others) * hidden,
            bytes_accessed=features * low * (b_group + others) * 2,
            transcendentals=0,
        ),
        name="sums",
    )(place, own_codes, codes, near, far)


def update_kernel(
    place_ref,
    first_ref,
    second_ref,
    table_ref,
    touched_ref,
    words_ref,
    accum_ref,
    noise_ref,
    w_ref,
    rows_ref,
    dense_noise_ref,
    *rest,
    base,
    cut,
):
    table_out, accum_out, dense_out, update = rest[-4:]
    step = pl.program_id(0)
    last = pl.num_programs(0) - 1
    rows_f, width = table_ref.shape[1:]
    count = first_ref.shape[1]
    features = range(PAIR)

    def touched_of(step, side):
        return touched_ref[pl.ds((place_ref[base] + step) * PAIR + side, 1)]

    def put():
        shape = (ROWS // HALF, HALF, count)
        number = (iota(shape, 0) * HALF + iota(shape, 1)).astype(jnp.int16)
        one = jnp.ones(shape, jnp.bfloat16)
        rows = [
            jnp.broadcast_to(touched_of(jnp.maximum(step - 1, 0), side), (HALF, count))
            for side in features
        ]
        for start in range(0, rows_f, ROWS):
            for side in features:
                row = (rows[side] - start).astype(jnp.int16)
                hit = number == jnp.broadcast_to(row[None], shape)
                hit = jnp.where(hit, one, jnp.zeros_like(one)).reshape(ROWS, count)
                steps = dot(hit, update[side])
                where = slice(start, start + ROWS)
                table_out[side, where] = table_ref[side, where] - (
                    steps[:, :width] + steps[:, width:]
                )

    def finish(side):
        sums = jnp.where(step < cut, first_ref[side], second_ref[side])
        dense_out[side] = dot(rows_ref[side], sums) + dense_noise_ref[side]
        listed = dot(sums, w_ref[side], NT) + noise_ref[side]

        square = jnp.concatenate(split(listed * listed, 2), axis=1)
        mean = dot(square, jnp.full((2 * width, LANES), 1 / width, jnp.bfloat16))
        shape = (LANES, LANES)
        eye = iota(shape, 0) == iota(shape, 1)
        sections = [slice(start, start + LANES) for start in range(0, count, LANES)]
        touched = touched_of(step, side)
        touched = jnp.concatenate([touched[:, lanes] for lanes in sections * 2], axis=0)
        lines = [accum_ref[side, number : number + 1] for number in range(rows_f // LANES)]
        old = pick_lanes(lines, touched >> 7, touched & (LANES - 1))
        ones = jnp.where(eye, 1.0, 0.0).astype(jnp.bfloat16)
        parts = split(old, 3)
        diagonal = jnp.concatenate(
            [
                jnp.concatenate(
                    [ones * jnp.broadcast_to(part[q : q + 1], shape) for part in parts], axis=1
                )
                for q in range(len(sections))
            ],
            axis=0,
        )
        total = mean + dot(diagonal, jnp.full((3 * LANES, LANES), 1, jnp.bfloat16))
        steps = listed * (LEARN / jnp.sqrt(total))
        update[side] = jnp.concatenate(split(steps, 2), axis=1)

        extra = [
            jnp.sum(jnp.where(eye, mean[rows], 0.0), axis=0, keepdims=True) for rows in sections
        ]
        words = words_ref[side]
        for half, word in enumerate((words & 0xFFFF, lax.shift_right_logical(words, HALF))):
            gain = pick_lanes(extra, word >> 10, word & (LANES - 1))
            rows = slice(half * words.shape[0], (half + 1) * words.shape[0])
            accum_out[side, rows] = accum_ref[side, rows] + jnp.where(
                (word >> 8) >= LISTED, gain, 0.0
            )

    @pl.when(step < last)
    def _():
        put()
        for side in features:
            finish(side)

    @pl.when(step == last)
    def _():
        put()


def update_rows(
    place, base, sums, table, touched, words, accum, noise, w_hidden, rows_t, dense_noise, before=None
):
    f_dev, rows_f, width = table.shape
    hidden = w_hidden.shape[2]
    count = touched.shape[1]
    part = dense_noise.shape[1]
    tall = rows_f // LANES
    lengths = [array.shape[0] // PAIR for array in sums]
    cut, steps = lengths[0], sum(lengths)
    first, second = (sums * 2)[:2]
    kept = () if before is None else tuple(before)

    def at(i, p):
        return p[base] + jnp.minimum(i, steps - 1)

    def now(*shape):
        return pl.BlockSpec((PAIR,) + shape, lambda i, p: (at(i, p), 0, 0))

    def late(*shape):
        return pl.BlockSpec((PAIR,) + shape, lambda i, p: (p[base] + jnp.maximum(i - 1, 0), 0, 0))

    def summed(start, length):
        return pl.BlockSpec(
            (PAIR, count, hidden), lambda i, p: (jnp.clip(i - start, 0, length - 1), 0, 0)
        )

    return pl.pallas_call(
        functools.partial(update_kernel, base=base, cut=cut),
        grid_spec=pltpu.PrefetchScalarGridSpec(
            num_scalar_prefetch=1,
            grid=(steps + 1,),
            in_specs=[
                summed(0, cut),
                summed(cut, lengths[-1]),
                late(rows_f, width),
                pl.BlockSpec(touched.shape, lambda i, p: (0, 0)),
                now(*words.shape[1:]),
                now(tall, LANES),
                now(count, width),
                pl.BlockSpec(
                    (PAIR, width, hidden),
                    lambda i, p: (p[OWN] * (f_dev // PAIR) + at(i, p), 0, 0),
                ),
                pl.BlockSpec((PAIR, part, count), lambda i, p: (at(i, p), p[GROUP], 0)),
                now(part, hidden),
            ]
            + [pl.BlockSpec(memory_space=pl.ANY)] * len(kept),
            out_specs=[late(rows_f, width), now(tall, LANES), now(part, hidden)],
            scratch_shapes=[pltpu.VMEM((PAIR, count, 2 * width), jnp.bfloat16)],
        ),
        out_shape=[
            jax.ShapeDtypeStruct((f_dev, rows_f, width), jnp.float32),
            jax.ShapeDtypeStruct((f_dev, tall, LANES), jnp.float32),
            jax.ShapeDtypeStruct((f_dev, part, hidden), jnp.float32),
        ],
        input_output_aliases={11 + number: number for number in range(len(kept))},
        compiler_params=pltpu.CompilerParams(vmem_limit_bytes=56 * MIB),
        cost_estimate=pl.CostEstimate(
            flops=4 * steps * PAIR * count * rows_f * width,
            bytes_accessed=steps * PAIR * rows_f * width * 8,
            transcendentals=0,
        ),
        name="update",
    )(
        place,
        first,
        second,
        table,
        touched,
        words,
        accum,
        noise,
        w_hidden,
        rows_t,
        dense_noise,
        *kept,
    )


def swap(array, axis, apart):
    size = lax.axis_size(axis)
    return lax.ppermute(array, axis, [(i, i ^ apart) for i in range(size)])


def body(table, accum, w_hidden, w_out, ids, labels, touched, row_noise, dense_noise):
    f_dev, rows_f = table.shape[:2]
    b_dev = labels.shape[0]
    low = touched.shape[1] // DIGITS
    groups, tables = lax.axis_size("group"), lax.axis_size("table")
    own = lax.axis_index("table").astype(jnp.int32)
    group = lax.axis_index("group").astype(jnp.int32)
    pairs = f_dev // 2 // PAIR
    base = (group & 1) * pairs
    far_base = pairs - base

    packed = ids[0::2] | (ids[1::2] << HALF)
    place = jnp.stack([own, group, base, far_base])
    halves = [lax.dynamic_slice_in_dim(packed, start, pairs, 0) for start in (base, far_base)]
    ids, halves, place = lax.optimization_barrier((ids, halves, place))
    packed = [swap(halves[d & 1], "group", d) for d in range(1, groups)]

    sent, rows_t, words, own_codes = pool(place, table, touched, ids, w_hidden, b_dev)
    packed = jnp.stack(packed)
    stops = [pairs * share // 4 for share in range(5)]

    def more_codes(number, codes, waits, ready=None):
        if stops[number + 1] > stops[number]:
            begin = words
            if ready is not None:
                begin, ready = lax.optimization_barrier((words, ready))
            codes = code_counts(
                place, begin, packed, low, stops[number], stops[number + 1], codes
            )
        return lax.optimization_barrier((codes, waits))

    arrived = lax.all_to_all(sent, "table", split_axis=0, concat_axis=0, tiled=True)
    codes, arrived = more_codes(0, None, arrived)
    clips = clip_rows(arrived, w_out, labels, w_hidden)
    column = [clips] + [swap(clips, "group", d) for d in range(1, groups)]
    codes, column = more_codes(1, codes, column, clips)
    column = jnp.stack(column)
    near = [column] + [swap(column, "table", d) for d in range(2, tables, 2)]
    codes, near = more_codes(2, codes, near, column)
    near = jnp.stack(near)
    far = swap(near, "table", 1)
    codes, far = more_codes(3, codes, far, near)

    cut = (pairs + 1) // 2
    mine = [sum_clips(place, own_codes, codes, near, far, 0, cut)]
    theirs = [swap(mine[0], "group", 1)]
    if cut < pairs:
        codes, mine[0] = lax.optimization_barrier((codes, mine[0]))
        mine.append(sum_clips(place, own_codes, codes, near, far, cut, pairs))
        theirs.append(swap(mine[1], "group", 1))
    given = (table, touched, words, accum.reshape(f_dev, rows_f // LANES, LANES), row_noise)
    given += (w_hidden, rows_t, dense_noise)
    found = update_rows(place, BASE, mine, *given)
    found = update_rows(place, FAR_BASE, theirs, *given, found)
    new_table, new_accum, dense = found
    return new_table, new_accum.reshape(f_dev, rows_f), dense


def solution(mesh):
    in_specs = (
        P("table", None, None),
        P("table", None),
        P(),
        P(),
        P("table", None, "group"),
        P(("group", "table")),
        P("table", None),
        P("table", None, None),
        P("table", "group", None),
    )
    out_specs = (P("table", None, None), P("table", None), P("table", "group", None))
    return jax.shard_map(body, mesh=mesh, in_specs=in_specs, out_specs=out_specs, check_vma=False)
```

time: 132 us -> 132 us (level)
  waiting for transfers between devices: 0.75 us -> 19.5 us
  between operations: 14.2 us -> 0.79 us
  Pallas kernels: 93.2 us -> 83.6 us
  starting transfers between devices: 15.8 us -> 19.9 us
    ppermute x14 -> x12, waiting for transfers between devices: 0.72 us -> 19.5 us  [swap(): return lax.ppermute(array, axis, [(i, i ^ apart) for i in range(size)])]
    pallas_call x4, Pallas kernels: 21.5 us -> 14.2 us  [code_counts(): pl.pallas_call(code_kernel, grid_spec=pltpu.PrefetchScalarGridSpec(num_sc...]
    all_to_all x0 -> x1, starting transfers between devices: none -> 5.31 us  [body(): lax.all_to_all(sent, 'table', split_axis=0, concat_axis=0, tiled=True)]
    pallas_call x2 -> x5, Pallas kernels: 45.3 us -> 44.1 us  [the longest x2 29.2 us: update_rows(): pl.pallas_call(functools.partial(update_kernel, base=base, cut=cut), grid...]
    ppermute x14 -> x12, starting transfers between devices: 15.7 us -> 14.6 us  [swap(): return lax.ppermute(array, axis, [(i, i ^ apart) for i in range(size)])]
    unnamed x20 -> x26, local copies, waits for them, and re-layouts: 5.55 us -> 6.15 us
  transfers between devices with their start and end apart: 15 -> 13, of which waited for: 1 -> 6; matrix products, arithmetic and copies ran while one was open for 1% -> 1% of each run, Pallas kernels for 36% -> 22%
where the time goes in v2:
time: 132 us
  Pallas kernels  83.6 us (63%)
  starting transfers between devices  19.9 us (15%)
  waiting for transfers between devices  19.5 us (15%)
  local copies, waits for them, and re-layouts  6.29 us (5%)
  other arithmetic  1.8 us (1%)
    pallas_call x2, Pallas kernels, update_rows(): pl.pallas_call(functools.partial(update_kernel, base=base, cut=cut), grid...  29.2 us
    pallas_call x1, Pallas kernels, pool(): pl.pallas_call(pool_kernel, grid_spec=pltpu.PrefetchScalarGridSpec(num_sc...  25.3 us
    ppermute x12, waiting for transfers between devices, swap(): return lax.ppermute(array, axis, [(i, i ^ apart) for i in range(size)])  19.5 us
    ppermute x12, starting transfers between devices, swap(): return lax.ppermute(array, axis, [(i, i ^ apart) for i in range(size)])  14.6 us
    pallas_call x4, Pallas kernels, code_counts(): pl.pallas_call(code_kernel, grid_spec=pltpu.PrefetchScalarGridSpec(num_sc...  14.2 us
    pallas_call x2, Pallas kernels, sum_clips(): pl.pallas_call(sum_kernel, grid_spec=pltpu.PrefetchScalarGridSpec(num_sca...  13.5 us
    unnamed x26, local copies, waits for them, and re-layouts  6.15 us
    all_to_all x1, starting transfers between devices, body(): lax.all_to_all(sent, 'table', split_axis=0, concat_axis=0, tiled=True)  5.31 us
  transfers between devices with their start and end apart: 13, of which 6 were waited for; matrix products, arithmetic and copies ran while one was open for 1% of the time, Pallas kernels for 22%

profile of v2, /device:TPU:0, one launch (start us, length us, event | category | flops | bytes accessed | tf_op | source)
XLA Modules:
  0.0 131.8 jit_solution(2366667779508264547)
XLA Ops:
  0.6 1.1 shift-left_or_fusion
  2.4 25.3 %pool.1 = (bf16[8,160,128]{2,1,0:T(8,128)(2,1)}, bf16[16,128,512]{2,1,0:T(8,128)(2,1)}, s32[16,8,128]{2,1,0:T(8,128)}, s16[16,128,1024]{2,1,0:T(8,128)(2,1)}) custom-call(s32[4]{0:T(128)} %pad_add_fusion.1.place_ref, f32[16,2048,128]{2,1,0:T(8,128)} %table_ref.5, s32[16,512]{1,0:T(8,128)} %touched_ref.5, s32[16,8,1024]{2,1,0:T(8,128)} %ids_ref, ...), custom_call_target="tpu_custom_call" | custom-call | flops 17179869184 | bytes 16777216 | tf_op jit(solution)/shard_map/pool/pallas_call | solution.py:231
  27.6 5.3 %all-to-all-start = ((bf16[8,160,128]{2,1,0:T(8,128)(2,1)}), bf16[8,160,128]{2,1,0:T(8,128)(2,1)S(1)}, u32[]{:S(2)}, u32[]{:S(2)}) async-start(bf16[8,160,128]{2,1,0:T(8,128)(2,1)} %get-tuple-element.42), calls=%async_computation | async-start | bytes 655360 | tf_op jit(solution)/shard_map/all_to_all | solution.py:671
  33.0 2.6 %collective-permute-start.1 = (s32[4,8,1024]{2,1,0:T(8,128)S(1)}, s32[4,8,1024]{2,1,0:T(8,128)S(1)}, u32[]{:S(2)}, u32[]{:S(2)}) collective-permute-start(s32[4,8,1024]{2,1,0:T(8,128)S(1)} %get-tuple-element.41), channel_id=1, source_target_pairs={{0,16},{8,24},{16,0},{24,8},{1,17},{9,25},{17,1},{25,9},{2,18},{10... | collective-permute-start | bytes 393224 | tf_op jit(solution)/shard_map/ppermute | solution.py:637
  35.6 1.4 %collective-permute-start.2 = (s32[4,8,1024]{2,1,0:T(8,128)S(1)}, s32[4,8,1024]{2,1,0:T(8,128)S(1)}, u32[]{:S(2)}, u32[]{:S(2)}) collective-permute-start(s32[4,8,1024]{2,1,0:T(8,128)S(1)} %get-tuple-element.40), channel_id=1, source_target_pairs={{0,24},{8,16},{16,8},{24,0},{1,25},{9,17},{17,9},{25,1},{2,26},{10... | collective-permute-start | bytes 393224 | tf_op jit(solution)/shard_map/ppermute | solution.py:637
  37.3 8.5 %collective-permute-done.1 = s32[4,8,1024]{2,1,0:T(8,128)S(1)} collective-permute-done((s32[4,8,1024]{2,1,0:T(8,128)S(1)}, s32[4,8,1024]{2,1,0:T(8,128)S(1)}, u32[]{:S(2)}, u32[]{:S(2)}) %collective-permute-start.1) | collective-permute-done | bytes 131104 | tf_op jit(solution)/shard_map/ppermute | solution.py:637
  45.8 0.9 collective-permute-done
  46.8 0.8 copy-done.2
  47.6 3.5 %code.4.rest_0_ = s16[8,128,3072]{2,1,0:T(8,128)(2,1)} custom-call(s32[4]{0:T(128)S(1)} %copy-done.6, s32[16,8,128]{2,1,0:T(8,128)S(1)} %copy-done.2, s32[3,4,8,1024]{3,2,1,0:T(8,128)S(1)} %pad_add_fusion.ids_ref), custom_call_target="tpu_custom_call" | custom-call | flops 314572800 | bytes 1572864 | tf_op jit(solution)/shard_map/code/pallas_call | solution.py:300
  51.2 2.2 %copy-done = bf16[128,128,128]{2,1,0:T(8,128)(2,1)S(1)} copy-done((bf16[128,128,128]{2,1,0:T(8,128)(2,1)S(1)}, bf16[128,128,128]{2,1,0:T(8,128)(2,1)}, u32[]{:S(2)}) %copy-start) | copy-done | bytes 4194328
  53.4 1.5 %clip.1 = bf16[128,128]{1,0:T(8,128)(2,1)S(1)} custom-call(f32[128,1]{1,0:T(8,128)S(1)} %copy.18.w_out_ref, f32[1,128]{1,0:T(1,128)S(1)} %bitcast.24, bf16[128,128,128]{2,1,0:T(8,128)(2,1)S(1)} %copy-done, bf16[8,160,128]{2,1,0:T(8,128)(2,1)S(1)} %all-to-all-done.sent_ref), custom_call_target="tpu_custom_call" | custom-call | flops 536870912 | bytes 4194304 | tf_op jit(solution)/shard_map/clip/pallas_call | solution.py:359
  54.8 3.6 %collective-permute-start.5 = (bf16[128,128]{1,0:T(8,128)(2,1)S(1)}, bf16[128,128]{1,0:T(8,128)(2,1)S(1)}, u32[]{:S(2)}, u32[]{:S(2)}) collective-permute-start(bf16[128,128]{1,0:T(8,128)(2,1)S(1)} %clip.1), channel_id=1, source_target_pairs={{0,24},{8,16},{16,8},{24,0},{1,25},{9,17},{17,9},{25,1},{2,26},{10... | collective-permute-start | bytes 98312 | tf_op jit(solution)/shard_map/ppermute | solution.py:637
  59.6 3.5 %code.5.rest_0_ = s16[8,128,3072]{2,1,0:T(8,128)(2,1)} custom-call(s32[4]{0:T(128)S(1)} %copy-done.6, s32[16,8,128]{2,1,0:T(8,128)S(1)} %copy-done.3, s32[3,4,8,1024]{3,2,1,0:T(8,128)S(1)} %pad_add_fusion.ids_ref, s16[8,128,3072]{2,1,0:T(8,128)(2,1)} %code.4.rest_0_), custom_call_target="tpu_custom_call", output_to_operand_aliasing={{}: (3, {})} | custom-call | flops 314572800 | bytes 1572864 | tf_op jit(solution)/shard_map/code/pallas_call | solution.py:300
  63.4 2.6 %collective-permute-start.8 = (bf16[4,128,128]{2,1,0:T(8,128)(2,1)S(1)}, bf16[4,128,128]{2,1,0:T(8,128)(2,1)S(1)}, u32[]{:S(2)}, u32[]{:S(2)}) collective-permute-start(bf16[4,128,128]{2,1,0:T(8,128)(2,1)S(1)} %pad_maximum_fusion.1), channel_id=1, source_target_pairs={{0,6},{1,7},{2,4},{3,5},{4,2},{5,3},{6,0},{7,1},{8,14},{9,15},{10,... | collective-permute-start | bytes 393224 | tf_op jit(solution)/shard_map/ppermute | solution.py:637
  66.9 3.5 %code.6.rest_0_ = s16[8,128,3072]{2,1,0:T(8,128)(2,1)} custom-call(s32[4]{0:T(128)S(1)} %copy-done.6, s32[16,8,128]{2,1,0:T(8,128)S(1)} %copy-done.3, s32[3,4,8,1024]{3,2,1,0:T(8,128)S(1)} %pad_add_fusion.ids_ref, s16[8,128,3072]{2,1,0:T(8,128)(2,1)} %code.5.rest_0_), custom_call_target="tpu_custom_call", output_to_operand_aliasing={{}: (3, {})} | custom-call | flops 314572800 | bytes 1572864 | tf_op jit(solution)/shard_map/code/pallas_call | solution.py:300
  70.5 1.4 %collective-permute-done.7 = bf16[4,128,128]{2,1,0:T(8,128)(2,1)S(1)} collective-permute-done((bf16[4,128,128]{2,1,0:T(8,128)(2,1)S(1)}, bf16[4,128,128]{2,1,0:T(8,128)(2,1)S(1)}, u32[]{:S(2)}, u32[]{:S(2)}) %collective-permute-start.7) | collective-permute-done | bytes 131104 | tf_op jit(solution)/shard_map/ppermute | solution.py:637
  72.2 3.5 %code.7.codes_ref = s16[8,128,3072]{2,1,0:T(8,128)(2,1)} custom-call(s32[4]{0:T(128)S(1)} %copy-done.6, s32[16,8,128]{2,1,0:T(8,128)S(1)} %copy-done.3, s32[3,4,8,1024]{3,2,1,0:T(8,128)S(1)} %pad_add_fusion.ids_ref, s16[8,128,3072]{2,1,0:T(8,128)(2,1)} %code.6.rest_0_), custom_call_target="tpu_custom_call", output_to_operand_aliasing={{}: (3, {})} | custom-call | flops 314572800 | bytes 1572864 | tf_op jit(solution)/shard_map/code/pallas_call | solution.py:300
  75.8 6.7 %sums.2.first_ref = bf16[4,512,128]{2,1,0:T(8,128)(2,1)S(1)} custom-call(s32[4]{0:T(128)S(1)} %copy-done.6, s16[16,128,1024]{2,1,0:T(8,128)(2,1)S(1)} %copy-done.1, s16[8,128,3072]{2,1,0:T(8,128)(2,1)} %code.7.codes_ref, bf16[4,4,128,128]{3,2,1,0:T(8,128)(2,1)S(1)} %pad_maximum_fusion.near_ref, bf16[4,4,128,128]{3,2,1,0:T(8,128)(2,1)S(1)} %collective-permute-done.9.far_ref), custom_call_target="tpu_custom_call" | custom-call | flops 2147483648 | bytes 4194304 | tf_op jit(solution)/shard_map/sums/pallas_call | solution.py:434
  82.5 6.8 %sums.3.second_ref = bf16[4,512,128]{2,1,0:T(8,128)(2,1)S(1)} custom-call(s32[4]{0:T(128)S(1)} %copy-done.6, s16[16,128,1024]{2,1,0:T(8,128)(2,1)S(1)} %copy-done.1, s16[8,128,3072]{2,1,0:T(8,128)(2,1)} %code.7.codes_ref, bf16[4,4,128,128]{3,2,1,0:T(8,128)(2,1)S(1)} %pad_maximum_fusion.near_ref, bf16[4,4,128,128]{3,2,1,0:T(8,128)(2,1)S(1)} %collective-permute-done.9.far_ref), custom_call_target="tpu_custom_call" | custom-call | flops 2147483648 | bytes 4194304 | tf_op jit(solution)/shard_map/sums/pallas_call | solution.py:434
  89.3 1.6 %collective-permute-start.11 = (bf16[4,512,128]{2,1,0:T(8,128)(2,1)S(1)}, bf16[4,512,128]{2,1,0:T(8,128)(2,1)S(1)}, u32[]{:S(2)}, u32[]{:S(2)}) collective-permute-start(bf16[4,512,128]{2,1,0:T(8,128)(2,1)S(1)} %sums.3.second_ref), channel_id=1, source_target_pairs={{0,8},{8,0},{16,24},{24,16},{1,9},{9,1},{17,25},{25,17},{2,10},{10... | collective-permute-start | bytes 1572872 | tf_op jit(solution)/shard_map/ppermute | solution.py:637
  92.1 14.7 %update.2 = (f32[16,2048,128]{2,1,0:T(8,128)}, f32[16,16,128]{2,1,0:T(8,128)}, f32[16,32,128]{2,1,0:T(8,128)}) custom-call(s32[4]{0:T(128)} %pad_add_fusion.1.place_ref, bf16[4,512,128]{2,1,0:T(8,128)(2,1)} %copy-done.4, bf16[4,512,128]{2,1,0:T(8,128)(2,1)} %copy-done.5, f32[16,2048,128]{2,1,0:T(8,128)} %table_ref.5, s32[16,512]{1,0:T(8,128)} %touched_ref.5, ...), custom_call_target="tpu_custom_call" | custom-call | flops 4294967296 | bytes 16777216 | tf_op jit(solution)/shard_map/update/pallas_call | solution.py:582
  106.8 8.1 %collective-permute-done.10.first_ref = bf16[4,512,128]{2,1,0:T(8,128)(2,1)S(1)} collective-permute-done((bf16[4,512,128]{2,1,0:T(8,128)(2,1)S(1)}, bf16[4,512,128]{2,1,0:T(8,128)(2,1)S(1)}, u32[]{:S(2)}, u32[]{:S(2)}) %collective-permute-start.10) | collective-permute-done | bytes 524320 | tf_op jit(solution)/shard_map/ppermute | solution.py:637
  115.8 14.5 %update.3 = (f32[16,2048,128]{2,1,0:T(8,128)}, f32[16,16,128]{2,1,0:T(8,128)}, f32[16,32,128]{2,1,0:T(8,128)}) custom-call(s32[4]{0:T(128)} %pad_add_fusion.1.place_ref, bf16[4,512,128]{2,1,0:T(8,128)(2,1)} %copy-done.9, bf16[4,512,128]{2,1,0:T(8,128)(2,1)} %copy-done.8, ...), custom_call_target="tpu_custom_call", output_to_operand_aliasing={{0}: (11, {}), {1}: (12, {}), {2}: (13, {})} | custom-call | flops 4294967296 | bytes 16777216 | tf_op jit(solution)/shard_map/update/pallas_call | solution.py:582
  130.2 1.6 %copy.22 = f32[2,8,16,128]{3,1,2,0:T(8,128)} copy(f32[2,8,16,128]{3,2,1,0:T(8,128)} %bitcast.27) | data formatting | bytes 262144
  (45 shorter events, 5.7 us)
Async XLA Ops:
  2.4 34.8 %copy-start.11 = (f32[128]{0:T(128)S(1)}, f32[128]{0:T(128)}, u32[]{:S(2)}) copy-start(f32[128]{0:T(128)} %param.12) | copy-start | bytes 1540
  2.4 44.4 %copy-start.6 = (s32[4]{0:T(128)S(1)}, s32[4]{0:T(128)}, u32[]{:S(2)}) copy-start(s32[4]{0:T(128)} %pad_add_fusion.1.place_ref) | copy-start | bytes 52
  27.6 23.5 %copy-start.7 = (f32[128]{0:T(128)S(1)}, f32[128]{0:T(128)}, u32[]{:S(2)}) copy-start(f32[128]{0:T(128)} %param.14) | copy-start | bytes 1540
  27.6 31.9 %copy-start.3 = (s32[16,8,128]{2,1,0:T(8,128)S(1)}, s32[16,8,128]{2,1,0:T(8,128)}, u32[]{:S(2)}) copy-start(s32[16,8,128]{2,1,0:T(8,128)} %get-tuple-element.56.words_ref) | copy-start | bytes 196612
  27.6 23.5 %all-to-all-start = ((bf16[8,160,128]{2,1,0:T(8,128)(2,1)}), bf16[8,160,128]{2,1,0:T(8,128)(2,1)S(1)}, u32[]{:S(2)}, u32[]{:S(2)}) async-start(bf16[8,160,128]{2,1,0:T(8,128)(2,1)} %get-tuple-element.42), calls=%async_computation | async-start | bytes 655360 | tf_op jit(solution)/shard_map/all_to_all | solution.py:671
  33.0 12.9 %collective-permute-start.1 = (s32[4,8,1024]{2,1,0:T(8,128)S(1)}, s32[4,8,1024]{2,1,0:T(8,128)S(1)}, u32[]{:S(2)}, u32[]{:S(2)}) collective-permute-start(s32[4,8,1024]{2,1,0:T(8,128)S(1)} %get-tuple-element.41), channel_id=1, source_target_pairs={{0,16},{8,24},{16,0},{24,8},{1,17},{9,25},{17,1},{25,9},{2,18},{10... | collective-permute-start | bytes 393224 | tf_op jit(solution)/shard_map/ppermute | solution.py:637
  35.6 10.2 %collective-permute-start.2 = (s32[4,8,1024]{2,1,0:T(8,128)S(1)}, s32[4,8,1024]{2,1,0:T(8,128)S(1)}, u32[]{:S(2)}, u32[]{:S(2)}) collective-permute-start(s32[4,8,1024]{2,1,0:T(8,128)S(1)} %get-tuple-element.40), channel_id=1, source_target_pairs={{0,24},{8,16},{16,8},{24,0},{1,25},{9,17},{17,9},{25,1},{2,26},{10... | collective-permute-start | bytes 393224 | tf_op jit(solution)/shard_map/ppermute | solution.py:637
  36.9 9.8 %collective-permute-start = (s32[4,8,1024]{2,1,0:T(8,128)S(1)}, s32[4,8,1024]{2,1,0:T(8,128)S(1)}, u32[]{:S(2)}, u32[]{:S(2)}) collective-permute-start(s32[4,8,1024]{2,1,0:T(8,128)S(1)} %get-tuple-element.40), channel_id=1, source_target_pairs={{0,8},{8,0},{16,24},{24,16},{1,9},{9,1},{17,25},{25,17},{2,10},{10... | collective-permute-start | bytes 393224 | tf_op jit(solution)/shard_map/ppermute | solution.py:637
  46.8 0.8 copy-start.2
  51.2 2.2 %copy-start = (bf16[128,128,128]{2,1,0:T(8,128)(2,1)S(1)}, bf16[128,128,128]{2,1,0:T(8,128)(2,1)}, u32[]{:S(2)}) copy-start(bf16[128,128,128]{2,1,0:T(8,128)(2,1)} %w_ref.7) | copy-start | bytes 12582916
  54.8 8.3 %collective-permute-start.5 = (bf16[128,128]{1,0:T(8,128)(2,1)S(1)}, bf16[128,128]{1,0:T(8,128)(2,1)S(1)}, u32[]{:S(2)}, u32[]{:S(2)}) collective-permute-start(bf16[128,128]{1,0:T(8,128)(2,1)S(1)} %clip.1), channel_id=1, source_target_pairs={{0,24},{8,16},{16,8},{24,0},{1,25},{9,17},{17,9},{25,1},{2,26},{10... | collective-permute-start | bytes 98312 | tf_op jit(solution)/shard_map/ppermute | solution.py:637
  58.4 4.9 %collective-permute-start.4 = (bf16[128,128]{1,0:T(8,128)(2,1)S(1)}, bf16[128,128]{1,0:T(8,128)(2,1)S(1)}, u32[]{:S(2)}, u32[]{:S(2)}) collective-permute-start(bf16[128,128]{1,0:T(8,128)(2,1)S(1)} %clip.1), channel_id=1, source_target_pairs={{0,16},{8,24},{16,0},{24,8},{1,17},{9,25},{17,1},{25,9},{2,18},{10... | collective-permute-start | bytes 98312 | tf_op jit(solution)/shard_map/ppermute | solution.py:637
  59.1 4.3 %collective-permute-start.3 = (bf16[128,128]{1,0:T(8,128)(2,1)S(1)}, bf16[128,128]{1,0:T(8,128)(2,1)S(1)}, u32[]{:S(2)}, u32[]{:S(2)}) collective-permute-start(bf16[128,128]{1,0:T(8,128)(2,1)S(1)} %clip.1), channel_id=1, source_target_pairs={{0,8},{8,0},{16,24},{24,16},{1,9},{9,1},{17,25},{25,17},{2,10},{10... | collective-permute-start | bytes 98312 | tf_op jit(solution)/shard_map/ppermute | solution.py:637
  63.4 7.1 %collective-permute-start.8 = (bf16[4,128,128]{2,1,0:T(8,128)(2,1)S(1)}, bf16[4,128,128]{2,1,0:T(8,128)(2,1)S(1)}, u32[]{:S(2)}, u32[]{:S(2)}) collective-permute-start(bf16[4,128,128]{2,1,0:T(8,128)(2,1)S(1)} %pad_maximum_fusion.1), channel_id=1, source_target_pairs={{0,6},{1,7},{2,4},{3,5},{4,2},{5,3},{6,0},{7,1},{8,14},{9,15},{10,... | collective-permute-start | bytes 393224 | tf_op jit(solution)/shard_map/ppermute | solution.py:637
  66.0 5.8 %collective-permute-start.7 = (bf16[4,128,128]{2,1,0:T(8,128)(2,1)S(1)}, bf16[4,128,128]{2,1,0:T(8,128)(2,1)S(1)}, u32[]{:S(2)}, u32[]{:S(2)}) collective-permute-start(bf16[4,128,128]{2,1,0:T(8,128)(2,1)S(1)} %pad_maximum_fusion.1), channel_id=1, source_target_pairs={{0,4},{1,5},{2,6},{3,7},{4,0},{5,1},{6,2},{7,3},{8,12},{9,13},{10,... | collective-permute-start | bytes 393224 | tf_op jit(solution)/shard_map/ppermute | solution.py:637
  66.6 5.5 %collective-permute-start.6 = (bf16[4,128,128]{2,1,0:T(8,128)(2,1)S(1)}, bf16[4,128,128]{2,1,0:T(8,128)(2,1)S(1)}, u32[]{:S(2)}, u32[]{:S(2)}) collective-permute-start(bf16[4,128,128]{2,1,0:T(8,128)(2,1)S(1)} %pad_maximum_fusion.1), channel_id=1, source_target_pairs={{0,2},{1,3},{2,0},{3,1},{4,6},{5,7},{6,4},{7,5},{8,10},{9,11},{10,... | collective-permute-start | bytes 393224 | tf_op jit(solution)/shard_map/ppermute | solution.py:637
  72.1 3.6 %copy-start.1 = (s16[16,128,1024]{2,1,0:T(8,128)(2,1)S(1)}, s16[16,128,1024]{2,1,0:T(8,128)(2,1)}, u32[]{:S(2)}) copy-start(s16[16,128,1024]{2,1,0:T(8,128)(2,1)} %get-tuple-element.38.own_codes_ref) | copy-start | bytes 12582916
  72.1 3.6 %collective-permute-start.9 = (bf16[4,4,128,128]{3,2,1,0:T(8,128)(2,1)S(1)}, bf16[4,4,128,128]{3,2,1,0:T(8,128)(2,1)S(1)}, u32[]{:S(2)}, u32[]{:S(2)}) collective-permute-start(bf16[4,4,128,128]{3,2,1,0:T(8,128)(2,1)S(1)} %pad_maximum_fusion.near_ref), channel_id=1, source_target_pairs={{0,1},{1,0},{2,3},{3,2},{4,5},{5,4},{6,7},{7,6},{8,9},{9,8},{10,11... | collective-permute-start | bytes 1572872 | tf_op jit(solution)/shard_map/ppermute | solution.py:637
  82.5 9.6 %copy-start.4 = (bf16[4,512,128]{2,1,0:T(8,128)(2,1)}, bf16[4,512,128]{2,1,0:T(8,128)(2,1)S(1)}, u32[]{:S(2)}) copy-start(bf16[4,512,128]{2,1,0:T(8,128)(2,1)S(1)} %sums.2.first_ref) | copy-start | bytes 1572868
  82.5 8.9 %copy-start.10 = (f32[16,2048]{1,0:T(8,128)S(1)}, f32[16,2048]{1,0:T(8,128)}, u32[]{:S(2)}) copy-start(f32[16,2048]{1,0:T(8,128)} %param.10) | copy-start | bytes 393220
  89.3 2.8 %copy-start.5 = (bf16[4,512,128]{2,1,0:T(8,128)(2,1)}, bf16[4,512,128]{2,1,0:T(8,128)(2,1)S(1)}, u32[]{:S(2)}) copy-start(bf16[4,512,128]{2,1,0:T(8,128)(2,1)S(1)} %sums.3.second_ref) | copy-start | bytes 1572868
  89.3 17.5 %collective-permute-start.11 = (bf16[4,512,128]{2,1,0:T(8,128)(2,1)S(1)}, bf16[4,512,128]{2,1,0:T(8,128)(2,1)S(1)}, u32[]{:S(2)}, u32[]{:S(2)}) collective-permute-start(bf16[4,512,128]{2,1,0:T(8,128)(2,1)S(1)} %sums.3.second_ref), channel_id=1, source_target_pairs={{0,8},{8,0},{16,24},{24,16},{1,9},{9,1},{17,25},{25,17},{2,10},{10... | collective-permute-start | bytes 1572872 | tf_op jit(solution)/shard_map/ppermute | solution.py:637
  90.9 24.0 %collective-permute-start.10 = (bf16[4,512,128]{2,1,0:T(8,128)(2,1)S(1)}, bf16[4,512,128]{2,1,0:T(8,128)(2,1)S(1)}, u32[]{:S(2)}, u32[]{:S(2)}) collective-permute-start(bf16[4,512,128]{2,1,0:T(8,128)(2,1)S(1)} %sums.2.first_ref), channel_id=1, source_target_pairs={{0,8},{8,0},{16,24},{24,16},{1,9},{9,1},{17,25},{25,17},{2,10},{10... | collective-permute-start | bytes 1572872 | tf_op jit(solution)/shard_map/ppermute | solution.py:637
  106.8 8.1 %copy-start.8 = (bf16[4,512,128]{2,1,0:T(8,128)(2,1)}, bf16[4,512,128]{2,1,0:T(8,128)(2,1)S(1)}, u32[]{:S(2)}) copy-start(bf16[4,512,128]{2,1,0:T(8,128)(2,1)S(1)} %collective-permute-done.11.second_ref) | copy-start | bytes 1572868
  (1 other events, 0.8 us)

commit v3 on v2

--- a/solution.py
+++ b/solution.py
@@ -73,14 +73,15 @@
 
 
 def tally(place, slots, where):
-    total = jnp.zeros(place.shape, jnp.int16)
+    total = None
     nothing = jnp.zeros(place.shape, jnp.int16)
     wide = (HALF, LANES)
     for hot in range(slots.shape[1]):
         one_group = jnp.broadcast_to(slots[0, hot : hot + 1, where], wide).astype(jnp.int16)
         one_code = jnp.broadcast_to(slots[1, hot : hot + 1, where], wide).astype(jnp.int16)
         hit = place == jnp.broadcast_to(one_group[None], place.shape)
-        total = total + jnp.where(hit, jnp.broadcast_to(one_code[None], place.shape), nothing)
+        part = jnp.where(hit, jnp.broadcast_to(one_code[None], place.shape), nothing)
+        total = part if total is None else total + part
     return total.reshape(-1, LANES)
 
 
@@ -515,8 +516,11 @@
         touched = jnp.concatenate([touched[:, lanes] for lanes in sections * 2], axis=0)
         lines = [accum_ref[side, number : number + 1] for number in range(rows_f // LANES)]
         old = pick_lanes(lines, touched >> 7, touched & (LANES - 1))
+        extra = [
+            jnp.sum(jnp.where(eye, mean[rows], 0.0), axis=0, keepdims=True) for rows in sections
+        ]
         ones = jnp.where(eye, 1.0, 0.0).astype(jnp.bfloat16)
-        parts = split(old, 3)
+        parts = split(LEARN / jnp.sqrt(old + jnp.concatenate(extra * 2, axis=0)), 3)
         diagonal = jnp.concatenate(
             [
                 jnp.concatenate(
@@ -526,13 +530,8 @@
             ],
             axis=0,
         )
-        total = mean + dot(diagonal, jnp.full((3 * LANES, LANES), 1, jnp.bfloat16))
-        steps = listed * (LEARN / jnp.sqrt(total))
+        steps = listed * dot(diagonal, jnp.full((3 * LANES, LANES), 1, jnp.bfloat16))
         update[side] = jnp.concatenate(split(steps, 2), axis=1)
-
-        extra = [
-            jnp.sum(jnp.where(eye, mean[rows], 0.0), axis=0, keepdims=True) for rows in sections
-        ]
         words = words_ref[side]
         for half, word in enumerate((words & 0xFFFF, lax.shift_right_logical(words, HALF))):
             gain = pick_lanes(extra, word >> 10, word & (LANES - 1))
@@ -611,9 +610,7 @@
         input_output_aliases={11 + number: number for number in range(len(kept))},
         compiler_params=pltpu.CompilerParams(vmem_limit_bytes=56 * MIB),
         cost_estimate=pl.CostEstimate(
-            flops=4 * steps * PAIR * count * rows_f * width,
-            bytes_accessed=steps * PAIR * rows_f * width * 8,
-            transcendentals=0,
+            flops=steps * count * hidden, bytes_accessed=steps * count, transcendentals=0
         ),
         name="update",
     )(
@@ -668,6 +665,7 @@
             )
         return lax.optimization_barrier((codes, waits))
 
+    sent, packed = lax.optimization_barrier((sent, packed))
     arrived = lax.all_to_all(sent, "table", split_axis=0, concat_axis=0, tiled=True)
     codes, arrived = more_codes(0, None, arrived)
     clips = clip_rows(arrived, w_out, labels, w_hidden)
@@ -689,6 +687,7 @@
         theirs.append(swap(mine[1], "group", 1))
     given = (table, touched, words, accum.reshape(f_dev, rows_f // LANES, LANES), row_noise)
     given += (w_hidden, rows_t, dense_noise)
+    mine, theirs[0] = lax.optimization_barrier((mine, theirs[0]))
     found = update_rows(place, BASE, mine, *given)
     found = update_rows(place, FAR_BASE, theirs, *given, found)
     new_table, new_accum, dense = found

time: 132 us -> 124 us (0.939)
  waiting for transfers between devices: 19.5 us -> 8.89 us
  Pallas kernels: 83.6 us -> 86.5 us
    ppermute x12, waiting for transfers between devices: 19.5 us -> 5.76 us  [swap(): return lax.ppermute(array, axis, [(i, i ^ apart) for i in range(size)])]
    all_to_all x1, waiting for transfers between devices: 0.01 us -> 3.13 us  [body(): lax.all_to_all(sent, 'table', split_axis=0, concat_axis=0, tiled=True)]
    pallas_call x2, Pallas kernels: 29.2 us -> 32.2 us  [update_rows(): pl.pallas_call(functools.partial(update_kernel, base=base, cut=cut), grid...]
    all_to_all x1, starting transfers between devices: 5.31 us -> 3.95 us  [body(): lax.all_to_all(sent, 'table', split_axis=0, concat_axis=0, tiled=True)]
  transfers between devices with their start and end apart: 13 -> 13, of which waited for: 6 -> 4; matrix products, arithmetic and copies ran while one was open for 1% -> 1% of each run, Pallas kernels for 22% -> 50%
where the time goes in v3:
time: 124 us
  Pallas kernels  86.5 us (70%)
  starting transfers between devices  19.8 us (16%)
  waiting for transfers between devices  8.89 us (7%)
  local copies, waits for them, and re-layouts  6.29 us (5%)
  other arithmetic  1.8 us (1%)
    pallas_call x2, Pallas kernels, update_rows(): pl.pallas_call(functools.partial(update_kernel, base=base, cut=cut), grid...  32.2 us
    pallas_call x1, Pallas kernels, pool(): pl.pallas_call(pool_kernel, grid_spec=pltpu.PrefetchScalarGridSpec(num_sc...  25.1 us
    ppermute x12, starting transfers between devices, swap(): return lax.ppermute(array, axis, [(i, i ^ apart) for i in range(size)])  15.8 us
    pallas_call x4, Pallas kernels, code_counts(): pl.pallas_call(code_kernel, grid_spec=pltpu.PrefetchScalarGridSpec(num_sc...  14.2 us
    pallas_call x2, Pallas kernels, sum_clips(): pl.pallas_call(sum_kernel, grid_spec=pltpu.PrefetchScalarGridSpec(num_sca...  13.5 us
    unnamed x26, local copies, waits for them, and re-layouts  6.15 us
    ppermute x12, waiting for transfers between devices, swap(): return lax.ppermute(array, axis, [(i, i ^ apart) for i in range(size)])  5.76 us
    all_to_all x1, starting transfers between devices, body(): lax.all_to_all(sent, 'table', split_axis=0, concat_axis=0, tiled=True)  3.95 us
  transfers between devices with their start and end apart: 13, of which 4 were waited for; matrix products, arithmetic and copies ran while one was open for 1% of the time, Pallas kernels for 50%

profile of v3, /device:TPU:0, one launch (start us, length us, event | category | flops | bytes accessed | tf_op | source)
XLA Modules:
  0.0 124.1 jit_solution(11639119709014562601)
XLA Ops:
  0.6 1.1 shift-left_or_fusion
  2.4 5.0 %collective-permute-start.2 = (s32[4,8,1024]{2,1,0:T(8,128)S(1)}, s32[4,8,1024]{2,1,0:T(8,128)S(1)}, u32[]{:S(2)}, u32[]{:S(2)}) collective-permute-start(s32[4,8,1024]{2,1,0:T(8,128)S(1)} %get-tuple-element.45), channel_id=1, source_target_pairs={{0,24},{8,16},{16,8},{24,0},{1,25},{9,17},{17,9},{25,1},{2,26},{10... | collective-permute-start | bytes 393224 | tf_op jit(solution)/shard_map/ppermute | solution.py:634
  8.0 25.1 %pool.1 = (bf16[8,160,128]{2,1,0:T(8,128)(2,1)}, bf16[16,128,512]{2,1,0:T(8,128)(2,1)}, s32[16,8,128]{2,1,0:T(8,128)}, s16[16,128,1024]{2,1,0:T(8,128)(2,1)}) custom-call(s32[4]{0:T(128)} %pad_add_fusion.1.place_ref, f32[16,2048,128]{2,1,0:T(8,128)} %table_ref.5, s32[16,512]{1,0:T(8,128)} %touched_ref.5, s32[16,8,1024]{2,1,0:T(8,128)} %ids_ref, ...), custom_call_target="tpu_custom_call" | custom-call | flops 17179869184 | bytes 16777216 | tf_op jit(solution)/shard_map/pool/pallas_call | solution.py:232
  33.2 4.0 %all-to-all-start = ((bf16[8,160,128]{2,1,0:T(8,128)(2,1)}), bf16[8,160,128]{2,1,0:T(8,128)(2,1)S(1)}, u32[]{:S(2)}, u32[]{:S(2)}) async-start(bf16[8,160,128]{2,1,0:T(8,128)(2,1)} %get-tuple-element.48), calls=%async_computation | async-start | bytes 655360 | tf_op jit(solution)/shard_map/all_to_all | solution.py:669
  37.3 0.8 copy-done.2
  38.1 3.5 %code.4.rest_0_ = s16[8,128,3072]{2,1,0:T(8,128)(2,1)} custom-call(s32[4]{0:T(128)S(1)} %copy-done.6, s32[16,8,128]{2,1,0:T(8,128)S(1)} %copy-done.2, s32[3,4,8,1024]{3,2,1,0:T(8,128)S(1)} %pad_add_fusion.ids_ref), custom_call_target="tpu_custom_call" | custom-call | flops 314572800 | bytes 1572864 | tf_op jit(solution)/shard_map/code/pallas_call | solution.py:301
  41.6 3.1 %all-to-all-done.sent_ref = bf16[8,160,128]{2,1,0:T(8,128)(2,1)S(1)} async-done(((bf16[8,160,128]{2,1,0:T(8,128)(2,1)}), bf16[8,160,128]{2,1,0:T(8,128)(2,1)S(1)}, u32[]{:S(2)}, u32[]{:S(2)}) %all-to-all-start) | async-done | bytes 327712 | tf_op jit(solution)/shard_map/all_to_all | solution.py:669
  44.8 2.2 %copy-done = bf16[128,128,128]{2,1,0:T(8,128)(2,1)S(1)} copy-done((bf16[128,128,128]{2,1,0:T(8,128)(2,1)S(1)}, bf16[128,128,128]{2,1,0:T(8,128)(2,1)}, u32[]{:S(2)}) %copy-start) | copy-done | bytes 4194328
  47.0 1.5 %clip.1 = bf16[128,128]{1,0:T(8,128)(2,1)S(1)} custom-call(f32[128,1]{1,0:T(8,128)S(1)} %copy.18.w_out_ref, f32[1,128]{1,0:T(1,128)S(1)} %bitcast.24, bf16[128,128,128]{2,1,0:T(8,128)(2,1)S(1)} %copy-done, bf16[8,160,128]{2,1,0:T(8,128)(2,1)S(1)} %all-to-all-done.sent_ref), custom_call_target="tpu_custom_call" | custom-call | flops 536870912 | bytes 4194304 | tf_op jit(solution)/shard_map/clip/pallas_call | solution.py:360
  48.5 3.7 %collective-permute-start.5 = (bf16[128,128]{1,0:T(8,128)(2,1)S(1)}, bf16[128,128]{1,0:T(8,128)(2,1)S(1)}, u32[]{:S(2)}, u32[]{:S(2)}) collective-permute-start(bf16[128,128]{1,0:T(8,128)(2,1)S(1)} %clip.1), channel_id=1, source_target_pairs={{0,24},{8,16},{16,8},{24,0},{1,25},{9,17},{17,9},{25,1},{2,26},{10... | collective-permute-start | bytes 98312 | tf_op jit(solution)/shard_map/ppermute | solution.py:634
  52.1 0.8 collective-permute-start.3
  52.9 3.5 %code.5.rest_0_ = s16[8,128,3072]{2,1,0:T(8,128)(2,1)} custom-call(s32[4]{0:T(128)S(1)} %copy-done.6, s32[16,8,128]{2,1,0:T(8,128)S(1)} %copy-done.3, s32[3,4,8,1024]{3,2,1,0:T(8,128)S(1)} %pad_add_fusion.ids_ref, s16[8,128,3072]{2,1,0:T(8,128)(2,1)} %code.4.rest_0_), custom_call_target="tpu_custom_call", output_to_operand_aliasing={{}: (3, {})} | custom-call | flops 314572800 | bytes 1572864 | tf_op jit(solution)/shard_map/code/pallas_call | solution.py:301
  57.6 1.5 %collective-permute-start.7 = (bf16[4,128,128]{2,1,0:T(8,128)(2,1)S(1)}, bf16[4,128,128]{2,1,0:T(8,128)(2,1)S(1)}, u32[]{:S(2)}, u32[]{:S(2)}) collective-permute-start(bf16[4,128,128]{2,1,0:T(8,128)(2,1)S(1)} %pad_maximum_fusion.1), channel_id=1, source_target_pairs={{0,4},{1,5},{2,6},{3,7},{4,0},{5,1},{6,2},{7,3},{8,12},{9,13},{10,... | collective-permute-start | bytes 393224 | tf_op jit(solution)/shard_map/ppermute | solution.py:634
  59.1 1.5 %collective-permute-start.6 = (bf16[4,128,128]{2,1,0:T(8,128)(2,1)S(1)}, bf16[4,128,128]{2,1,0:T(8,128)(2,1)S(1)}, u32[]{:S(2)}, u32[]{:S(2)}) collective-permute-start(bf16[4,128,128]{2,1,0:T(8,128)(2,1)S(1)} %pad_maximum_fusion.1), channel_id=1, source_target_pairs={{0,2},{1,3},{2,0},{3,1},{4,6},{5,7},{6,4},{7,5},{8,10},{9,11},{10,... | collective-permute-start | bytes 393224 | tf_op jit(solution)/shard_map/ppermute | solution.py:634
  60.5 3.5 %code.6.rest_0_ = s16[8,128,3072]{2,1,0:T(8,128)(2,1)} custom-call(s32[4]{0:T(128)S(1)} %copy-done.6, s32[16,8,128]{2,1,0:T(8,128)S(1)} %copy-done.3, s32[3,4,8,1024]{3,2,1,0:T(8,128)S(1)} %pad_add_fusion.ids_ref, s16[8,128,3072]{2,1,0:T(8,128)(2,1)} %code.5.rest_0_), custom_call_target="tpu_custom_call", output_to_operand_aliasing={{}: (3, {})} | custom-call | flops 314572800 | bytes 1572864 | tf_op jit(solution)/shard_map/code/pallas_call | solution.py:301
  64.3 3.5 %code.7.codes_ref = s16[8,128,3072]{2,1,0:T(8,128)(2,1)} custom-call(s32[4]{0:T(128)S(1)} %copy-done.6, s32[16,8,128]{2,1,0:T(8,128)S(1)} %copy-done.3, s32[3,4,8,1024]{3,2,1,0:T(8,128)S(1)} %pad_add_fusion.ids_ref, s16[8,128,3072]{2,1,0:T(8,128)(2,1)} %code.6.rest_0_), custom_call_target="tpu_custom_call", output_to_operand_aliasing={{}: (3, {})} | custom-call | flops 314572800 | bytes 1572864 | tf_op jit(solution)/shard_map/code/pallas_call | solution.py:301
  67.9 6.8 %sums.2.first_ref = bf16[4,512,128]{2,1,0:T(8,128)(2,1)S(1)} custom-call(s32[4]{0:T(128)S(1)} %copy-done.6, s16[16,128,1024]{2,1,0:T(8,128)(2,1)S(1)} %copy-done.1, s16[8,128,3072]{2,1,0:T(8,128)(2,1)} %code.7.codes_ref, bf16[4,4,128,128]{3,2,1,0:T(8,128)(2,1)S(1)} %pad_maximum_fusion.near_ref, bf16[4,4,128,128]{3,2,1,0:T(8,128)(2,1)S(1)} %collective-permute-done.9.far_ref), custom_call_target="tpu_custom_call" | custom-call | flops 2147483648 | bytes 4194304 | tf_op jit(solution)/shard_map/sums/pallas_call | solution.py:435
  74.6 1.4 %collective-permute-start.10 = (bf16[4,512,128]{2,1,0:T(8,128)(2,1)S(1)}, bf16[4,512,128]{2,1,0:T(8,128)(2,1)S(1)}, u32[]{:S(2)}, u32[]{:S(2)}) collective-permute-start(bf16[4,512,128]{2,1,0:T(8,128)(2,1)S(1)} %sums.2.first_ref), channel_id=1, source_target_pairs={{0,8},{8,0},{16,24},{24,16},{1,9},{9,1},{17,25},{25,17},{2,10},{10... | collective-permute-start | bytes 1572872 | tf_op jit(solution)/shard_map/ppermute | solution.py:634
  76.1 6.8 %sums.3.second_ref = bf16[4,512,128]{2,1,0:T(8,128)(2,1)S(1)} custom-call(s32[4]{0:T(128)S(1)} %copy-done.6, s16[16,128,1024]{2,1,0:T(8,128)(2,1)S(1)} %copy-done.1, s16[8,128,3072]{2,1,0:T(8,128)(2,1)} %code.7.codes_ref, bf16[4,4,128,128]{3,2,1,0:T(8,128)(2,1)S(1)} %pad_maximum_fusion.near_ref, bf16[4,4,128,128]{3,2,1,0:T(8,128)(2,1)S(1)} %collective-permute-done.9.far_ref), custom_call_target="tpu_custom_call" | custom-call | flops 2147483648 | bytes 4194304 | tf_op jit(solution)/shard_map/sums/pallas_call | solution.py:435
  84.3 5.2 %collective-permute-done.10.first_ref = bf16[4,512,128]{2,1,0:T(8,128)(2,1)S(1)} collective-permute-done((bf16[4,512,128]{2,1,0:T(8,128)(2,1)S(1)}, bf16[4,512,128]{2,1,0:T(8,128)(2,1)S(1)}, u32[]{:S(2)}, u32[]{:S(2)}) %collective-permute-start.10) | collective-permute-done | bytes 524320 | tf_op jit(solution)/shard_map/ppermute | solution.py:634
  89.4 16.2 %update.2 = (f32[16,2048,128]{2,1,0:T(8,128)}, f32[16,16,128]{2,1,0:T(8,128)}, f32[16,32,128]{2,1,0:T(8,128)}) custom-call(s32[4]{0:T(128)} %pad_add_fusion.1.place_ref, bf16[4,512,128]{2,1,0:T(8,128)(2,1)} %copy-done.4, bf16[4,512,128]{2,1,0:T(8,128)(2,1)} %copy-done.5, f32[16,2048,128]{2,1,0:T(8,128)} %table_ref.5, s32[16,512]{1,0:T(8,128)} %touched_ref.5, ...), custom_call_target="tpu_custom_call" | custom-call | flops 262144 | bytes 2048 | tf_op jit(solution)/shard_map/update/pallas_call | solution.py:581
  105.7 0.8 copy-done.9
  106.5 16.0 %update.3 = (f32[16,2048,128]{2,1,0:T(8,128)}, f32[16,16,128]{2,1,0:T(8,128)}, f32[16,32,128]{2,1,0:T(8,128)}) custom-call(s32[4]{0:T(128)} %pad_add_fusion.1.place_ref, bf16[4,512,128]{2,1,0:T(8,128)(2,1)} %copy-done.8, bf16[4,512,128]{2,1,0:T(8,128)(2,1)} %copy-done.9, ...), custom_call_target="tpu_custom_call", output_to_operand_aliasing={{0}: (11, {}), {1}: (12, {}), {2}: (13, {})} | custom-call | flops 262144 | bytes 2048 | tf_op jit(solution)/shard_map/update/pallas_call | solution.py:581
  122.5 1.6 %copy.22 = f32[2,8,16,128]{3,1,2,0:T(8,128)} copy(f32[2,8,16,128]{3,2,1,0:T(8,128)} %bitcast.27) | data formatting | bytes 262144
  (45 shorter events, 4.1 us)
Async XLA Ops:
  2.4 34.8 %copy-start.11 = (f32[128]{0:T(128)S(1)}, f32[128]{0:T(128)}, u32[]{:S(2)}) copy-start(f32[128]{0:T(128)} %param.12) | copy-start | bytes 1540
  2.4 34.9 %copy-start.6 = (s32[4]{0:T(128)S(1)}, s32[4]{0:T(128)}, u32[]{:S(2)}) copy-start(s32[4]{0:T(128)} %pad_add_fusion.1.place_ref) | copy-start | bytes 52
  2.4 30.8 %collective-permute-start.2 = (s32[4,8,1024]{2,1,0:T(8,128)S(1)}, s32[4,8,1024]{2,1,0:T(8,128)S(1)}, u32[]{:S(2)}, u32[]{:S(2)}) collective-permute-start(s32[4,8,1024]{2,1,0:T(8,128)S(1)} %get-tuple-element.45), channel_id=1, source_target_pairs={{0,24},{8,16},{16,8},{24,0},{1,25},{9,17},{17,9},{25,1},{2,26},{10... | collective-permute-start | bytes 393224 | tf_op jit(solution)/shard_map/ppermute | solution.py:634
  7.4 25.7 %collective-permute-start = (s32[4,8,1024]{2,1,0:T(8,128)S(1)}, s32[4,8,1024]{2,1,0:T(8,128)S(1)}, u32[]{:S(2)}, u32[]{:S(2)}) collective-permute-start(s32[4,8,1024]{2,1,0:T(8,128)S(1)} %get-tuple-element.45), channel_id=1, source_target_pairs={{0,8},{8,0},{16,24},{24,16},{1,9},{9,1},{17,25},{25,17},{2,10},{10... | collective-permute-start | bytes 393224 | tf_op jit(solution)/shard_map/ppermute | solution.py:634
  7.4 25.7 %collective-permute-start.1 = (s32[4,8,1024]{2,1,0:T(8,128)S(1)}, s32[4,8,1024]{2,1,0:T(8,128)S(1)}, u32[]{:S(2)}, u32[]{:S(2)}) collective-permute-start(s32[4,8,1024]{2,1,0:T(8,128)S(1)} %get-tuple-element.46), channel_id=1, source_target_pairs={{0,16},{8,24},{16,0},{24,8},{1,17},{9,25},{17,1},{25,9},{2,18},{10... | collective-permute-start | bytes 393224 | tf_op jit(solution)/shard_map/ppermute | solution.py:634
  33.1 11.7 %copy-start.7 = (f32[128]{0:T(128)S(1)}, f32[128]{0:T(128)}, u32[]{:S(2)}) copy-start(f32[128]{0:T(128)} %param.14) | copy-start | bytes 1540
  33.1 19.8 %copy-start.3 = (s32[16,8,128]{2,1,0:T(8,128)S(1)}, s32[16,8,128]{2,1,0:T(8,128)}, u32[]{:S(2)}) copy-start(s32[16,8,128]{2,1,0:T(8,128)} %get-tuple-element.62.words_ref) | copy-start | bytes 196612
  33.2 11.6 %all-to-all-start = ((bf16[8,160,128]{2,1,0:T(8,128)(2,1)}), bf16[8,160,128]{2,1,0:T(8,128)(2,1)S(1)}, u32[]{:S(2)}, u32[]{:S(2)}) async-start(bf16[8,160,128]{2,1,0:T(8,128)(2,1)} %get-tuple-element.48), calls=%async_computation | async-start | bytes 655360 | tf_op jit(solution)/shard_map/all_to_all | solution.py:669
  37.3 0.8 copy-start.2
  44.8 2.2 %copy-start = (bf16[128,128,128]{2,1,0:T(8,128)(2,1)S(1)}, bf16[128,128,128]{2,1,0:T(8,128)(2,1)}, u32[]{:S(2)}) copy-start(bf16[128,128,128]{2,1,0:T(8,128)(2,1)} %w_ref.7) | copy-start | bytes 12582916
  48.5 8.0 %collective-permute-start.5 = (bf16[128,128]{1,0:T(8,128)(2,1)S(1)}, bf16[128,128]{1,0:T(8,128)(2,1)S(1)}, u32[]{:S(2)}, u32[]{:S(2)}) collective-permute-start(bf16[128,128]{1,0:T(8,128)(2,1)S(1)} %clip.1), channel_id=1, source_target_pairs={{0,24},{8,16},{16,8},{24,0},{1,25},{9,17},{17,9},{25,1},{2,26},{10... | collective-permute-start | bytes 98312 | tf_op jit(solution)/shard_map/ppermute | solution.py:634
  52.1 4.8 %collective-permute-start.4 = (bf16[128,128]{1,0:T(8,128)(2,1)S(1)}, bf16[128,128]{1,0:T(8,128)(2,1)S(1)}, u32[]{:S(2)}, u32[]{:S(2)}) collective-permute-start(bf16[128,128]{1,0:T(8,128)(2,1)S(1)} %clip.1), channel_id=1, source_target_pairs={{0,16},{8,24},{16,0},{24,8},{1,17},{9,25},{17,1},{25,9},{2,18},{10... | collective-permute-start | bytes 98312 | tf_op jit(solution)/shard_map/ppermute | solution.py:634
  52.1 4.8 %collective-permute-start.3 = (bf16[128,128]{1,0:T(8,128)(2,1)S(1)}, bf16[128,128]{1,0:T(8,128)(2,1)S(1)}, u32[]{:S(2)}, u32[]{:S(2)}) collective-permute-start(bf16[128,128]{1,0:T(8,128)(2,1)S(1)} %clip.1), channel_id=1, source_target_pairs={{0,8},{8,0},{16,24},{24,16},{1,9},{9,1},{17,25},{25,17},{2,10},{10... | collective-permute-start | bytes 98312 | tf_op jit(solution)/shard_map/ppermute | solution.py:634
  57.0 7.1 %collective-permute-start.8 = (bf16[4,128,128]{2,1,0:T(8,128)(2,1)S(1)}, bf16[4,128,128]{2,1,0:T(8,128)(2,1)S(1)}, u32[]{:S(2)}, u32[]{:S(2)}) collective-permute-start(bf16[4,128,128]{2,1,0:T(8,128)(2,1)S(1)} %pad_maximum_fusion.1), channel_id=1, source_target_pairs={{0,6},{1,7},{2,4},{3,5},{4,2},{5,3},{6,0},{7,1},{8,14},{9,15},{10,... | collective-permute-start | bytes 393224 | tf_op jit(solution)/shard_map/ppermute | solution.py:634
  57.6 6.5 %collective-permute-start.7 = (bf16[4,128,128]{2,1,0:T(8,128)(2,1)S(1)}, bf16[4,128,128]{2,1,0:T(8,128)(2,1)S(1)}, u32[]{:S(2)}, u32[]{:S(2)}) collective-permute-start(bf16[4,128,128]{2,1,0:T(8,128)(2,1)S(1)} %pad_maximum_fusion.1), channel_id=1, source_target_pairs={{0,4},{1,5},{2,6},{3,7},{4,0},{5,1},{6,2},{7,3},{8,12},{9,13},{10,... | collective-permute-start | bytes 393224 | tf_op jit(solution)/shard_map/ppermute | solution.py:634
  59.1 5.1 %collective-permute-start.6 = (bf16[4,128,128]{2,1,0:T(8,128)(2,1)S(1)}, bf16[4,128,128]{2,1,0:T(8,128)(2,1)S(1)}, u32[]{:S(2)}, u32[]{:S(2)}) collective-permute-start(bf16[4,128,128]{2,1,0:T(8,128)(2,1)S(1)} %pad_maximum_fusion.1), channel_id=1, source_target_pairs={{0,2},{1,3},{2,0},{3,1},{4,6},{5,7},{6,4},{7,5},{8,10},{9,11},{10,... | collective-permute-start | bytes 393224 | tf_op jit(solution)/shard_map/ppermute | solution.py:634
  64.2 3.6 %copy-start.1 = (s16[16,128,1024]{2,1,0:T(8,128)(2,1)S(1)}, s16[16,128,1024]{2,1,0:T(8,128)(2,1)}, u32[]{:S(2)}) copy-start(s16[16,128,1024]{2,1,0:T(8,128)(2,1)} %get-tuple-element.65.own_codes_ref) | copy-start | bytes 12582916
  64.2 3.6 %collective-permute-start.9 = (bf16[4,4,128,128]{3,2,1,0:T(8,128)(2,1)S(1)}, bf16[4,4,128,128]{3,2,1,0:T(8,128)(2,1)S(1)}, u32[]{:S(2)}, u32[]{:S(2)}) collective-permute-start(bf16[4,4,128,128]{3,2,1,0:T(8,128)(2,1)S(1)} %pad_maximum_fusion.near_ref), channel_id=1, source_target_pairs={{0,1},{1,0},{2,3},{3,2},{4,5},{5,4},{6,7},{7,6},{8,9},{9,8},{10,11... | collective-permute-start | bytes 1572872 | tf_op jit(solution)/shard_map/ppermute | solution.py:634
  74.6 14.8 %copy-start.4 = (bf16[4,512,128]{2,1,0:T(8,128)(2,1)}, bf16[4,512,128]{2,1,0:T(8,128)(2,1)S(1)}, u32[]{:S(2)}) copy-start(bf16[4,512,128]{2,1,0:T(8,128)(2,1)S(1)} %sums.2.first_ref) | copy-start | bytes 1572868
  74.6 8.9 %copy-start.10 = (f32[16,2048]{1,0:T(8,128)S(1)}, f32[16,2048]{1,0:T(8,128)}, u32[]{:S(2)}) copy-start(f32[16,2048]{1,0:T(8,128)} %param.10) | copy-start | bytes 393220
  74.6 14.8 %collective-permute-start.10 = (bf16[4,512,128]{2,1,0:T(8,128)(2,1)S(1)}, bf16[4,512,128]{2,1,0:T(8,128)(2,1)S(1)}, u32[]{:S(2)}, u32[]{:S(2)}) collective-permute-start(bf16[4,512,128]{2,1,0:T(8,128)(2,1)S(1)} %sums.2.first_ref), channel_id=1, source_target_pairs={{0,8},{8,0},{16,24},{24,16},{1,9},{9,1},{17,25},{25,17},{2,10},{10... | collective-permute-start | bytes 1572872 | tf_op jit(solution)/shard_map/ppermute | solution.py:634
  82.9 6.6 %copy-start.5 = (bf16[4,512,128]{2,1,0:T(8,128)(2,1)}, bf16[4,512,128]{2,1,0:T(8,128)(2,1)S(1)}, u32[]{:S(2)}) copy-start(bf16[4,512,128]{2,1,0:T(8,128)(2,1)S(1)} %sums.3.second_ref) | copy-start | bytes 1572868
  82.9 22.8 %collective-permute-start.11 = (bf16[4,512,128]{2,1,0:T(8,128)(2,1)S(1)}, bf16[4,512,128]{2,1,0:T(8,128)(2,1)S(1)}, u32[]{:S(2)}, u32[]{:S(2)}) collective-permute-start(bf16[4,512,128]{2,1,0:T(8,128)(2,1)S(1)} %sums.3.second_ref), channel_id=1, source_target_pairs={{0,8},{8,0},{16,24},{24,16},{1,9},{9,1},{17,25},{25,17},{2,10},{10... | collective-permute-start | bytes 1572872 | tf_op jit(solution)/shard_map/ppermute | solution.py:634
  89.4 16.2 %copy-start.8 = (bf16[4,512,128]{2,1,0:T(8,128)(2,1)}, bf16[4,512,128]{2,1,0:T(8,128)(2,1)S(1)}, u32[]{:S(2)}) copy-start(bf16[4,512,128]{2,1,0:T(8,128)(2,1)S(1)} %collective-permute-done.10.first_ref) | copy-start | bytes 1572868
  (1 other events, 0.8 us)

commit v4 on v1

--- a/solution.py
+++ b/solution.py
@@ -14,6 +14,8 @@
 HALF = 16
 BLOCK = 1024
 BATCH = 32
+ROWS = 512
+OWN, GROUP = range(2)
 PAIR = 2
 LISTED = 16
 MIB = 1 << 20
@@ -47,15 +49,19 @@
 
 
 def pick_lanes(lines, row, lane):
-    found = jnp.zeros(row.shape, lines[0].dtype)
-    for number, line in enumerate(lines):
-        got = jnp.take_along_axis(jnp.broadcast_to(line, row.shape), lane, axis=1)
-        found = jnp.where(row == number, got, found)
-    return found
+    got = [
+        jnp.take_along_axis(jnp.broadcast_to(line, row.shape), lane, axis=1) for line in lines
+    ]
+    bit = 1
+    while len(got) > 1:
+        odd = (row & bit) != 0
+        got = [jnp.where(odd, got[i + 1], got[i]) for i in range(0, len(got), 2)]
+        bit *= 2
+    return got[0]
 
 
 def look_up(lines, ids, slots, where):
-    word = pick_lanes(lines, (ids >> 7) & (len(lines) - 1), ids & (LANES - 1))
+    word = pick_lanes(lines, ids >> 7, ids & (LANES - 1))
     upper = ids >= len(lines) * LANES
     word = jnp.where(upper, lax.shift_right_logical(word, HALF), word) & 0xFFFF
     slots[0, :, where] = word & 0xFF
@@ -68,14 +74,15 @@
 
 
 def tally(place, slots, where):
-    total = jnp.zeros(place.shape, jnp.int16)
+    total = None
     nothing = jnp.zeros(place.shape, jnp.int16)
     wide = (HALF, LANES)
     for hot in range(slots.shape[1]):
         one_group = jnp.broadcast_to(slots[0, hot : hot + 1, where], wide).astype(jnp.int16)
         one_code = jnp.broadcast_to(slots[1, hot : hot + 1, where], wide).astype(jnp.int16)
         hit = place == jnp.broadcast_to(one_group[None], place.shape)
-        total = total + jnp.where(hit, jnp.broadcast_to(one_code[None], place.shape), nothing)
+        part = jnp.where(hit, jnp.broadcast_to(one_code[None], place.shape), nothing)
+        total = part if total is None else total + part
     return total.reshape(-1, LANES)
 
 
@@ -90,12 +97,34 @@
     return jnp.concatenate(parts, axis=0)
 
 
+def spread_pairs(codes):
+    parts = []
+    lower = codes & jnp.full(codes.shape, 0xFF, jnp.int16)
+    upper = lax.shift_right_logical(codes, jnp.full(codes.shape, 8, jnp.int16))
+    for both in (lower.astype(jnp.bfloat16), upper.astype(jnp.bfloat16)):
+        up = jnp.bfloat16(128)
+        parts += [both, (both * jnp.bfloat16(1 / 16) + up) - up]
+    return jnp.concatenate(parts, axis=0)
+
+
 def scale(digit):
     return float(16**digit if digit < DIGITS - 1 else 1)
 
 
-def pool_kernel(own_ref, listed_ref, table_ref, touched_ref, ids_ref, w_ref, *rest):
-    sent_refs, (rows_ref, words_ref, codes_ref, picked, sums, same, slots) = rest[:-7], rest[-7:]
+def pool_kernel(
+    place_ref,
+    table_ref,
+    touched_ref,
+    ids_ref,
+    w_ref,
+    sent_ref,
+    rows_ref,
+    words_ref,
+    codes_ref,
+    sums,
+    same,
+    slots,
+):
     step = pl.program_id(0)
     rows_f, width = table_ref.shape[1:]
     hots, b_group = ids_ref.shape[1:]
@@ -117,13 +146,23 @@
         words = slot_words(touched_ref[pl.ds(step * PAIR + side, 1)], rows_f)
         words_ref[side] = words
         lines.append([words[number : number + 1] for number in range(words.shape[0])])
-    for start in range(0, count, BATCH):
+    lane = iota((HALF, LANES), 1)
+    columns, picked = [], []
+    for side in features:
+        row = touched_ref[pl.ds(step * PAIR + side, 1)].astype(jnp.float32)
+        column = jnp.broadcast_to(row, (LANES, count)).T.astype(jnp.int32).astype(jnp.int16)
+        columns.append(column.reshape(count // HALF, HALF, LANES))
+        picked.append(jnp.zeros((count, width), jnp.float32))
+    one = jnp.ones(columns[0].shape, jnp.bfloat16)
+    for start in range(0, rows_f, ROWS):
         for side in features:
-            batch = range(start, start + BATCH)
-            listed = [listed_ref[step * PAIR + side, slot] for slot in batch]
-            rows = [table_ref[side, pl.ds(row, 1), :] for row in listed]
-            for slot, row in zip(batch, rows):
-                picked[side, slot : slot + 1, :] = row
+            parts = []
+            for first in range(start, start + ROWS, LANES):
+                number = (lane + first).astype(jnp.int16)
+                hit = columns[side] == jnp.broadcast_to(number[None], one.shape)
+                parts.append(jnp.where(hit, one, jnp.zeros_like(one)).reshape(count, LANES))
+            rows = table_ref[side, start : start + ROWS].astype(jnp.bfloat16)
+            picked[side] = picked[side] + dot(jnp.concatenate(parts, axis=1), rows)
     rows_t, w_t = [], []
     for side in features:
         whole = picked[side].astype(jnp.bfloat16).T
@@ -171,10 +210,9 @@
 
     @pl.when(step == pl.num_programs(0) - 1)
     def _():
-        for apart, sent_ref in enumerate(sent_refs):
-            part = own_ref[0] ^ apart
-            sent_ref[:tall] = sums[part].astype(jnp.bfloat16)
-            sent_ref[tall:] = same[part].astype(jnp.bfloat16)
+        for part in range(blocks):
+            sent_ref[part, :tall] = sums[part].astype(jnp.bfloat16)
+            sent_ref[part, tall:] = same[part].astype(jnp.bfloat16)
 
 
 def each(times, step):
@@ -187,44 +225,46 @@
             step(number)
 
 
-def pool(own, table, touched, ids, w_hidden, chunk):
+def pool(place, table, touched, ids, w_hidden, chunk):
     f_dev, rows_f, width = table.shape
     hots, b_group = ids.shape[1:]
     count = touched.shape[1]
+    low = count // DIGITS
     hidden = w_hidden.shape[2]
     blocks = b_group // chunk
     repeat_rows = -(-f_dev // HALF) * HALF
     tall = hidden + HALF
-    sent = (tall + repeat_rows, chunk)
+    sent = (blocks, tall + repeat_rows, chunk)
+    steps = f_dev // PAIR
 
     def now(*shape):
-        return pl.BlockSpec((PAIR,) + shape, lambda i, o, s: (i, 0, 0))
-
-    low = count // DIGITS
-    outs = pl.pallas_call(
+        return pl.BlockSpec((PAIR,) + shape, lambda i, p: (i, 0, 0))
+
+    return pl.pallas_call(
         pool_kernel,
         grid_spec=pltpu.PrefetchScalarGridSpec(
-            num_scalar_prefetch=2,
-            grid=(f_dev // PAIR,),
+            num_scalar_prefetch=1,
+            grid=(steps,),
             in_specs=[
                 now(rows_f, width),
-                pl.BlockSpec(touched.shape, lambda i, o, s: (0, 0)),
+                pl.BlockSpec(touched.shape, lambda i, p: (0, 0)),
                 now(hots, b_group),
-                pl.BlockSpec(
-                    (PAIR, width, hidden), lambda i, o, s: (o[0] * (f_dev // PAIR) + i, 0, 0)
-                ),
+                pl.BlockSpec((PAIR, width, hidden), lambda i, p: (p[OWN] * steps + i, 0, 0)),
             ],
-            out_specs=[pl.BlockSpec(sent, lambda i, o, s: (0, 0))] * blocks
-            + [now(width, count), now(rows_f // 256, LANES), now(low, b_group)],
+            out_specs=[
+                pl.BlockSpec(sent, lambda i, p: (0, 0, 0)),
+                now(width, count),
+                now(rows_f // 256, LANES),
+                now(low, b_group),
+            ],
             scratch_shapes=[
-                pltpu.VMEM((PAIR, count, width), jnp.float32),
                 pltpu.VMEM((blocks, tall, chunk), jnp.float32),
                 pltpu.VMEM((blocks, repeat_rows, chunk), jnp.float32),
                 pltpu.VMEM((PAIR, 2, hots, min(b_group, BLOCK)), jnp.int32),
             ],
         ),
-        out_shape=[jax.ShapeDtypeStruct(sent, jnp.bfloat16)] * blocks
-        + [
+        out_shape=[
+            jax.ShapeDtypeStruct(sent, jnp.bfloat16),
             jax.ShapeDtypeStruct((f_dev, width, count), jnp.bfloat16),
             jax.ShapeDtypeStruct((f_dev, rows_f // 256, LANES), jnp.int32),
             jax.ShapeDtypeStruct((f_dev, low, b_group), jnp.int16),
@@ -236,78 +276,68 @@
             transcendentals=0,
         ),
         name="pool",
-    )(own, touched, table, touched, ids, w_hidden)
-    return outs[:-3], *outs[-3:]
-
-
-def code_kernel(place_ref, lower_ref, upper_ref, ids_ref, *rest):
+    )(place, table, touched, ids, w_hidden)
+
+
+def code_kernel(words_ref, ids_ref, *rest):
     codes_ref, slots = rest[-2:]
-    low, b_group = codes_ref.shape[2:]
+    low, b_group = codes_ref.shape[1:]
     block = min(b_group, BLOCK)
     place = places(low)
     lines = [
-        [words_ref[0, number : number + 1] for number in range(words_ref.shape[1])]
-        for words_ref in (lower_ref, upper_ref)
+        [words_ref[side, number : number + 1] for number in range(words_ref.shape[1])]
+        for side in range(PAIR)
     ]
 
     def one_block(number):
         for inner in range(0, block, LANES):
             where = pl.ds(pl.multiple_of(number * block + inner, LANES), LANES)
             packed = ids_ref[0, 0, :, where]
-            for half, ids in enumerate((packed & 0xFFFF, packed >> HALF)):
-                look_up(lines[half], ids, slots.at[half], slice(inner, inner + LANES))
+            for side, ids in enumerate((packed & 0xFFFF, packed >> HALF)):
+                look_up(lines[side], ids, slots.at[side], slice(inner, inner + LANES))
         for inner in range(0, block, LANES):
             where = pl.ds(pl.multiple_of(number * block + inner, LANES), LANES)
-            for half in range(2):
-                codes_ref[half, 0, :, where] = tally(
-                    place, slots.at[half], slice(inner, inner + LANES)
+            for side in range(PAIR):
+                codes_ref[side, :, where] = tally(
+                    place, slots.at[side], slice(inner, inner + LANES)
                 )
 
     each(b_group // block, one_block)
 
 
-def code_counts(own, words, packed, low, start, stop, before=None):
-    groups, half, hots, b_group = packed.shape
-    others = groups - 1
-    size = (stop - start) * 2 * low * others * b_group
+def code_counts(words, packed, low, start, stop, before=None):
+    others, pairs, hots, b_group = packed.shape
+    size = (stop - start) * PAIR * low * others * b_group
     kept = () if before is None else (before,)
     return pl.pallas_call(
         code_kernel,
-        grid_spec=pltpu.PrefetchScalarGridSpec(
-            num_scalar_prefetch=1,
-            grid=(stop - start, others),
-            in_specs=[
-                pl.BlockSpec((1,) + words.shape[1:], lambda f, g, o: (f + start, 0, 0)),
-                pl.BlockSpec((1,) + words.shape[1:], lambda f, g, o: (f + start + half, 0, 0)),
-                pl.BlockSpec(
-                    (1, 1, hots, b_group), lambda f, g, o: (o[0] ^ (g + 1), f + start, 0, 0)
-                ),
-            ]
-            + [pl.BlockSpec(memory_space=pl.ANY)] * len(kept),
-            out_specs=pl.BlockSpec((2, 1, low, b_group), lambda f, g, o: (0, f + start, 0, g)),
-            scratch_shapes=[pltpu.VMEM((2, 2, hots, min(b_group, BLOCK)), jnp.int32)],
-        ),
-        out_shape=jax.ShapeDtypeStruct((2, half, low, others * b_group), jnp.int16),
-        input_output_aliases={4: 0} if kept else {},
+        grid=(stop - start, others),
+        in_specs=[
+            pl.BlockSpec((PAIR,) + words.shape[1:], lambda f, g: (f + start, 0, 0)),
+            pl.BlockSpec((1, 1, hots, b_group), lambda f, g: (g, f + start, 0, 0)),
+        ]
+        + [pl.BlockSpec(memory_space=pl.ANY)] * len(kept),
+        out_specs=pl.BlockSpec((PAIR, low, b_group), lambda f, g: (f + start, 0, g)),
+        scratch_shapes=[pltpu.VMEM((PAIR, 2, hots, min(b_group, BLOCK)), jnp.int32)],
+        out_shape=jax.ShapeDtypeStruct((pairs * PAIR, low, others * b_group), jnp.int16),
+        input_output_aliases={2: 0} if kept else {},
         compiler_params=pltpu.CompilerParams(vmem_limit_bytes=48 * MIB),
         cost_estimate=pl.CostEstimate(
             flops=size * 400, bytes_accessed=size * 2, transcendentals=0
         ),
         name="code",
-    )(own, words, words, packed, *kept)
-
-
-def clip_kernel(own_ref, w_out_ref, labels_ref, w_ref, *rest):
-    sent_refs, clip_ref = rest[:-1], rest[-1]
+    )(words, packed, *kept)
+
+
+def clip_kernel(w_out_ref, labels_ref, w_ref, sent_ref, clip_ref):
     features, width, hidden = w_ref.shape
-    share = features // len(sent_refs)
+    devices = sent_ref.shape[0]
+    share = features // devices
     tall = hidden + HALF
-    own = own_ref[0]
-
     w_out = w_out_ref[...]
-    red = sent_refs[0][:tall].astype(jnp.float32)
-    for sent_ref in sent_refs[1:]:
-        red = red + sent_ref[:tall].astype(jnp.float32)
+    red = sent_ref[0, :tall].astype(jnp.float32)
+    for device in range(1, devices):
+        red = red + sent_ref[device, :tall].astype(jnp.float32)
     pre = red[:hidden]
     flat_sq = jnp.sum(red[hidden:], axis=0, keepdims=True)
     gate = jax.nn.sigmoid(pre)
@@ -318,11 +348,11 @@
     lanes = pre.shape[1]
 
     total = jnp.zeros((8, lanes), jnp.float32)
-    for apart, sent_ref in enumerate(sent_refs):
-        w_part = w_ref[pl.ds((own ^ apart) * share, share)].reshape(share * width, hidden)
+    for device in range(devices):
+        w_part = w_ref[device * share : (device + 1) * share].reshape(share * width, hidden)
         grad = dot(w_part, delta_low)
         square = jnp.sum((grad * grad).reshape(share, width // 8, 8, lanes), axis=1)
-        repeats = sent_ref[tall:].astype(jnp.float32)
+        repeats = sent_ref[device, tall:].astype(jnp.float32)
         for inner in range(share):
             total = total + square[inner] * repeats[inner : inner + 1]
     norm_sq = jnp.sum(total, axis=0, keepdims=True)
@@ -331,13 +361,13 @@
     clip_ref[...] = (factor * delta).T.astype(jnp.bfloat16)
 
 
-def clip_rows(own, sent, w_out, labels, w_hidden):
+def clip_rows(sent, w_out, labels, w_hidden):
     features, width, hidden = w_hidden.shape
     b_dev = labels.shape[0]
     vmem = pl.BlockSpec(memory_space=pltpu.VMEM)
     return pl.pallas_call(
         clip_kernel,
-        in_specs=[pl.BlockSpec(memory_space=pltpu.SMEM)] + [vmem] * (3 + len(sent)),
+        in_specs=[vmem] * 4,
         out_specs=vmem,
         out_shape=jax.ShapeDtypeStruct((b_dev, hidden), jnp.bfloat16),
         compiler_params=pltpu.CompilerParams(vmem_limit_bytes=32 * MIB),
@@ -347,7 +377,7 @@
             transcendentals=b_dev * hidden,
         ),
         name="clip",
-    )(own, w_out.reshape(hidden, 1), labels.reshape(1, b_dev), w_hidden, *sent)
+    )(w_out.reshape(hidden, 1), labels.reshape(1, b_dev), w_hidden, sent)
 
 
 def split(array, parts):
@@ -395,7 +425,7 @@
         for core, source in enumerate((near_ref, far_ref)):
             for chip in range(chips):
                 for group in range(groups):
-                    start = group * b_group + (place_ref[1] ^ (2 * chip + core)) * rows
+                    start = group * b_group + (place_ref[OWN] ^ (2 * chip + core)) * rows
                     clips[pl.ds(pl.multiple_of(start, rows), rows)] = source[chip, group]
 
     def put(side, start, stop):
@@ -408,23 +438,20 @@
             for spot, row, one_step in zip(spots, rows, steps):
                 table_out[side, spot, :] = row - one_step
 
-    def add(group, number, sums):
+    def add(group, side, number, sums):
         where = pl.ds(pl.multiple_of(number * block, block), block)
         at = pl.ds(pl.multiple_of(group * b_group + number * block, block), block)
-        found = []
-        for side in features:
-            if group == 0:
-                codes = own_codes_ref[side, :, where]
-            else:
-                start = pl.multiple_of((group - 1) * b_group + number * block, block)
-                codes = codes_ref[0, side, :, pl.ds(start, block)]
-            found.append(sums[side] + dot(spread(codes), clips[at]))
-        return tuple(found)
+        if group == 0:
+            codes = own_codes_ref[side, :, where]
+        else:
+            start = pl.multiple_of((group - 1) * b_group + number * block, block)
+            codes = codes_ref[side, :, pl.ds(start, block)]
+        return sums + dot(spread_pairs(codes), clips[at])
 
     def finish(side, sums):
-        parts = [
-            sums[digit * low : (digit + 1) * low] * (1 / scale(digit)) for digit in range(DIGITS)
-        ]
+        parts = [sums[start : start + low] for start in range(0, count, low)]
+        for pair in range(0, DIGITS, 2):
+            parts[pair] = parts[pair] - 16.0 * parts[pair + 1]
         both = jnp.concatenate(split(jnp.concatenate(parts, axis=0), 2), axis=1)
         dense = dot(rows_ref[side], both)
         dense_out[side] = dense[:, :hidden] + dense[:, hidden:] + dense_noise_ref[side]
@@ -468,20 +495,17 @@
     @pl.when(step < last)
     def _():
         table_out[...] = table_ref[...]
-        sums = tuple(jnp.zeros((count, hidden), jnp.float32) for side in features)
-        if b_group == block:
-            share = count // groups
+        share = count // groups
+        for side in features:
+            sums = jnp.zeros((count, hidden), jnp.float32)
             for group in range(groups):
-                for side in features:
-                    put(side, group * share, (group + 1) * share)
-                sums = add(group, 0, sums)
-        else:
-            for side in features:
-                put(side, 0, count)
-            for group in range(groups):
-                sums = lax.fori_loop(0, b_group // block, functools.partial(add, group), sums)
-        for side in features:
-            finish(side, sums[side])
+                put(side, group * share, (group + 1) * share)
+                if b_group == block:
+                    sums = add(group, side, 0, sums)
+                else:
+                    some = functools.partial(add, group, side)
+                    sums = lax.fori_loop(0, b_group // block, some, sums)
+            finish(side, sums)
 
     @pl.when(step == last)
     def _():
@@ -507,7 +531,7 @@
 ):
     f_dev, rows_f, width = table.shape
     low, b_group = own_codes.shape[1:]
-    half, others = codes.shape[1], codes.shape[3]
+    others = codes.shape[2]
     hidden = near.shape[-1]
     count = touched.shape[1]
     part = dense_noise.shape[1]
@@ -525,9 +549,6 @@
 
     def whole(array):
         return pl.BlockSpec(array.shape, lambda i, p, s: (0,) * array.ndim)
-
-    def code_place(i, p, s):
-        return (current(i) // (half // PAIR), current(i) % (half // PAIR), 0, 0)
 
     new_table, new_accum, dense = pl.pallas_call(
         update_kernel,
@@ -536,7 +557,7 @@
             grid=(steps + 1,),
             in_specs=[
                 now(low, b_group),
-                pl.BlockSpec((1, PAIR, low, others), code_place),
+                now(low, others),
                 whole(near),
                 whole(far),
                 before(rows_f, width),
@@ -545,9 +566,9 @@
                 now(tall, LANES),
                 now(count, width),
                 pl.BlockSpec(
-                    (PAIR, width, hidden), lambda i, p, s: (p[1] * steps + current(i), 0, 0)
+                    (PAIR, width, hidden), lambda i, p, s: (p[OWN] * steps + current(i), 0, 0)
                 ),
-                pl.BlockSpec((PAIR, part, count), lambda i, p, s: (current(i), p[0], 0)),
+                pl.BlockSpec((PAIR, part, count), lambda i, p, s: (current(i), p[GROUP], 0)),
                 now(part, hidden),
             ],
             out_specs=[before(rows_f, width), now(tall, LANES), now(part, hidden)],
@@ -596,45 +617,43 @@
     f_dev = table.shape[0]
     b_dev = labels.shape[0]
     low = touched.shape[1] // DIGITS
-    own = lax.axis_index("table")
-    group = lax.axis_index("group")
     groups, tables = lax.axis_size("group"), lax.axis_size("table")
-    place = jnp.stack([group, own]).astype(jnp.int32)
-    own_index = own.astype(jnp.int32).reshape(1)
-    group_index = group.astype(jnp.int32).reshape(1)
-
-    half = f_dev // 2
-    packed = ids[:half] | (ids[half:] << HALF)
-    ids, packed = lax.optimization_barrier((ids, packed))
-    packed = lax.all_gather(packed, "group")
-
-    sent, rows_t, slots, own_codes = pool(own_index, table, touched, ids, w_hidden, b_dev)
-    words = slots
-    stops = [half * share // 8 for share in (1, 3, 5)] + [half]
-    arrived = [sent[0]] + [swap(sent[d], "table", d) for d in range(1, tables)]
-    codes = None
-    if stops[0]:
-        codes = code_counts(group_index, words, packed, low, 0, stops[0])
-    arrived, codes = lax.optimization_barrier((arrived, codes))
-    clips = clip_rows(own_index, arrived, w_out, labels, w_hidden)
-
-    def go_on(number, codes, words, waits):
-        if stops[number] > stops[number - 1]:
-            span = (stops[number - 1], stops[number])
-            codes = code_counts(group_index, words, packed, low, *span, codes)
+    own = lax.axis_index("table").astype(jnp.int32)
+    group = lax.axis_index("group").astype(jnp.int32)
+    place = jnp.stack([own, group])
+    pairs = f_dev // PAIR
+
+    packed = ids[0::2] | (ids[1::2] << HALF)
+    ids, packed, place = lax.optimization_barrier((ids, packed, place))
+    packed = [swap(packed, "group", d) for d in range(1, groups)]
+
+    sent, rows_t, words, own_codes = pool(place, table, touched, ids, w_hidden, b_dev)
+    packed = jnp.stack(packed)
+    stops = [pairs * share // 4 for share in range(5)]
+
+    def more_codes(number, codes, waits, ready=None):
+        if stops[number + 1] > stops[number]:
+            begin = words
+            if ready is not None:
+                begin, ready = lax.optimization_barrier((words, ready))
+            codes = code_counts(
+                begin, packed, low, stops[number], stops[number + 1], codes
+            )
         return lax.optimization_barrier((codes, waits))
 
-    words, clips = lax.optimization_barrier((words, clips))
+    sent, packed = lax.optimization_barrier((sent, packed))
+    arrived = lax.all_to_all(sent, "table", split_axis=0, concat_axis=0, tiled=True)
+    codes, arrived = more_codes(0, None, arrived)
+    clips = clip_rows(arrived, w_out, labels, w_hidden)
     column = [clips] + [swap(clips, "group", d) for d in range(1, groups)]
-    codes, column = go_on(1, codes, words, column)
+    codes, column = more_codes(1, codes, column, clips)
     column = jnp.stack(column)
-    words, column = lax.optimization_barrier((words, column))
     near = [column] + [swap(column, "table", d) for d in range(2, tables, 2)]
-    codes, near = go_on(2, codes, words, near)
+    codes, near = more_codes(2, codes, near, column)
     near = jnp.stack(near)
-    words, near = lax.optimization_barrier((words, near))
     far = swap(near, "table", 1)
-    codes, far = go_on(3, codes, words, far)
+    codes, far = more_codes(3, codes, far, near)
+
     return update_rows(
         place,
         own_codes,
@@ -643,7 +662,7 @@
         far,
         table,
         touched,
-        slots,
+        words,
         accum,
         row_noise,
         w_hidden,

time: 132 us -> 138 us (1.045)
  Pallas kernels: 93.2 us -> 109 us
  between operations: 14.2 us -> 0.76 us
  starting transfers between devices: 15.8 us -> 17.7 us
    pallas_call x1, Pallas kernels: 43.8 us -> 61.4 us  [update_rows(): pl.pallas_call(update_kernel, grid_spec=pltpu.PrefetchScalarGridSpec(num_...]
    all_to_all x0 -> x1, starting transfers between devices: none -> 3.96 us  [body(): lax.all_to_all(sent, 'table', split_axis=0, concat_axis=0, tiled=True)]
    ppermute x14 -> x10, starting transfers between devices: 15.7 us -> 13.7 us  [swap(): return lax.ppermute(array, axis, [(i, i ^ apart) for i in range(size)])]
    unnamed x20 -> x18, local copies, waits for them, and re-layouts: 5.55 us -> 6.17 us
  transfers between devices with their start and end apart: 15 -> 11, of which waited for: 1 -> 1; matrix products, arithmetic and copies ran while one was open for 1% -> 1% of each run, Pallas kernels for 36% -> 34%
where the time goes in v4:
time: 138 us; the launch traced here: 137 us
  Pallas kernels  109 us (79%)
  starting transfers between devices  17.7 us (13%)
  local copies, waits for them, and re-layouts  6.28 us (5%)
  other arithmetic  1.8 us (1%)
    pallas_call x1, Pallas kernels, update_rows(): pl.pallas_call(update_kernel, grid_spec=pltpu.PrefetchScalarGridSpec(num_...  61.4 us
    pallas_call x1, Pallas kernels, pool(): pl.pallas_call(pool_kernel, grid_spec=pltpu.PrefetchScalarGridSpec(num_sc...  25.1 us
    pallas_call x4, Pallas kernels, code_counts(): pl.pallas_call(code_kernel, grid=(stop - start, others), in_specs=[pl.Blo...  21.3 us
    ppermute x10, starting transfers between devices, swap(): return lax.ppermute(array, axis, [(i, i ^ apart) for i in range(size)])  13.7 us
    unnamed x18, local copies, waits for them, and re-layouts  6.17 us
    all_to_all x1, starting transfers between devices, body(): lax.all_to_all(sent, 'table', split_axis=0, concat_axis=0, tiled=True)  3.96 us
  transfers between devices with their start and end apart: 11, of which 1 were waited for; matrix products, arithmetic and copies ran while one was open for 1% of the time, Pallas kernels for 34%

profile of v4, /device:TPU:0, one launch (start us, length us, event | category | flops | bytes accessed | tf_op | source)
XLA Modules:
  0.0 137.2 jit_solution(7760392363162541290)
XLA Ops:
  0.6 1.1 shift-left_or_fusion
  1.7 0.6 pad_add_fusion.1.place_ref
  2.3 5.0 %collective-permute-start.2 = (s32[8,8,1024]{2,1,0:T(8,128)S(1)}, s32[8,8,1024]{2,1,0:T(8,128)S(1)}, u32[]{:S(2)}, u32[]{:S(2)}) collective-permute-start(s32[8,8,1024]{2,1,0:T(8,128)S(1)} %shift-left_or_fusion), channel_id=1, source_target_pairs={{0,24},{8,16},{16,8},{24,0},{1,25},{9,17},{17,9},{25,1},{2,26},{10... | collective-permute-start | bytes 786440 | tf_op jit(solution)/shard_map/ppermute | solution.py:613
  7.4 0.6 collective-permute-start
  7.9 25.1 %pool.1 = (bf16[8,160,128]{2,1,0:T(8,128)(2,1)}, bf16[16,128,512]{2,1,0:T(8,128)(2,1)}, s32[16,8,128]{2,1,0:T(8,128)}, s16[16,128,1024]{2,1,0:T(8,128)(2,1)}) custom-call(s32[2]{0:T(128)} %pad_add_fusion.1.place_ref, f32[16,2048,128]{2,1,0:T(8,128)} %table_ref.3, s32[16,512]{1,0:T(8,128)} %touched_ref.3, s32[16,8,1024]{2,1,0:T(8,128)} %ids_ref, ...), custom_call_target="tpu_custom_call" | custom-call | flops 17179869184 | bytes 16777216 | tf_op jit(solution)/shard_map/pool/pallas_call | solution.py:243
  33.1 4.0 %all-to-all-start = ((bf16[8,160,128]{2,1,0:T(8,128)(2,1)}), bf16[8,160,128]{2,1,0:T(8,128)(2,1)S(1)}, u32[]{:S(2)}, u32[]{:S(2)}) async-start(bf16[8,160,128]{2,1,0:T(8,128)(2,1)} %get-tuple-element.39), calls=%async_computation | async-start | bytes 655360 | tf_op jit(solution)/shard_map/all_to_all | solution.py:645
  37.1 0.1 copy.15.w_out_ref
  37.2 0.8 copy-done.1
  38.1 5.3 %code.4.rest_0_ = s16[16,128,3072]{2,1,0:T(8,128)(2,1)} custom-call(s32[16,8,128]{2,1,0:T(8,128)S(1)} %copy-done.1, s32[3,8,8,1024]{3,2,1,0:T(8,128)S(1)} %pad_add_fusion.ids_ref), custom_call_target="tpu_custom_call" | custom-call | flops 629145600 | bytes 3145728 | tf_op jit(solution)/shard_map/code/pallas_call | solution.py:312
  43.4 1.3 all-to-all-done.sent_ref
  44.7 2.2 %copy-done = bf16[128,128,128]{2,1,0:T(8,128)(2,1)S(1)} copy-done((bf16[128,128,128]{2,1,0:T(8,128)(2,1)S(1)}, bf16[128,128,128]{2,1,0:T(8,128)(2,1)}, u32[]{:S(2)}) %copy-start) | copy-done | bytes 4194328
  46.9 1.5 %clip.1 = bf16[128,128]{1,0:T(8,128)(2,1)S(1)} custom-call(f32[128,1]{1,0:T(8,128)S(1)} %copy.15.w_out_ref, f32[1,128]{1,0:T(1,128)S(1)} %bitcast.22, bf16[128,128,128]{2,1,0:T(8,128)(2,1)S(1)} %copy-done, bf16[8,160,128]{2,1,0:T(8,128)(2,1)S(1)} %all-to-all-done.sent_ref), custom_call_target="tpu_custom_call" | custom-call | flops 536870912 | bytes 4194304 | tf_op jit(solution)/shard_map/clip/pallas_call | solution.py:368
  48.4 3.7 %collective-permute-start.5 = (bf16[128,128]{1,0:T(8,128)(2,1)S(1)}, bf16[128,128]{1,0:T(8,128)(2,1)S(1)}, u32[]{:S(2)}, u32[]{:S(2)}) collective-permute-start(bf16[128,128]{1,0:T(8,128)(2,1)S(1)} %clip.1), channel_id=1, source_target_pairs={{0,24},{8,16},{16,8},{24,0},{1,25},{9,17},{17,9},{25,1},{2,26},{10... | collective-permute-start | bytes 98312 | tf_op jit(solution)/shard_map/ppermute | solution.py:613
  52.1 0.8 collective-permute-start.3
  52.9 5.3 %code.5.rest_0_ = s16[16,128,3072]{2,1,0:T(8,128)(2,1)} custom-call(s32[16,8,128]{2,1,0:T(8,128)S(1)} %copy-done.2, s32[3,8,8,1024]{3,2,1,0:T(8,128)S(1)} %pad_add_fusion.ids_ref, s16[16,128,3072]{2,1,0:T(8,128)(2,1)} %code.4.rest_0_), custom_call_target="tpu_custom_call", output_to_operand_aliasing={{}: (2, {})} | custom-call | flops 629145600 | bytes 3145728 | tf_op jit(solution)/shard_map/code/pallas_call | solution.py:312
  58.3 1.6 %collective-permute-start.8 = (bf16[4,128,128]{2,1,0:T(8,128)(2,1)S(1)}, bf16[4,128,128]{2,1,0:T(8,128)(2,1)S(1)}, u32[]{:S(2)}, u32[]{:S(2)}) collective-permute-start(bf16[4,128,128]{2,1,0:T(8,128)(2,1)S(1)} %pad_maximum_fusion.1), channel_id=1, source_target_pairs={{0,6},{1,7},{2,4},{3,5},{4,2},{5,3},{6,0},{7,1},{8,14},{9,15},{10,... | collective-permute-start | bytes 393224 | tf_op jit(solution)/shard_map/ppermute | solution.py:613
  59.9 0.6 collective-permute-start.7
  60.5 1.4 collective-permute-start.6
  61.8 5.3 %code.6.rest_0_ = s16[16,128,3072]{2,1,0:T(8,128)(2,1)} custom-call(s32[16,8,128]{2,1,0:T(8,128)S(1)} %copy-done.2, s32[3,8,8,1024]{3,2,1,0:T(8,128)S(1)} %pad_add_fusion.ids_ref, s16[16,128,3072]{2,1,0:T(8,128)(2,1)} %code.5.rest_0_), custom_call_target="tpu_custom_call", output_to_operand_aliasing={{}: (2, {})} | custom-call | flops 629145600 | bytes 3145728 | tf_op jit(solution)/shard_map/code/pallas_call | solution.py:312
  67.3 0.7 copy.16
  68.1 5.3 %code.7.codes_ref = s16[16,128,3072]{2,1,0:T(8,128)(2,1)} custom-call(s32[16,8,128]{2,1,0:T(8,128)S(1)} %copy-done.2, s32[3,8,8,1024]{3,2,1,0:T(8,128)S(1)} %pad_add_fusion.ids_ref, s16[16,128,3072]{2,1,0:T(8,128)(2,1)} %code.6.rest_0_), custom_call_target="tpu_custom_call", output_to_operand_aliasing={{}: (2, {})} | custom-call | flops 629145600 | bytes 3145728 | tf_op jit(solution)/shard_map/code/pallas_call | solution.py:312
  73.4 0.8 copy-done.5
  74.2 61.4 %update.1 = (f32[16,2048,128]{2,1,0:T(8,128)}, f32[16,16,128]{2,1,0:T(8,128)}, f32[16,32,128]{2,1,0:T(8,128)}) custom-call(s32[2]{0:T(128)} %pad_add_fusion.1.place_ref, s32[16,512]{1,0:T(8,128)} %touched_ref.3, s16[16,128,1024]{2,1,0:T(8,128)(2,1)} %get-tuple-element.34.own_codes_ref, s16[16,128,3072]{2,1,0:T(8,128)(2,1)} %code.7.codes_ref, ...), custom_call_target="tpu_custom_call" | custom-call | flops 8589934592 | bytes 46137344 | tf_op jit(solution)/shard_map/update/pallas_call | solution.py:553
  135.6 1.6 %copy.19 = f32[2,8,16,128]{3,1,2,0:T(8,128)} copy(f32[2,8,16,128]{3,2,1,0:T(8,128)} %bitcast.30) | data formatting | bytes 262144
  (29 shorter events, 0.3 us)
Async XLA Ops:
  2.3 34.8 %copy-start.7 = (f32[128]{0:T(128)S(1)}, f32[128]{0:T(128)}, u32[]{:S(2)}) copy-start(f32[128]{0:T(128)} %param.12) | copy-start | bytes 1540
  2.3 30.8 %collective-permute-start.2 = (s32[8,8,1024]{2,1,0:T(8,128)S(1)}, s32[8,8,1024]{2,1,0:T(8,128)S(1)}, u32[]{:S(2)}, u32[]{:S(2)}) collective-permute-start(s32[8,8,1024]{2,1,0:T(8,128)S(1)} %shift-left_or_fusion), channel_id=1, source_target_pairs={{0,24},{8,16},{16,8},{24,0},{1,25},{9,17},{17,9},{25,1},{2,26},{10... | collective-permute-start | bytes 786440 | tf_op jit(solution)/shard_map/ppermute | solution.py:613
  7.3 25.7 %collective-permute-start.1 = (s32[8,8,1024]{2,1,0:T(8,128)S(1)}, s32[8,8,1024]{2,1,0:T(8,128)S(1)}, u32[]{:S(2)}, u32[]{:S(2)}) collective-permute-start(s32[8,8,1024]{2,1,0:T(8,128)S(1)} %shift-left_or_fusion), channel_id=1, source_target_pairs={{0,16},{8,24},{16,0},{24,8},{1,17},{9,25},{17,1},{25,9},{2,18},{10... | collective-permute-start | bytes 786440 | tf_op jit(solution)/shard_map/ppermute | solution.py:613
  7.4 25.7 %collective-permute-start = (s32[8,8,1024]{2,1,0:T(8,128)S(1)}, s32[8,8,1024]{2,1,0:T(8,128)S(1)}, u32[]{:S(2)}, u32[]{:S(2)}) collective-permute-start(s32[8,8,1024]{2,1,0:T(8,128)S(1)} %shift-left_or_fusion), channel_id=1, source_target_pairs={{0,8},{8,0},{16,24},{24,16},{1,9},{9,1},{17,25},{25,17},{2,10},{10... | collective-permute-start | bytes 786440 | tf_op jit(solution)/shard_map/ppermute | solution.py:613
  33.0 11.7 %copy-start.3 = (f32[128]{0:T(128)S(1)}, f32[128]{0:T(128)}, u32[]{:S(2)}) copy-start(f32[128]{0:T(128)} %param.14) | copy-start | bytes 1540
  33.0 19.8 %copy-start.2 = (s32[16,8,128]{2,1,0:T(8,128)S(1)}, s32[16,8,128]{2,1,0:T(8,128)}, u32[]{:S(2)}) copy-start(s32[16,8,128]{2,1,0:T(8,128)} %get-tuple-element.53.words_ref) | copy-start | bytes 196612
  33.1 11.6 %all-to-all-start = ((bf16[8,160,128]{2,1,0:T(8,128)(2,1)}), bf16[8,160,128]{2,1,0:T(8,128)(2,1)S(1)}, u32[]{:S(2)}, u32[]{:S(2)}) async-start(bf16[8,160,128]{2,1,0:T(8,128)(2,1)} %get-tuple-element.39), calls=%async_computation | async-start | bytes 655360 | tf_op jit(solution)/shard_map/all_to_all | solution.py:645
  37.2 0.8 copy-start.1
  44.7 2.2 %copy-start = (bf16[128,128,128]{2,1,0:T(8,128)(2,1)S(1)}, bf16[128,128,128]{2,1,0:T(8,128)(2,1)}, u32[]{:S(2)}) copy-start(bf16[128,128,128]{2,1,0:T(8,128)(2,1)} %w_ref.5) | copy-start | bytes 12582916
  48.4 9.8 %collective-permute-start.5 = (bf16[128,128]{1,0:T(8,128)(2,1)S(1)}, bf16[128,128]{1,0:T(8,128)(2,1)S(1)}, u32[]{:S(2)}, u32[]{:S(2)}) collective-permute-start(bf16[128,128]{1,0:T(8,128)(2,1)S(1)} %clip.1), channel_id=1, source_target_pairs={{0,24},{8,16},{16,8},{24,0},{1,25},{9,17},{17,9},{25,1},{2,26},{10... | collective-permute-start | bytes 98312 | tf_op jit(solution)/shard_map/ppermute | solution.py:613
  52.1 6.1 %collective-permute-start.4 = (bf16[128,128]{1,0:T(8,128)(2,1)S(1)}, bf16[128,128]{1,0:T(8,128)(2,1)S(1)}, u32[]{:S(2)}, u32[]{:S(2)}) collective-permute-start(bf16[128,128]{1,0:T(8,128)(2,1)S(1)} %clip.1), channel_id=1, source_target_pairs={{0,16},{8,24},{16,0},{24,8},{1,17},{9,25},{17,1},{25,9},{2,18},{10... | collective-permute-start | bytes 98312 | tf_op jit(solution)/shard_map/ppermute | solution.py:613
  52.1 6.1 %collective-permute-start.3 = (bf16[128,128]{1,0:T(8,128)(2,1)S(1)}, bf16[128,128]{1,0:T(8,128)(2,1)S(1)}, u32[]{:S(2)}, u32[]{:S(2)}) collective-permute-start(bf16[128,128]{1,0:T(8,128)(2,1)S(1)} %clip.1), channel_id=1, source_target_pairs={{0,8},{8,0},{16,24},{24,16},{1,9},{9,1},{17,25},{25,17},{2,10},{10... | collective-permute-start | bytes 98312 | tf_op jit(solution)/shard_map/ppermute | solution.py:613
  58.2 9.1 %copy-start.6 = (f32[16,2048]{1,0:T(8,128)S(1)}, f32[16,2048]{1,0:T(8,128)}, u32[]{:S(2)}) copy-start(f32[16,2048]{1,0:T(8,128)} %param.10) | copy-start | bytes 393220
  58.3 8.9 %collective-permute-start.8 = (bf16[4,128,128]{2,1,0:T(8,128)(2,1)S(1)}, bf16[4,128,128]{2,1,0:T(8,128)(2,1)S(1)}, u32[]{:S(2)}, u32[]{:S(2)}) collective-permute-start(bf16[4,128,128]{2,1,0:T(8,128)(2,1)S(1)} %pad_maximum_fusion.1), channel_id=1, source_target_pairs={{0,6},{1,7},{2,4},{3,5},{4,2},{5,3},{6,0},{7,1},{8,14},{9,15},{10,... | collective-permute-start | bytes 393224 | tf_op jit(solution)/shard_map/ppermute | solution.py:613
  59.9 7.3 %collective-permute-start.7 = (bf16[4,128,128]{2,1,0:T(8,128)(2,1)S(1)}, bf16[4,128,128]{2,1,0:T(8,128)(2,1)S(1)}, u32[]{:S(2)}, u32[]{:S(2)}) collective-permute-start(bf16[4,128,128]{2,1,0:T(8,128)(2,1)S(1)} %pad_maximum_fusion.1), channel_id=1, source_target_pairs={{0,4},{1,5},{2,6},{3,7},{4,0},{5,1},{6,2},{7,3},{8,12},{9,13},{10,... | collective-permute-start | bytes 393224 | tf_op jit(solution)/shard_map/ppermute | solution.py:613
  60.5 6.7 %collective-permute-start.6 = (bf16[4,128,128]{2,1,0:T(8,128)(2,1)S(1)}, bf16[4,128,128]{2,1,0:T(8,128)(2,1)S(1)}, u32[]{:S(2)}, u32[]{:S(2)}) collective-permute-start(bf16[4,128,128]{2,1,0:T(8,128)(2,1)S(1)} %pad_maximum_fusion.1), channel_id=1, source_target_pairs={{0,2},{1,3},{2,0},{3,1},{4,6},{5,7},{6,4},{7,5},{8,10},{9,11},{10,... | collective-permute-start | bytes 393224 | tf_op jit(solution)/shard_map/ppermute | solution.py:613
  67.2 6.1 %copy-start.4 = (bf16[4,4,128,128]{3,2,1,0:T(8,128)(2,1)}, bf16[4,4,128,128]{3,2,1,0:T(8,128)(2,1)S(1)}, u32[]{:S(2)}) copy-start(bf16[4,4,128,128]{3,2,1,0:T(8,128)(2,1)S(1)} %pad_maximum_fusion.near_ref) | copy-start | bytes 1572868
  67.2 6.1 %collective-permute-start.9 = (bf16[4,4,128,128]{3,2,1,0:T(8,128)(2,1)S(1)}, bf16[4,4,128,128]{3,2,1,0:T(8,128)(2,1)S(1)}, u32[]{:S(2)}, u32[]{:S(2)}) collective-permute-start(bf16[4,4,128,128]{3,2,1,0:T(8,128)(2,1)S(1)} %pad_maximum_fusion.near_ref), channel_id=1, source_target_pairs={{0,1},{1,0},{2,3},{3,2},{4,5},{5,4},{6,7},{7,6},{8,9},{9,8},{10,11... | collective-permute-start | bytes 1572872 | tf_op jit(solution)/shard_map/ppermute | solution.py:613
  73.4 0.8 copy-start.5

commit v5 on v4

--- a/solution.py
+++ b/solution.py
@@ -97,16 +97,6 @@
     return jnp.concatenate(parts, axis=0)
 
 
-def spread_pairs(codes):
-    parts = []
-    lower = codes & jnp.full(codes.shape, 0xFF, jnp.int16)
-    upper = lax.shift_right_logical(codes, jnp.full(codes.shape, 8, jnp.int16))
-    for both in (lower.astype(jnp.bfloat16), upper.astype(jnp.bfloat16)):
-        up = jnp.bfloat16(128)
-        parts += [both, (both * jnp.bfloat16(1 / 16) + up) - up]
-    return jnp.concatenate(parts, axis=0)
-
-
 def scale(digit):
     return float(16**digit if digit < DIGITS - 1 else 1)
 
@@ -120,7 +110,7 @@
     sent_ref,
     rows_ref,
     words_ref,
-    codes_ref,
+    counts_ref,
     sums,
     same,
     slots,
@@ -192,11 +182,13 @@
             for side in features:
                 parts = []
                 for start in (inner, inner + chunk):
-                    codes = tally(place, slots.at[side], slice(start, start + chunk))
-                    where = pl.ds(pl.multiple_of(number * block + start, chunk), chunk)
-                    codes_ref[side, :, where] = codes
-                    parts.append(spread(codes))
-                pooled = dot(rows_t[side], jnp.concatenate(parts, axis=1)).astype(jnp.bfloat16)
+                    parts.append(
+                        spread(tally(place, slots.at[side], slice(start, start + chunk)))
+                    )
+                counts = jnp.concatenate(parts, axis=1)
+                where = pl.ds(pl.multiple_of(number * block + inner, 2 * chunk), 2 * chunk)
+                counts_ref[side, :, where] = counts
+                pooled = dot(rows_t[side], counts).astype(jnp.bfloat16)
                 wide = pooled.astype(jnp.float32)
                 square += jnp.sum((wide * wide).reshape(width // HALF, HALF, 2 * chunk), axis=0)
                 pre += dot(w_t[side], pooled)
@@ -229,7 +221,6 @@
     f_dev, rows_f, width = table.shape
     hots, b_group = ids.shape[1:]
     count = touched.shape[1]
-    low = count // DIGITS
     hidden = w_hidden.shape[2]
     blocks = b_group // chunk
     repeat_rows = -(-f_dev // HALF) * HALF
@@ -255,7 +246,7 @@
                 pl.BlockSpec(sent, lambda i, p: (0, 0, 0)),
                 now(width, count),
                 now(rows_f // 256, LANES),
-                now(low, b_group),
+                now(count, b_group),
             ],
             scratch_shapes=[
                 pltpu.VMEM((blocks, tall, chunk), jnp.float32),
@@ -267,7 +258,7 @@
             jax.ShapeDtypeStruct(sent, jnp.bfloat16),
             jax.ShapeDtypeStruct((f_dev, width, count), jnp.bfloat16),
             jax.ShapeDtypeStruct((f_dev, rows_f // 256, LANES), jnp.int32),
-            jax.ShapeDtypeStruct((f_dev, low, b_group), jnp.int16),
+            jax.ShapeDtypeStruct((f_dev, count, b_group), jnp.bfloat16),
         ],
         compiler_params=pltpu.CompilerParams(vmem_limit_bytes=56 * MIB),
         cost_estimate=pl.CostEstimate(
@@ -391,7 +382,7 @@
 def update_kernel(
     place_ref,
     listed_ref,
-    own_codes_ref,
+    own_counts_ref,
     codes_ref,
     near_ref,
     far_ref,
@@ -411,11 +402,11 @@
 ):
     step = pl.program_id(0)
     last = pl.num_programs(0) - 1
-    low, b_group = own_codes_ref.shape[1:]
+    count, b_group = own_counts_ref.shape[1:]
+    low = count // DIGITS
     groups = near_ref.shape[1]
     rows_f, width = table_ref.shape[1:]
     hidden = clips.shape[1]
-    count = low * DIGITS
     block = min(b_group, BLOCK)
     features = range(PAIR)
 
@@ -438,20 +429,23 @@
             for spot, row, one_step in zip(spots, rows, steps):
                 table_out[side, spot, :] = row - one_step
 
-    def add(group, side, number, sums):
+    def add(group, number, sums):
         where = pl.ds(pl.multiple_of(number * block, block), block)
         at = pl.ds(pl.multiple_of(group * b_group + number * block, block), block)
-        if group == 0:
-            codes = own_codes_ref[side, :, where]
-        else:
-            start = pl.multiple_of((group - 1) * b_group + number * block, block)
-            codes = codes_ref[side, :, pl.ds(start, block)]
-        return sums + dot(spread_pairs(codes), clips[at])
+        found = []
+        for side in features:
+            if group == 0:
+                counts = own_counts_ref[side, :, where]
+            else:
+                start = pl.multiple_of((group - 1) * b_group + number * block, block)
+                counts = spread(codes_ref[side, :, pl.ds(start, block)])
+            found.append(sums[side] + dot(counts, clips[at]))
+        return tuple(found)
 
     def finish(side, sums):
-        parts = [sums[start : start + low] for start in range(0, count, low)]
-        for pair in range(0, DIGITS, 2):
-            parts[pair] = parts[pair] - 16.0 * parts[pair + 1]
+        parts = [
+            sums[digit * low : (digit + 1) * low] * (1 / scale(digit)) for digit in range(DIGITS)
+        ]
         both = jnp.concatenate(split(jnp.concatenate(parts, axis=0), 2), axis=1)
         dense = dot(rows_ref[side], both)
         dense_out[side] = dense[:, :hidden] + dense[:, hidden:] + dense_noise_ref[side]
@@ -479,7 +473,7 @@
             axis=0,
         )
         total = mean + dot(diagonal, jnp.full((3 * LANES, LANES), 1, jnp.bfloat16))
-        update[side] = listed * (LEARN / jnp.sqrt(total))
+        update[side] = listed * (LEARN * lax.rsqrt(total))
 
         extra = [
             jnp.sum(jnp.where(eye, mean[rows], 0.0), axis=0, keepdims=True) for rows in sections
@@ -495,17 +489,17 @@
     @pl.when(step < last)
     def _():
         table_out[...] = table_ref[...]
+        sums = tuple(jnp.zeros((count, hidden), jnp.float32) for side in features)
         share = count // groups
+        for group in range(groups):
+            for side in features:
+                put(side, group * share, (group + 1) * share)
+            if b_group == block:
+                sums = add(group, 0, sums)
+            else:
+                sums = lax.fori_loop(0, b_group // block, functools.partial(add, group), sums)
         for side in features:
-            sums = jnp.zeros((count, hidden), jnp.float32)
-            for group in range(groups):
-                put(side, group * share, (group + 1) * share)
-                if b_group == block:
-                    sums = add(group, side, 0, sums)
-                else:
-                    some = functools.partial(add, group, side)
-                    sums = lax.fori_loop(0, b_group // block, some, sums)
-            finish(side, sums)
+            finish(side, sums[side])
 
     @pl.when(step == last)
     def _():
@@ -516,7 +510,7 @@
 
 def update_rows(
     place,
-    own_codes,
+    own_counts,
     codes,
     near,
     far,
@@ -530,10 +524,10 @@
     dense_noise,
 ):
     f_dev, rows_f, width = table.shape
-    low, b_group = own_codes.shape[1:]
+    count, b_group = own_counts.shape[1:]
+    low = count // DIGITS
     others = codes.shape[2]
     hidden = near.shape[-1]
-    count = touched.shape[1]
     part = dense_noise.shape[1]
     tall = rows_f // LANES
     steps = f_dev // PAIR
@@ -556,7 +550,7 @@
             num_scalar_prefetch=2,
             grid=(steps + 1,),
             in_specs=[
-                now(low, b_group),
+                now(count, b_group),
                 now(low, others),
                 whole(near),
                 whole(far),
@@ -592,7 +586,7 @@
     )(
         place,
         touched,
-        own_codes,
+        own_counts,
         codes,
         near,
         far,
@@ -627,7 +621,7 @@
     ids, packed, place = lax.optimization_barrier((ids, packed, place))
     packed = [swap(packed, "group", d) for d in range(1, groups)]
 
-    sent, rows_t, words, own_codes = pool(place, table, touched, ids, w_hidden, b_dev)
+    sent, rows_t, words, own_counts = pool(place, table, touched, ids, w_hidden, b_dev)
     packed = jnp.stack(packed)
     stops = [pairs * share // 4 for share in range(5)]
 
@@ -656,7 +650,7 @@
 
     return update_rows(
         place,
-        own_codes,
+        own_counts,
         codes,
         near,
         far,

time: 138 us -> 121 us (0.88)
  Pallas kernels: 109 us -> 92.4 us
    pallas_call x1, Pallas kernels: 61.4 us -> 43.7 us  [update_rows(): pl.pallas_call(update_kernel, grid_spec=pltpu.PrefetchScalarGridSpec(num_...]
  transfers between devices with their start and end apart: 11 -> 11, of which waited for: 1 -> 1; matrix products, arithmetic and copies ran while one was open for 1% -> 1% of each run, Pallas kernels for 34% -> 39%
where the time goes in v5:
time: 121 us; the launch traced here: 120 us
  Pallas kernels  92.4 us (76%)
  starting transfers between devices  17.7 us (15%)
  local copies, waits for them, and re-layouts  6.29 us (5%)
  other arithmetic  1.79 us (1%)
  waiting for transfers between devices  1.38 us (1%)
    pallas_call x1, Pallas kernels, update_rows(): pl.pallas_call(update_kernel, grid_spec=pltpu.PrefetchScalarGridSpec(num_...  43.7 us
    pallas_call x1, Pallas kernels, pool(): pl.pallas_call(pool_kernel, grid_spec=pltpu.PrefetchScalarGridSpec(num_sc...  25.9 us
    pallas_call x4, Pallas kernels, code_counts(): pl.pallas_call(code_kernel, grid=(stop - start, others), in_specs=[pl.Blo...  21.3 us
    ppermute x10, starting transfers between devices, swap(): return lax.ppermute(array, axis, [(i, i ^ apart) for i in range(size)])  13.7 us
    unnamed x18, local copies, waits for them, and re-layouts  6.18 us
    all_to_all x1, starting transfers between devices, body(): lax.all_to_all(sent, 'table', split_axis=0, concat_axis=0, tiled=True)  3.96 us
  transfers between devices with their start and end apart: 11, of which 1 were waited for; matrix products, arithmetic and copies ran while one was open for 1% of the time, Pallas kernels for 39%

profile of v5, /device:TPU:0, one launch (start us, length us, event | category | flops | bytes accessed | tf_op | source)
XLA Modules:
  0.0 120.3 jit_solution(12155116941304524943)
XLA Ops:
  0.6 1.1 shift-left_or_fusion
  1.7 0.6 pad_add_fusion.1.place_ref
  2.3 5.0 %collective-permute-start.2 = (s32[8,8,1024]{2,1,0:T(8,128)S(1)}, s32[8,8,1024]{2,1,0:T(8,128)S(1)}, u32[]{:S(2)}, u32[]{:S(2)}) collective-permute-start(s32[8,8,1024]{2,1,0:T(8,128)S(1)} %shift-left_or_fusion), channel_id=1, source_target_pairs={{0,24},{8,16},{16,8},{24,0},{1,25},{9,17},{17,9},{25,1},{2,26},{10... | collective-permute-start | bytes 786440 | tf_op jit(solution)/shard_map/ppermute | solution.py:607
  7.3 0.6 collective-permute-start
  7.9 25.9 %pool.1 = (bf16[8,160,128]{2,1,0:T(8,128)(2,1)}, bf16[16,128,512]{2,1,0:T(8,128)(2,1)}, s32[16,8,128]{2,1,0:T(8,128)}, bf16[16,512,1024]{2,1,0:T(8,128)(2,1)}) custom-call(s32[2]{0:T(128)} %pad_add_fusion.1.place_ref, f32[16,2048,128]{2,1,0:T(8,128)} %table_ref.3, s32[16,512]{1,0:T(8,128)} %touched_ref.3, s32[16,8,1024]{2,1,0:T(8,128)} %ids_ref, ...), custom_call_target="tpu_custom_call" | custom-call | flops 17179869184 | bytes 16777216 | tf_op jit(solution)/shard_map/pool/pallas_call | solution.py:234
  33.9 4.0 %all-to-all-start = ((bf16[8,160,128]{2,1,0:T(8,128)(2,1)}), bf16[8,160,128]{2,1,0:T(8,128)(2,1)S(1)}, u32[]{:S(2)}, u32[]{:S(2)}) async-start(bf16[8,160,128]{2,1,0:T(8,128)(2,1)} %get-tuple-element.39), calls=%async_computation | async-start | bytes 655360 | tf_op jit(solution)/shard_map/all_to_all | solution.py:639
  37.9 0.1 copy.15.w_out_ref
  38.0 0.8 copy-done.1
  38.8 5.3 %code.4.rest_0_ = s16[16,128,3072]{2,1,0:T(8,128)(2,1)} custom-call(s32[16,8,128]{2,1,0:T(8,128)S(1)} %copy-done.1, s32[3,8,8,1024]{3,2,1,0:T(8,128)S(1)} %pad_add_fusion.ids_ref), custom_call_target="tpu_custom_call" | custom-call | flops 629145600 | bytes 3145728 | tf_op jit(solution)/shard_map/code/pallas_call | solution.py:303
  44.2 1.4 %all-to-all-done.sent_ref = bf16[8,160,128]{2,1,0:T(8,128)(2,1)S(1)} async-done(((bf16[8,160,128]{2,1,0:T(8,128)(2,1)}), bf16[8,160,128]{2,1,0:T(8,128)(2,1)S(1)}, u32[]{:S(2)}, u32[]{:S(2)}) %all-to-all-start) | async-done | bytes 327712 | tf_op jit(solution)/shard_map/all_to_all | solution.py:639
  45.5 2.2 %copy-done = bf16[128,128,128]{2,1,0:T(8,128)(2,1)S(1)} copy-done((bf16[128,128,128]{2,1,0:T(8,128)(2,1)S(1)}, bf16[128,128,128]{2,1,0:T(8,128)(2,1)}, u32[]{:S(2)}) %copy-start) | copy-done | bytes 4194328
  47.7 1.5 %clip.1 = bf16[128,128]{1,0:T(8,128)(2,1)S(1)} custom-call(f32[128,1]{1,0:T(8,128)S(1)} %copy.15.w_out_ref, f32[1,128]{1,0:T(1,128)S(1)} %bitcast.22, bf16[128,128,128]{2,1,0:T(8,128)(2,1)S(1)} %copy-done, bf16[8,160,128]{2,1,0:T(8,128)(2,1)S(1)} %all-to-all-done.sent_ref), custom_call_target="tpu_custom_call" | custom-call | flops 536870912 | bytes 4194304 | tf_op jit(solution)/shard_map/clip/pallas_call | solution.py:359
  49.2 3.7 %collective-permute-start.5 = (bf16[128,128]{1,0:T(8,128)(2,1)S(1)}, bf16[128,128]{1,0:T(8,128)(2,1)S(1)}, u32[]{:S(2)}, u32[]{:S(2)}) collective-permute-start(bf16[128,128]{1,0:T(8,128)(2,1)S(1)} %clip.1), channel_id=1, source_target_pairs={{0,24},{8,16},{16,8},{24,0},{1,25},{9,17},{17,9},{25,1},{2,26},{10... | collective-permute-start | bytes 98312 | tf_op jit(solution)/shard_map/ppermute | solution.py:607
  52.8 0.8 collective-permute-start.3
  53.6 5.3 %code.5.rest_0_ = s16[16,128,3072]{2,1,0:T(8,128)(2,1)} custom-call(s32[16,8,128]{2,1,0:T(8,128)S(1)} %copy-done.2, s32[3,8,8,1024]{3,2,1,0:T(8,128)S(1)} %pad_add_fusion.ids_ref, s16[16,128,3072]{2,1,0:T(8,128)(2,1)} %code.4.rest_0_), custom_call_target="tpu_custom_call", output_to_operand_aliasing={{}: (2, {})} | custom-call | flops 629145600 | bytes 3145728 | tf_op jit(solution)/shard_map/code/pallas_call | solution.py:303
  59.0 1.6 %collective-permute-start.8 = (bf16[4,128,128]{2,1,0:T(8,128)(2,1)S(1)}, bf16[4,128,128]{2,1,0:T(8,128)(2,1)S(1)}, u32[]{:S(2)}, u32[]{:S(2)}) collective-permute-start(bf16[4,128,128]{2,1,0:T(8,128)(2,1)S(1)} %pad_maximum_fusion.1), channel_id=1, source_target_pairs={{0,6},{1,7},{2,4},{3,5},{4,2},{5,3},{6,0},{7,1},{8,14},{9,15},{10,... | collective-permute-start | bytes 393224 | tf_op jit(solution)/shard_map/ppermute | solution.py:607
  60.7 0.6 collective-permute-start.7
  61.2 1.4 %collective-permute-start.6 = (bf16[4,128,128]{2,1,0:T(8,128)(2,1)S(1)}, bf16[4,128,128]{2,1,0:T(8,128)(2,1)S(1)}, u32[]{:S(2)}, u32[]{:S(2)}) collective-permute-start(bf16[4,128,128]{2,1,0:T(8,128)(2,1)S(1)} %pad_maximum_fusion.1), channel_id=1, source_target_pairs={{0,2},{1,3},{2,0},{3,1},{4,6},{5,7},{6,4},{7,5},{8,10},{9,11},{10,... | collective-permute-start | bytes 393224 | tf_op jit(solution)/shard_map/ppermute | solution.py:607
  62.6 5.3 %code.6.rest_0_ = s16[16,128,3072]{2,1,0:T(8,128)(2,1)} custom-call(s32[16,8,128]{2,1,0:T(8,128)S(1)} %copy-done.2, s32[3,8,8,1024]{3,2,1,0:T(8,128)S(1)} %pad_add_fusion.ids_ref, s16[16,128,3072]{2,1,0:T(8,128)(2,1)} %code.5.rest_0_), custom_call_target="tpu_custom_call", output_to_operand_aliasing={{}: (2, {})} | custom-call | flops 629145600 | bytes 3145728 | tf_op jit(solution)/shard_map/code/pallas_call | solution.py:303
  68.1 0.7 copy.16
  68.8 5.3 %code.7.codes_ref = s16[16,128,3072]{2,1,0:T(8,128)(2,1)} custom-call(s32[16,8,128]{2,1,0:T(8,128)S(1)} %copy-done.2, s32[3,8,8,1024]{3,2,1,0:T(8,128)S(1)} %pad_add_fusion.ids_ref, s16[16,128,3072]{2,1,0:T(8,128)(2,1)} %code.6.rest_0_), custom_call_target="tpu_custom_call", output_to_operand_aliasing={{}: (2, {})} | custom-call | flops 629145600 | bytes 3145728 | tf_op jit(solution)/shard_map/code/pallas_call | solution.py:303
  74.1 0.8 copy-done.5
  74.9 43.7 %update.1 = (f32[16,2048,128]{2,1,0:T(8,128)}, f32[16,16,128]{2,1,0:T(8,128)}, f32[16,32,128]{2,1,0:T(8,128)}) custom-call(s32[2]{0:T(128)} %pad_add_fusion.1.place_ref, s32[16,512]{1,0:T(8,128)} %touched_ref.3, bf16[16,512,1024]{2,1,0:T(8,128)(2,1)} %get-tuple-element.34.own_counts_ref, s16[16,128,3072]{2,1,0:T(8,128)(2,1)} %code.7.codes_ref, ...), custom_call_target="tpu_custom_call" | custom-call | flops 8589934592 | bytes 46137344 | tf_op jit(solution)/shard_map/update/pallas_call | solution.py:547
  118.7 1.6 %copy.19 = f32[2,8,16,128]{3,1,2,0:T(8,128)} copy(f32[2,8,16,128]{3,2,1,0:T(8,128)} %bitcast.30) | data formatting | bytes 262144
  (29 shorter events, 0.3 us)
Async XLA Ops:
  2.3 35.6 %copy-start.7 = (f32[128]{0:T(128)S(1)}, f32[128]{0:T(128)}, u32[]{:S(2)}) copy-start(f32[128]{0:T(128)} %param.12) | copy-start | bytes 1540
  2.3 31.5 %collective-permute-start.2 = (s32[8,8,1024]{2,1,0:T(8,128)S(1)}, s32[8,8,1024]{2,1,0:T(8,128)S(1)}, u32[]{:S(2)}, u32[]{:S(2)}) collective-permute-start(s32[8,8,1024]{2,1,0:T(8,128)S(1)} %shift-left_or_fusion), channel_id=1, source_target_pairs={{0,24},{8,16},{16,8},{24,0},{1,25},{9,17},{17,9},{25,1},{2,26},{10... | collective-permute-start | bytes 786440 | tf_op jit(solution)/shard_map/ppermute | solution.py:607
  7.3 26.5 %collective-permute-start.1 = (s32[8,8,1024]{2,1,0:T(8,128)S(1)}, s32[8,8,1024]{2,1,0:T(8,128)S(1)}, u32[]{:S(2)}, u32[]{:S(2)}) collective-permute-start(s32[8,8,1024]{2,1,0:T(8,128)S(1)} %shift-left_or_fusion), channel_id=1, source_target_pairs={{0,16},{8,24},{16,0},{24,8},{1,17},{9,25},{17,1},{25,9},{2,18},{10... | collective-permute-start | bytes 786440 | tf_op jit(solution)/shard_map/ppermute | solution.py:607
  7.3 26.5 %collective-permute-start = (s32[8,8,1024]{2,1,0:T(8,128)S(1)}, s32[8,8,1024]{2,1,0:T(8,128)S(1)}, u32[]{:S(2)}, u32[]{:S(2)}) collective-permute-start(s32[8,8,1024]{2,1,0:T(8,128)S(1)} %shift-left_or_fusion), channel_id=1, source_target_pairs={{0,8},{8,0},{16,24},{24,16},{1,9},{9,1},{17,25},{25,17},{2,10},{10... | collective-permute-start | bytes 786440 | tf_op jit(solution)/shard_map/ppermute | solution.py:607
  33.8 11.7 %copy-start.3 = (f32[128]{0:T(128)S(1)}, f32[128]{0:T(128)}, u32[]{:S(2)}) copy-start(f32[128]{0:T(128)} %param.14) | copy-start | bytes 1540
  33.8 19.8 %copy-start.2 = (s32[16,8,128]{2,1,0:T(8,128)S(1)}, s32[16,8,128]{2,1,0:T(8,128)}, u32[]{:S(2)}) copy-start(s32[16,8,128]{2,1,0:T(8,128)} %get-tuple-element.53.words_ref) | copy-start | bytes 196612
  33.9 11.6 %all-to-all-start = ((bf16[8,160,128]{2,1,0:T(8,128)(2,1)}), bf16[8,160,128]{2,1,0:T(8,128)(2,1)S(1)}, u32[]{:S(2)}, u32[]{:S(2)}) async-start(bf16[8,160,128]{2,1,0:T(8,128)(2,1)} %get-tuple-element.39), calls=%async_computation | async-start | bytes 655360 | tf_op jit(solution)/shard_map/all_to_all | solution.py:639
  38.0 0.8 copy-start.1
  45.5 2.2 %copy-start = (bf16[128,128,128]{2,1,0:T(8,128)(2,1)S(1)}, bf16[128,128,128]{2,1,0:T(8,128)(2,1)}, u32[]{:S(2)}) copy-start(bf16[128,128,128]{2,1,0:T(8,128)(2,1)} %w_ref.5) | copy-start | bytes 12582916
  49.2 9.8 %collective-permute-start.5 = (bf16[128,128]{1,0:T(8,128)(2,1)S(1)}, bf16[128,128]{1,0:T(8,128)(2,1)S(1)}, u32[]{:S(2)}, u32[]{:S(2)}) collective-permute-start(bf16[128,128]{1,0:T(8,128)(2,1)S(1)} %clip.1), channel_id=1, source_target_pairs={{0,24},{8,16},{16,8},{24,0},{1,25},{9,17},{17,9},{25,1},{2,26},{10... | collective-permute-start | bytes 98312 | tf_op jit(solution)/shard_map/ppermute | solution.py:607
  52.8 6.1 %collective-permute-start.4 = (bf16[128,128]{1,0:T(8,128)(2,1)S(1)}, bf16[128,128]{1,0:T(8,128)(2,1)S(1)}, u32[]{:S(2)}, u32[]{:S(2)}) collective-permute-start(bf16[128,128]{1,0:T(8,128)(2,1)S(1)} %clip.1), channel_id=1, source_target_pairs={{0,16},{8,24},{16,0},{24,8},{1,17},{9,25},{17,1},{25,9},{2,18},{10... | collective-permute-start | bytes 98312 | tf_op jit(solution)/shard_map/ppermute | solution.py:607
  52.8 6.1 %collective-permute-start.3 = (bf16[128,128]{1,0:T(8,128)(2,1)S(1)}, bf16[128,128]{1,0:T(8,128)(2,1)S(1)}, u32[]{:S(2)}, u32[]{:S(2)}) collective-permute-start(bf16[128,128]{1,0:T(8,128)(2,1)S(1)} %clip.1), channel_id=1, source_target_pairs={{0,8},{8,0},{16,24},{24,16},{1,9},{9,1},{17,25},{25,17},{2,10},{10... | collective-permute-start | bytes 98312 | tf_op jit(solution)/shard_map/ppermute | solution.py:607
  59.0 9.1 %copy-start.6 = (f32[16,2048]{1,0:T(8,128)S(1)}, f32[16,2048]{1,0:T(8,128)}, u32[]{:S(2)}) copy-start(f32[16,2048]{1,0:T(8,128)} %param.10) | copy-start | bytes 393220
  59.0 8.9 %collective-permute-start.8 = (bf16[4,128,128]{2,1,0:T(8,128)(2,1)S(1)}, bf16[4,128,128]{2,1,0:T(8,128)(2,1)S(1)}, u32[]{:S(2)}, u32[]{:S(2)}) collective-permute-start(bf16[4,128,128]{2,1,0:T(8,128)(2,1)S(1)} %pad_maximum_fusion.1), channel_id=1, source_target_pairs={{0,6},{1,7},{2,4},{3,5},{4,2},{5,3},{6,0},{7,1},{8,14},{9,15},{10,... | collective-permute-start | bytes 393224 | tf_op jit(solution)/shard_map/ppermute | solution.py:607
  60.7 7.2 %collective-permute-start.7 = (bf16[4,128,128]{2,1,0:T(8,128)(2,1)S(1)}, bf16[4,128,128]{2,1,0:T(8,128)(2,1)S(1)}, u32[]{:S(2)}, u32[]{:S(2)}) collective-permute-start(bf16[4,128,128]{2,1,0:T(8,128)(2,1)S(1)} %pad_maximum_fusion.1), channel_id=1, source_target_pairs={{0,4},{1,5},{2,6},{3,7},{4,0},{5,1},{6,2},{7,3},{8,12},{9,13},{10,... | collective-permute-start | bytes 393224 | tf_op jit(solution)/shard_map/ppermute | solution.py:607
  61.2 6.7 %collective-permute-start.6 = (bf16[4,128,128]{2,1,0:T(8,128)(2,1)S(1)}, bf16[4,128,128]{2,1,0:T(8,128)(2,1)S(1)}, u32[]{:S(2)}, u32[]{:S(2)}) collective-permute-start(bf16[4,128,128]{2,1,0:T(8,128)(2,1)S(1)} %pad_maximum_fusion.1), channel_id=1, source_target_pairs={{0,2},{1,3},{2,0},{3,1},{4,6},{5,7},{6,4},{7,5},{8,10},{9,11},{10,... | collective-permute-start | bytes 393224 | tf_op jit(solution)/shard_map/ppermute | solution.py:607
  68.0 6.1 %copy-start.4 = (bf16[4,4,128,128]{3,2,1,0:T(8,128)(2,1)}, bf16[4,4,128,128]{3,2,1,0:T(8,128)(2,1)S(1)}, u32[]{:S(2)}) copy-start(bf16[4,4,128,128]{3,2,1,0:T(8,128)(2,1)S(1)} %pad_maximum_fusion.near_ref) | copy-start | bytes 1572868
  68.0 6.1 %collective-permute-start.9 = (bf16[4,4,128,128]{3,2,1,0:T(8,128)(2,1)S(1)}, bf16[4,4,128,128]{3,2,1,0:T(8,128)(2,1)S(1)}, u32[]{:S(2)}, u32[]{:S(2)}) collective-permute-start(bf16[4,4,128,128]{3,2,1,0:T(8,128)(2,1)S(1)} %pad_maximum_fusion.near_ref), channel_id=1, source_target_pairs={{0,1},{1,0},{2,3},{3,2},{4,5},{5,4},{6,7},{7,6},{8,9},{9,8},{10,11... | collective-permute-start | bytes 1572872 | tf_op jit(solution)/shard_map/ppermute | solution.py:607
  74.1 0.8 copy-start.5

commit v6 on v5

--- a/solution.py
+++ b/solution.py
@@ -406,7 +406,7 @@
     low = count // DIGITS
     groups = near_ref.shape[1]
     rows_f, width = table_ref.shape[1:]
-    hidden = clips.shape[1]
+    hidden = clips.shape[0]
     block = min(b_group, BLOCK)
     features = range(PAIR)
 
@@ -417,7 +417,7 @@
             for chip in range(chips):
                 for group in range(groups):
                     start = group * b_group + (place_ref[OWN] ^ (2 * chip + core)) * rows
-                    clips[pl.ds(pl.multiple_of(start, rows), rows)] = source[chip, group]
+                    clips[:, pl.ds(pl.multiple_of(start, rows), rows)] = source[chip, group].T
 
     def put(side, start, stop):
         feature = jnp.maximum(step - 1, 0) * PAIR + side
@@ -439,10 +439,11 @@
             else:
                 start = pl.multiple_of((group - 1) * b_group + number * block, block)
                 counts = spread(codes_ref[side, :, pl.ds(start, block)])
-            found.append(sums[side] + dot(counts, clips[at]))
+            found.append(sums[side] + dot(clips[:, at], counts, NT))
         return tuple(found)
 
     def finish(side, sums):
+        sums = sums.T
         parts = [
             sums[digit * low : (digit + 1) * low] * (1 / scale(digit)) for digit in range(DIGITS)
         ]
@@ -462,7 +463,7 @@
         lines = [accum_ref[side, number : number + 1] for number in range(rows_f // LANES)]
         old = pick_lanes(lines, touched >> 7, touched & (LANES - 1))
         ones = jnp.where(eye, 1.0, 0.0).astype(jnp.bfloat16)
-        parts = split(old, 3)
+        parts = split(old, 2)
         diagonal = jnp.concatenate(
             [
                 jnp.concatenate(
@@ -472,7 +473,7 @@
             ],
             axis=0,
         )
-        total = mean + dot(diagonal, jnp.full((3 * LANES, LANES), 1, jnp.bfloat16))
+        total = mean + dot(diagonal, jnp.full((2 * LANES, LANES), 1, jnp.bfloat16))
         update[side] = listed * (LEARN * lax.rsqrt(total))
 
         extra = [
@@ -489,7 +490,7 @@
     @pl.when(step < last)
     def _():
         table_out[...] = table_ref[...]
-        sums = tuple(jnp.zeros((count, hidden), jnp.float32) for side in features)
+        sums = tuple(jnp.zeros((hidden, count), jnp.float32) for side in features)
         share = count // groups
         for group in range(groups):
             for side in features:
@@ -568,7 +569,7 @@
             out_specs=[before(rows_f, width), now(tall, LANES), now(part, hidden)],
             scratch_shapes=[
                 pltpu.VMEM((PAIR, count, width), jnp.float32),
-                pltpu.VMEM((b_group + others, hidden), jnp.bfloat16),
+                pltpu.VMEM((hidden, b_group + others), jnp.bfloat16),
             ],
         ),
         out_shape=[

time: 121 us -> 126 us (1.041)
  Pallas kernels: 92.4 us -> 97.4 us
    pallas_call x1, Pallas kernels: 43.7 us -> 48.8 us  [update_rows(): pl.pallas_call(update_kernel, grid_spec=pltpu.PrefetchScalarGridSpec(num_...]
  transfers between devices with their start and end apart: 11 -> 11, of which waited for: 1 -> 1; matrix products, arithmetic and copies ran while one was open for 1% -> 1% of each run, Pallas kernels for 39% -> 38%
where the time goes in v6:
time: 126 us; the launch traced here: 125 us
  Pallas kernels  97.4 us (77%)
  starting transfers between devices  17.7 us (14%)
  local copies, waits for them, and re-layouts  6.29 us (5%)
  other arithmetic  1.79 us (1%)
  waiting for transfers between devices  1.38 us (1%)
    pallas_call x1, Pallas kernels, update_rows(): pl.pallas_call(update_kernel, grid_spec=pltpu.PrefetchScalarGridSpec(num_...  48.8 us
    pallas_call x1, Pallas kernels, pool(): pl.pallas_call(pool_kernel, grid_spec=pltpu.PrefetchScalarGridSpec(num_sc...  25.9 us
    pallas_call x4, Pallas kernels, code_counts(): pl.pallas_call(code_kernel, grid=(stop - start, others), in_specs=[pl.Blo...  21.3 us
    ppermute x10, starting transfers between devices, swap(): return lax.ppermute(array, axis, [(i, i ^ apart) for i in range(size)])  13.7 us
    unnamed x18, local copies, waits for them, and re-layouts  6.18 us
    all_to_all x1, starting transfers between devices, body(): lax.all_to_all(sent, 'table', split_axis=0, concat_axis=0, tiled=True)  3.96 us
  transfers between devices with their start and end apart: 11, of which 1 were waited for; matrix products, arithmetic and copies ran while one was open for 1% of the time, Pallas kernels for 38%

profile of v6, /device:TPU:0, one launch (start us, length us, event | category | flops | bytes accessed | tf_op | source)
XLA Modules:
  0.0 125.3 jit_solution(1762972288023604531)
XLA Ops:
  0.6 1.1 shift-left_or_fusion
  1.7 0.6 pad_add_fusion.1.place_ref
  2.3 5.0 %collective-permute-start.2 = (s32[8,8,1024]{2,1,0:T(8,128)S(1)}, s32[8,8,1024]{2,1,0:T(8,128)S(1)}, u32[]{:S(2)}, u32[]{:S(2)}) collective-permute-start(s32[8,8,1024]{2,1,0:T(8,128)S(1)} %shift-left_or_fusion), channel_id=1, source_target_pairs={{0,24},{8,16},{16,8},{24,0},{1,25},{9,17},{17,9},{25,1},{2,26},{10... | collective-permute-start | bytes 786440 | tf_op jit(solution)/shard_map/ppermute | solution.py:608
  7.3 0.6 collective-permute-start
  7.9 25.9 %pool.1 = (bf16[8,160,128]{2,1,0:T(8,128)(2,1)}, bf16[16,128,512]{2,1,0:T(8,128)(2,1)}, s32[16,8,128]{2,1,0:T(8,128)}, bf16[16,512,1024]{2,1,0:T(8,128)(2,1)}) custom-call(s32[2]{0:T(128)} %pad_add_fusion.1.place_ref, f32[16,2048,128]{2,1,0:T(8,128)} %table_ref.3, s32[16,512]{1,0:T(8,128)} %touched_ref.3, s32[16,8,1024]{2,1,0:T(8,128)} %ids_ref, ...), custom_call_target="tpu_custom_call" | custom-call | flops 17179869184 | bytes 16777216 | tf_op jit(solution)/shard_map/pool/pallas_call | solution.py:234
  33.9 4.0 %all-to-all-start = ((bf16[8,160,128]{2,1,0:T(8,128)(2,1)}), bf16[8,160,128]{2,1,0:T(8,128)(2,1)S(1)}, u32[]{:S(2)}, u32[]{:S(2)}) async-start(bf16[8,160,128]{2,1,0:T(8,128)(2,1)} %get-tuple-element.39), calls=%async_computation | async-start | bytes 655360 | tf_op jit(solution)/shard_map/all_to_all | solution.py:640
  37.9 0.1 copy.15.w_out_ref
  38.0 0.8 copy-done.1
  38.8 5.3 %code.4.rest_0_ = s16[16,128,3072]{2,1,0:T(8,128)(2,1)} custom-call(s32[16,8,128]{2,1,0:T(8,128)S(1)} %copy-done.1, s32[3,8,8,1024]{3,2,1,0:T(8,128)S(1)} %pad_add_fusion.ids_ref), custom_call_target="tpu_custom_call" | custom-call | flops 629145600 | bytes 3145728 | tf_op jit(solution)/shard_map/code/pallas_call | solution.py:303
  44.2 1.4 %all-to-all-done.sent_ref = bf16[8,160,128]{2,1,0:T(8,128)(2,1)S(1)} async-done(((bf16[8,160,128]{2,1,0:T(8,128)(2,1)}), bf16[8,160,128]{2,1,0:T(8,128)(2,1)S(1)}, u32[]{:S(2)}, u32[]{:S(2)}) %all-to-all-start) | async-done | bytes 327712 | tf_op jit(solution)/shard_map/all_to_all | solution.py:640
  45.5 2.2 %copy-done = bf16[128,128,128]{2,1,0:T(8,128)(2,1)S(1)} copy-done((bf16[128,128,128]{2,1,0:T(8,128)(2,1)S(1)}, bf16[128,128,128]{2,1,0:T(8,128)(2,1)}, u32[]{:S(2)}) %copy-start) | copy-done | bytes 4194328
  47.7 1.5 %clip.1 = bf16[128,128]{1,0:T(8,128)(2,1)S(1)} custom-call(f32[128,1]{1,0:T(8,128)S(1)} %copy.15.w_out_ref, f32[1,128]{1,0:T(1,128)S(1)} %bitcast.22, bf16[128,128,128]{2,1,0:T(8,128)(2,1)S(1)} %copy-done, bf16[8,160,128]{2,1,0:T(8,128)(2,1)S(1)} %all-to-all-done.sent_ref), custom_call_target="tpu_custom_call" | custom-call | flops 536870912 | bytes 4194304 | tf_op jit(solution)/shard_map/clip/pallas_call | solution.py:359
  49.2 3.7 %collective-permute-start.5 = (bf16[128,128]{1,0:T(8,128)(2,1)S(1)}, bf16[128,128]{1,0:T(8,128)(2,1)S(1)}, u32[]{:S(2)}, u32[]{:S(2)}) collective-permute-start(bf16[128,128]{1,0:T(8,128)(2,1)S(1)} %clip.1), channel_id=1, source_target_pairs={{0,24},{8,16},{16,8},{24,0},{1,25},{9,17},{17,9},{25,1},{2,26},{10... | collective-permute-start | bytes 98312 | tf_op jit(solution)/shard_map/ppermute | solution.py:608
  52.8 0.8 collective-permute-start.3
  53.6 5.3 %code.5.rest_0_ = s16[16,128,3072]{2,1,0:T(8,128)(2,1)} custom-call(s32[16,8,128]{2,1,0:T(8,128)S(1)} %copy-done.2, s32[3,8,8,1024]{3,2,1,0:T(8,128)S(1)} %pad_add_fusion.ids_ref, s16[16,128,3072]{2,1,0:T(8,128)(2,1)} %code.4.rest_0_), custom_call_target="tpu_custom_call", output_to_operand_aliasing={{}: (2, {})} | custom-call | flops 629145600 | bytes 3145728 | tf_op jit(solution)/shard_map/code/pallas_call | solution.py:303
  59.0 1.6 %collective-permute-start.8 = (bf16[4,128,128]{2,1,0:T(8,128)(2,1)S(1)}, bf16[4,128,128]{2,1,0:T(8,128)(2,1)S(1)}, u32[]{:S(2)}, u32[]{:S(2)}) collective-permute-start(bf16[4,128,128]{2,1,0:T(8,128)(2,1)S(1)} %pad_maximum_fusion.1), channel_id=1, source_target_pairs={{0,6},{1,7},{2,4},{3,5},{4,2},{5,3},{6,0},{7,1},{8,14},{9,15},{10,... | collective-permute-start | bytes 393224 | tf_op jit(solution)/shard_map/ppermute | solution.py:608
  60.7 0.6 collective-permute-start.7
  61.2 1.4 %collective-permute-start.6 = (bf16[4,128,128]{2,1,0:T(8,128)(2,1)S(1)}, bf16[4,128,128]{2,1,0:T(8,128)(2,1)S(1)}, u32[]{:S(2)}, u32[]{:S(2)}) collective-permute-start(bf16[4,128,128]{2,1,0:T(8,128)(2,1)S(1)} %pad_maximum_fusion.1), channel_id=1, source_target_pairs={{0,2},{1,3},{2,0},{3,1},{4,6},{5,7},{6,4},{7,5},{8,10},{9,11},{10,... | collective-permute-start | bytes 393224 | tf_op jit(solution)/shard_map/ppermute | solution.py:608
  62.6 5.3 %code.6.rest_0_ = s16[16,128,3072]{2,1,0:T(8,128)(2,1)} custom-call(s32[16,8,128]{2,1,0:T(8,128)S(1)} %copy-done.2, s32[3,8,8,1024]{3,2,1,0:T(8,128)S(1)} %pad_add_fusion.ids_ref, s16[16,128,3072]{2,1,0:T(8,128)(2,1)} %code.5.rest_0_), custom_call_target="tpu_custom_call", output_to_operand_aliasing={{}: (2, {})} | custom-call | flops 629145600 | bytes 3145728 | tf_op jit(solution)/shard_map/code/pallas_call | solution.py:303
  68.1 0.7 copy.16
  68.8 5.3 %code.7.codes_ref = s16[16,128,3072]{2,1,0:T(8,128)(2,1)} custom-call(s32[16,8,128]{2,1,0:T(8,128)S(1)} %copy-done.2, s32[3,8,8,1024]{3,2,1,0:T(8,128)S(1)} %pad_add_fusion.ids_ref, s16[16,128,3072]{2,1,0:T(8,128)(2,1)} %code.6.rest_0_), custom_call_target="tpu_custom_call", output_to_operand_aliasing={{}: (2, {})} | custom-call | flops 629145600 | bytes 3145728 | tf_op jit(solution)/shard_map/code/pallas_call | solution.py:303
  74.1 0.8 copy-done.5
  74.9 48.8 %update.1 = (f32[16,2048,128]{2,1,0:T(8,128)}, f32[16,16,128]{2,1,0:T(8,128)}, f32[16,32,128]{2,1,0:T(8,128)}) custom-call(s32[2]{0:T(128)} %pad_add_fusion.1.place_ref, s32[16,512]{1,0:T(8,128)} %touched_ref.3, bf16[16,512,1024]{2,1,0:T(8,128)(2,1)} %get-tuple-element.34.own_counts_ref, s16[16,128,3072]{2,1,0:T(8,128)(2,1)} %code.7.codes_ref, ...), custom_call_target="tpu_custom_call" | custom-call | flops 8589934592 | bytes 46137344 | tf_op jit(solution)/shard_map/update/pallas_call | solution.py:548
  123.7 1.6 %copy.19 = f32[2,8,16,128]{3,1,2,0:T(8,128)} copy(f32[2,8,16,128]{3,2,1,0:T(8,128)} %bitcast.30) | data formatting | bytes 262144
  (29 shorter events, 0.3 us)
Async XLA Ops:
  2.3 35.6 %copy-start.7 = (f32[128]{0:T(128)S(1)}, f32[128]{0:T(128)}, u32[]{:S(2)}) copy-start(f32[128]{0:T(128)} %param.12) | copy-start | bytes 1540
  2.3 31.5 %collective-permute-start.2 = (s32[8,8,1024]{2,1,0:T(8,128)S(1)}, s32[8,8,1024]{2,1,0:T(8,128)S(1)}, u32[]{:S(2)}, u32[]{:S(2)}) collective-permute-start(s32[8,8,1024]{2,1,0:T(8,128)S(1)} %shift-left_or_fusion), channel_id=1, source_target_pairs={{0,24},{8,16},{16,8},{24,0},{1,25},{9,17},{17,9},{25,1},{2,26},{10... | collective-permute-start | bytes 786440 | tf_op jit(solution)/shard_map/ppermute | solution.py:608
  7.3 26.5 %collective-permute-start.1 = (s32[8,8,1024]{2,1,0:T(8,128)S(1)}, s32[8,8,1024]{2,1,0:T(8,128)S(1)}, u32[]{:S(2)}, u32[]{:S(2)}) collective-permute-start(s32[8,8,1024]{2,1,0:T(8,128)S(1)} %shift-left_or_fusion), channel_id=1, source_target_pairs={{0,16},{8,24},{16,0},{24,8},{1,17},{9,25},{17,1},{25,9},{2,18},{10... | collective-permute-start | bytes 786440 | tf_op jit(solution)/shard_map/ppermute | solution.py:608
  7.3 26.5 %collective-permute-start = (s32[8,8,1024]{2,1,0:T(8,128)S(1)}, s32[8,8,1024]{2,1,0:T(8,128)S(1)}, u32[]{:S(2)}, u32[]{:S(2)}) collective-permute-start(s32[8,8,1024]{2,1,0:T(8,128)S(1)} %shift-left_or_fusion), channel_id=1, source_target_pairs={{0,8},{8,0},{16,24},{24,16},{1,9},{9,1},{17,25},{25,17},{2,10},{10... | collective-permute-start | bytes 786440 | tf_op jit(solution)/shard_map/ppermute | solution.py:608
  33.8 11.7 %copy-start.3 = (f32[128]{0:T(128)S(1)}, f32[128]{0:T(128)}, u32[]{:S(2)}) copy-start(f32[128]{0:T(128)} %param.14) | copy-start | bytes 1540
  33.8 19.8 %copy-start.2 = (s32[16,8,128]{2,1,0:T(8,128)S(1)}, s32[16,8,128]{2,1,0:T(8,128)}, u32[]{:S(2)}) copy-start(s32[16,8,128]{2,1,0:T(8,128)} %get-tuple-element.53.words_ref) | copy-start | bytes 196612
  33.9 11.6 %all-to-all-start = ((bf16[8,160,128]{2,1,0:T(8,128)(2,1)}), bf16[8,160,128]{2,1,0:T(8,128)(2,1)S(1)}, u32[]{:S(2)}, u32[]{:S(2)}) async-start(bf16[8,160,128]{2,1,0:T(8,128)(2,1)} %get-tuple-element.39), calls=%async_computation | async-start | bytes 655360 | tf_op jit(solution)/shard_map/all_to_all | solution.py:640
  38.0 0.8 copy-start.1
  45.5 2.2 %copy-start = (bf16[128,128,128]{2,1,0:T(8,128)(2,1)S(1)}, bf16[128,128,128]{2,1,0:T(8,128)(2,1)}, u32[]{:S(2)}) copy-start(bf16[128,128,128]{2,1,0:T(8,128)(2,1)} %w_ref.5) | copy-start | bytes 12582916
  49.2 9.8 %collective-permute-start.5 = (bf16[128,128]{1,0:T(8,128)(2,1)S(1)}, bf16[128,128]{1,0:T(8,128)(2,1)S(1)}, u32[]{:S(2)}, u32[]{:S(2)}) collective-permute-start(bf16[128,128]{1,0:T(8,128)(2,1)S(1)} %clip.1), channel_id=1, source_target_pairs={{0,24},{8,16},{16,8},{24,0},{1,25},{9,17},{17,9},{25,1},{2,26},{10... | collective-permute-start | bytes 98312 | tf_op jit(solution)/shard_map/ppermute | solution.py:608
  52.8 6.1 %collective-permute-start.4 = (bf16[128,128]{1,0:T(8,128)(2,1)S(1)}, bf16[128,128]{1,0:T(8,128)(2,1)S(1)}, u32[]{:S(2)}, u32[]{:S(2)}) collective-permute-start(bf16[128,128]{1,0:T(8,128)(2,1)S(1)} %clip.1), channel_id=1, source_target_pairs={{0,16},{8,24},{16,0},{24,8},{1,17},{9,25},{17,1},{25,9},{2,18},{10... | collective-permute-start | bytes 98312 | tf_op jit(solution)/shard_map/ppermute | solution.py:608
  52.8 6.1 %collective-permute-start.3 = (bf16[128,128]{1,0:T(8,128)(2,1)S(1)}, bf16[128,128]{1,0:T(8,128)(2,1)S(1)}, u32[]{:S(2)}, u32[]{:S(2)}) collective-permute-start(bf16[128,128]{1,0:T(8,128)(2,1)S(1)} %clip.1), channel_id=1, source_target_pairs={{0,8},{8,0},{16,24},{24,16},{1,9},{9,1},{17,25},{25,17},{2,10},{10... | collective-permute-start | bytes 98312 | tf_op jit(solution)/shard_map/ppermute | solution.py:608
  59.0 9.1 %copy-start.6 = (f32[16,2048]{1,0:T(8,128)S(1)}, f32[16,2048]{1,0:T(8,128)}, u32[]{:S(2)}) copy-start(f32[16,2048]{1,0:T(8,128)} %param.10) | copy-start | bytes 393220
  59.0 8.9 %collective-permute-start.8 = (bf16[4,128,128]{2,1,0:T(8,128)(2,1)S(1)}, bf16[4,128,128]{2,1,0:T(8,128)(2,1)S(1)}, u32[]{:S(2)}, u32[]{:S(2)}) collective-permute-start(bf16[4,128,128]{2,1,0:T(8,128)(2,1)S(1)} %pad_maximum_fusion.1), channel_id=1, source_target_pairs={{0,6},{1,7},{2,4},{3,5},{4,2},{5,3},{6,0},{7,1},{8,14},{9,15},{10,... | collective-permute-start | bytes 393224 | tf_op jit(solution)/shard_map/ppermute | solution.py:608
  60.7 7.2 %collective-permute-start.7 = (bf16[4,128,128]{2,1,0:T(8,128)(2,1)S(1)}, bf16[4,128,128]{2,1,0:T(8,128)(2,1)S(1)}, u32[]{:S(2)}, u32[]{:S(2)}) collective-permute-start(bf16[4,128,128]{2,1,0:T(8,128)(2,1)S(1)} %pad_maximum_fusion.1), channel_id=1, source_target_pairs={{0,4},{1,5},{2,6},{3,7},{4,0},{5,1},{6,2},{7,3},{8,12},{9,13},{10,... | collective-permute-start | bytes 393224 | tf_op jit(solution)/shard_map/ppermute | solution.py:608
  61.2 6.7 %collective-permute-start.6 = (bf16[4,128,128]{2,1,0:T(8,128)(2,1)S(1)}, bf16[4,128,128]{2,1,0:T(8,128)(2,1)S(1)}, u32[]{:S(2)}, u32[]{:S(2)}) collective-permute-start(bf16[4,128,128]{2,1,0:T(8,128)(2,1)S(1)} %pad_maximum_fusion.1), channel_id=1, source_target_pairs={{0,2},{1,3},{2,0},{3,1},{4,6},{5,7},{6,4},{7,5},{8,10},{9,11},{10,... | collective-permute-start | bytes 393224 | tf_op jit(solution)/shard_map/ppermute | solution.py:608
  68.0 6.1 %copy-start.4 = (bf16[4,4,128,128]{3,2,1,0:T(8,128)(2,1)}, bf16[4,4,128,128]{3,2,1,0:T(8,128)(2,1)S(1)}, u32[]{:S(2)}) copy-start(bf16[4,4,128,128]{3,2,1,0:T(8,128)(2,1)S(1)} %pad_maximum_fusion.near_ref) | copy-start | bytes 1572868
  68.0 6.1 %collective-permute-start.9 = (bf16[4,4,128,128]{3,2,1,0:T(8,128)(2,1)S(1)}, bf16[4,4,128,128]{3,2,1,0:T(8,128)(2,1)S(1)}, u32[]{:S(2)}, u32[]{:S(2)}) collective-permute-start(bf16[4,4,128,128]{3,2,1,0:T(8,128)(2,1)S(1)} %pad_maximum_fusion.near_ref), channel_id=1, source_target_pairs={{0,1},{1,0},{2,3},{3,2},{4,5},{5,4},{6,7},{7,6},{8,9},{9,8},{10,11... | collective-permute-start | bytes 1572872 | tf_op jit(solution)/shard_map/ppermute | solution.py:608
  74.1 0.8 copy-start.5

commit v7 on v5

--- a/solution.py
+++ b/solution.py
@@ -459,10 +459,16 @@
         sections = [slice(start, start + LANES) for start in range(0, count, LANES)]
         touched = touched_ref[pl.ds(step * PAIR + side, 1)]
         touched = jnp.concatenate([touched[:, lanes] for lanes in sections * 2], axis=0)
-        lines = [accum_ref[side, number : number + 1] for number in range(rows_f // LANES)]
+        feature = step * PAIR + side
+        mine = iota((accum_ref.shape[0], LANES), 0) == feature
+        stretches = [slice(start, start + LANES) for start in range(0, rows_f, LANES)]
+        lines = [
+            jnp.sum(jnp.where(mine, accum_ref[:, lanes], 0.0), axis=0, keepdims=True)
+            for lanes in stretches
+        ]
         old = pick_lanes(lines, touched >> 7, touched & (LANES - 1))
         ones = jnp.where(eye, 1.0, 0.0).astype(jnp.bfloat16)
-        parts = split(old, 3)
+        parts = split(old, 2)
         diagonal = jnp.concatenate(
             [
                 jnp.concatenate(
@@ -472,7 +478,7 @@
             ],
             axis=0,
         )
-        total = mean + dot(diagonal, jnp.full((3 * LANES, LANES), 1, jnp.bfloat16))
+        total = mean + dot(diagonal, jnp.full((2 * LANES, LANES), 1, jnp.bfloat16))
         update[side] = listed * (LEARN * lax.rsqrt(total))
 
         extra = [
@@ -481,10 +487,12 @@
         words = words_ref[side]
         for half, word in enumerate((words & 0xFFFF, lax.shift_right_logical(words, HALF))):
             gain = pick_lanes(extra, (word >> 10) & (DIGITS - 1), word & (LANES - 1))
-            rows = slice(half * words.shape[0], (half + 1) * words.shape[0])
-            accum_out[side, rows] = accum_ref[side, rows] + jnp.where(
-                (word >> 8) >= LISTED, gain, 0.0
-            )
+            gain = jnp.where((word >> 8) >= LISTED, gain, 0.0)
+            for number in range(words.shape[0]):
+                place = half * words.shape[0] + number
+                line = jnp.broadcast_to(lines[place] + gain[number : number + 1], mine.shape)
+                lanes = stretches[place]
+                accum_out[:, lanes] = jnp.where(mine, line, accum_out[:, lanes])
 
     @pl.when(step < last)
     def _():
@@ -529,7 +537,6 @@
     others = codes.shape[2]
     hidden = near.shape[-1]
     part = dense_noise.shape[1]
-    tall = rows_f // LANES
     steps = f_dev // PAIR
 
     def current(i):
@@ -544,7 +551,7 @@
     def whole(array):
         return pl.BlockSpec(array.shape, lambda i, p, s: (0,) * array.ndim)
 
-    new_table, new_accum, dense = pl.pallas_call(
+    return pl.pallas_call(
         update_kernel,
         grid_spec=pltpu.PrefetchScalarGridSpec(
             num_scalar_prefetch=2,
@@ -557,7 +564,7 @@
                 before(rows_f, width),
                 whole(touched),
                 now(*words.shape[1:]),
-                now(tall, LANES),
+                whole(accum),
                 now(count, width),
                 pl.BlockSpec(
                     (PAIR, width, hidden), lambda i, p, s: (p[OWN] * steps + current(i), 0, 0)
@@ -565,7 +572,7 @@
                 pl.BlockSpec((PAIR, part, count), lambda i, p, s: (current(i), p[GROUP], 0)),
                 now(part, hidden),
             ],
-            out_specs=[before(rows_f, width), now(tall, LANES), now(part, hidden)],
+            out_specs=[before(rows_f, width), whole(accum), now(part, hidden)],
             scratch_shapes=[
                 pltpu.VMEM((PAIR, count, width), jnp.float32),
                 pltpu.VMEM((b_group + others, hidden), jnp.bfloat16),
@@ -573,7 +580,7 @@
         ),
         out_shape=[
             jax.ShapeDtypeStruct((f_dev, rows_f, width), jnp.float32),
-            jax.ShapeDtypeStruct((f_dev, tall, LANES), jnp.float32),
+            jax.ShapeDtypeStruct(accum.shape, jnp.float32),
             jax.ShapeDtypeStruct((f_dev, part, hidden), jnp.float32),
         ],
         compiler_params=pltpu.CompilerParams(vmem_limit_bytes=56 * MIB),
@@ -593,13 +600,12 @@
         table,
         touched,
         words,
-        accum.reshape(f_dev, tall, LANES),
+        accum,
         noise,
         w_hidden,
         rows_t,
         dense_noise,
     )
-    return new_table, new_accum.reshape(f_dev, rows_f), dense
 
 
 def swap(array, axis, apart):

time: 121 us -> 119 us (0.983)
  local copies, waits for them, and re-layouts: 6.29 us -> 3.97 us
    unnamed x18 -> x14, local copies, waits for them, and re-layouts: 6.18 us -> 3.85 us
  transfers between devices with their start and end apart: 11 -> 11, of which waited for: 1 -> 1; matrix products, arithmetic and copies ran while one was open for 1% -> 0% of each run, Pallas kernels for 39% -> 40%
where the time goes in v7:
time: 119 us
  Pallas kernels  92.9 us (78%)
  starting transfers between devices  17.7 us (15%)
  local copies, waits for them, and re-layouts  3.97 us (3%)
  other arithmetic  1.78 us (1%)
  waiting for transfers between devices  1.39 us (1%)
    pallas_call x1, Pallas kernels, update_rows(): pl.pallas_call(update_kernel, grid_spec=pltpu.PrefetchScalarGridSpec(num_...  44.2 us
    pallas_call x1, Pallas kernels, pool(): pl.pallas_call(pool_kernel, grid_spec=pltpu.PrefetchScalarGridSpec(num_sc...  25.9 us
    pallas_call x4, Pallas kernels, code_counts(): pl.pallas_call(code_kernel, grid=(stop - start, others), in_specs=[pl.Blo...  21.3 us
    ppermute x10, starting transfers between devices, swap(): return lax.ppermute(array, axis, [(i, i ^ apart) for i in range(size)])  13.7 us
    all_to_all x1, starting transfers between devices, body(): lax.all_to_all(sent, 'table', split_axis=0, concat_axis=0, tiled=True)  3.96 us
    unnamed x14, local copies, waits for them, and re-layouts  3.85 us
  transfers between devices with their start and end apart: 11, of which 1 were waited for; matrix products, arithmetic and copies ran while one was open for 0% of the time, Pallas kernels for 40%

profile of v7, /device:TPU:0, one launch (start us, length us, event | category | flops | bytes accessed | tf_op | source)
XLA Modules:
  0.0 118.6 jit_solution(7558076705829080248)
XLA Ops:
  0.6 1.1 shift-left_or_fusion
  1.7 0.6 pad_add_fusion.1.place_ref
  2.3 5.0 %collective-permute-start.2 = (s32[8,8,1024]{2,1,0:T(8,128)S(1)}, s32[8,8,1024]{2,1,0:T(8,128)S(1)}, u32[]{:S(2)}, u32[]{:S(2)}) collective-permute-start(s32[8,8,1024]{2,1,0:T(8,128)S(1)} %shift-left_or_fusion), channel_id=1, source_target_pairs={{0,24},{8,16},{16,8},{24,0},{1,25},{9,17},{17,9},{25,1},{2,26},{10... | collective-permute-start | bytes 786440 | tf_op jit(solution)/shard_map/ppermute | solution.py:613
  7.3 0.6 collective-permute-start
  7.9 25.9 %pool.1 = (bf16[8,160,128]{2,1,0:T(8,128)(2,1)}, bf16[16,128,512]{2,1,0:T(8,128)(2,1)}, s32[16,8,128]{2,1,0:T(8,128)}, bf16[16,512,1024]{2,1,0:T(8,128)(2,1)}) custom-call(s32[2]{0:T(128)} %pad_add_fusion.1.place_ref, f32[16,2048,128]{2,1,0:T(8,128)} %table_ref.3, s32[16,512]{1,0:T(8,128)} %touched_ref.3, s32[16,8,1024]{2,1,0:T(8,128)} %ids_ref, ...), custom_call_target="tpu_custom_call" | custom-call | flops 17179869184 | bytes 16777216 | tf_op jit(solution)/shard_map/pool/pallas_call | solution.py:234
  33.9 4.0 %all-to-all-start = ((bf16[8,160,128]{2,1,0:T(8,128)(2,1)}), bf16[8,160,128]{2,1,0:T(8,128)(2,1)S(1)}, u32[]{:S(2)}, u32[]{:S(2)}) async-start(bf16[8,160,128]{2,1,0:T(8,128)(2,1)} %get-tuple-element.36), calls=%async_computation | async-start | bytes 655360 | tf_op jit(solution)/shard_map/all_to_all | solution.py:645
  37.8 0.1 copy.15.w_out_ref
  38.0 0.8 copy-done.1
  38.8 5.3 %code.4.rest_0_ = s16[16,128,3072]{2,1,0:T(8,128)(2,1)} custom-call(s32[16,8,128]{2,1,0:T(8,128)S(1)} %copy-done.1, s32[3,8,8,1024]{3,2,1,0:T(8,128)S(1)} %pad_add_fusion.ids_ref), custom_call_target="tpu_custom_call" | custom-call | flops 629145600 | bytes 3145728 | tf_op jit(solution)/shard_map/code/pallas_call | solution.py:303
  44.1 1.4 %all-to-all-done.sent_ref = bf16[8,160,128]{2,1,0:T(8,128)(2,1)S(1)} async-done(((bf16[8,160,128]{2,1,0:T(8,128)(2,1)}), bf16[8,160,128]{2,1,0:T(8,128)(2,1)S(1)}, u32[]{:S(2)}, u32[]{:S(2)}) %all-to-all-start) | async-done | bytes 327712 | tf_op jit(solution)/shard_map/all_to_all | solution.py:645
  45.5 2.2 %copy-done = bf16[128,128,128]{2,1,0:T(8,128)(2,1)S(1)} copy-done((bf16[128,128,128]{2,1,0:T(8,128)(2,1)S(1)}, bf16[128,128,128]{2,1,0:T(8,128)(2,1)}, u32[]{:S(2)}) %copy-start) | copy-done | bytes 4194328
  47.7 1.5 %clip.1 = bf16[128,128]{1,0:T(8,128)(2,1)S(1)} custom-call(f32[128,1]{1,0:T(8,128)S(1)} %copy.15.w_out_ref, f32[1,128]{1,0:T(1,128)S(1)} %bitcast.16, bf16[128,128,128]{2,1,0:T(8,128)(2,1)S(1)} %copy-done, bf16[8,160,128]{2,1,0:T(8,128)(2,1)S(1)} %all-to-all-done.sent_ref), custom_call_target="tpu_custom_call" | custom-call | flops 536870912 | bytes 4194304 | tf_op jit(solution)/shard_map/clip/pallas_call | solution.py:359
  49.2 3.7 %collective-permute-start.5 = (bf16[128,128]{1,0:T(8,128)(2,1)S(1)}, bf16[128,128]{1,0:T(8,128)(2,1)S(1)}, u32[]{:S(2)}, u32[]{:S(2)}) collective-permute-start(bf16[128,128]{1,0:T(8,128)(2,1)S(1)} %clip.1), channel_id=1, source_target_pairs={{0,24},{8,16},{16,8},{24,0},{1,25},{9,17},{17,9},{25,1},{2,26},{10... | collective-permute-start | bytes 98312 | tf_op jit(solution)/shard_map/ppermute | solution.py:613
  52.8 0.8 collective-permute-start.3
  53.6 5.4 %code.5.rest_0_ = s16[16,128,3072]{2,1,0:T(8,128)(2,1)} custom-call(s32[16,8,128]{2,1,0:T(8,128)S(1)} %copy-done.2, s32[3,8,8,1024]{3,2,1,0:T(8,128)S(1)} %pad_add_fusion.ids_ref, s16[16,128,3072]{2,1,0:T(8,128)(2,1)} %code.4.rest_0_), custom_call_target="tpu_custom_call", output_to_operand_aliasing={{}: (2, {})} | custom-call | flops 629145600 | bytes 3145728 | tf_op jit(solution)/shard_map/code/pallas_call | solution.py:303
  59.0 1.6 %collective-permute-start.8 = (bf16[4,128,128]{2,1,0:T(8,128)(2,1)S(1)}, bf16[4,128,128]{2,1,0:T(8,128)(2,1)S(1)}, u32[]{:S(2)}, u32[]{:S(2)}) collective-permute-start(bf16[4,128,128]{2,1,0:T(8,128)(2,1)S(1)} %pad_maximum_fusion.1), channel_id=1, source_target_pairs={{0,6},{1,7},{2,4},{3,5},{4,2},{5,3},{6,0},{7,1},{8,14},{9,15},{10,... | collective-permute-start | bytes 393224 | tf_op jit(solution)/shard_map/ppermute | solution.py:613
  60.6 0.6 collective-permute-start.7
  61.2 1.4 %collective-permute-start.6 = (bf16[4,128,128]{2,1,0:T(8,128)(2,1)S(1)}, bf16[4,128,128]{2,1,0:T(8,128)(2,1)S(1)}, u32[]{:S(2)}, u32[]{:S(2)}) collective-permute-start(bf16[4,128,128]{2,1,0:T(8,128)(2,1)S(1)} %pad_maximum_fusion.1), channel_id=1, source_target_pairs={{0,2},{1,3},{2,0},{3,1},{4,6},{5,7},{6,4},{7,5},{8,10},{9,11},{10,... | collective-permute-start | bytes 393224 | tf_op jit(solution)/shard_map/ppermute | solution.py:613
  62.6 5.3 %code.6.rest_0_ = s16[16,128,3072]{2,1,0:T(8,128)(2,1)} custom-call(s32[16,8,128]{2,1,0:T(8,128)S(1)} %copy-done.2, s32[3,8,8,1024]{3,2,1,0:T(8,128)S(1)} %pad_add_fusion.ids_ref, s16[16,128,3072]{2,1,0:T(8,128)(2,1)} %code.5.rest_0_), custom_call_target="tpu_custom_call", output_to_operand_aliasing={{}: (2, {})} | custom-call | flops 629145600 | bytes 3145728 | tf_op jit(solution)/shard_map/code/pallas_call | solution.py:303
  67.9 0.1 pad_maximum_fusion.near_ref
  68.0 0.1 collective-permute-start.9
  68.1 5.3 %code.7.codes_ref = s16[16,128,3072]{2,1,0:T(8,128)(2,1)} custom-call(s32[16,8,128]{2,1,0:T(8,128)S(1)} %copy-done.2, s32[3,8,8,1024]{3,2,1,0:T(8,128)S(1)} %pad_add_fusion.ids_ref, s16[16,128,3072]{2,1,0:T(8,128)(2,1)} %code.6.rest_0_), custom_call_target="tpu_custom_call", output_to_operand_aliasing={{}: (2, {})} | custom-call | flops 629145600 | bytes 3145728 | tf_op jit(solution)/shard_map/code/pallas_call | solution.py:303
  73.4 0.8 copy-done.5
  74.2 44.2 %update.1 = (f32[16,2048,128]{2,1,0:T(8,128)}, f32[16,2048]{1,0:T(8,128)}, f32[16,32,128]{2,1,0:T(8,128)}) custom-call(s32[2]{0:T(128)} %pad_add_fusion.1.place_ref, s32[16,512]{1,0:T(8,128)} %touched_ref.3, bf16[16,512,1024]{2,1,0:T(8,128)(2,1)} %get-tuple-element.31.own_counts_ref, s16[16,128,3072]{2,1,0:T(8,128)(2,1)} %code.7.codes_ref, ...), custom_call_target="tpu_custom_call" | custom-call | flops 8589934592 | bytes 46137344 | tf_op jit(solution)/shard_map/update/pallas_call | solution.py:554
  (25 shorter events, 0.1 us)
Async XLA Ops:
  2.3 35.6 %copy-start.6 = (f32[128]{0:T(128)S(1)}, f32[128]{0:T(128)}, u32[]{:S(2)}) copy-start(f32[128]{0:T(128)} %param.12) | copy-start | bytes 1540
  2.3 31.5 %collective-permute-start.2 = (s32[8,8,1024]{2,1,0:T(8,128)S(1)}, s32[8,8,1024]{2,1,0:T(8,128)S(1)}, u32[]{:S(2)}, u32[]{:S(2)}) collective-permute-start(s32[8,8,1024]{2,1,0:T(8,128)S(1)} %shift-left_or_fusion), channel_id=1, source_target_pairs={{0,24},{8,16},{16,8},{24,0},{1,25},{9,17},{17,9},{25,1},{2,26},{10... | collective-permute-start | bytes 786440 | tf_op jit(solution)/shard_map/ppermute | solution.py:613
  7.3 26.5 %collective-permute-start.1 = (s32[8,8,1024]{2,1,0:T(8,128)S(1)}, s32[8,8,1024]{2,1,0:T(8,128)S(1)}, u32[]{:S(2)}, u32[]{:S(2)}) collective-permute-start(s32[8,8,1024]{2,1,0:T(8,128)S(1)} %shift-left_or_fusion), channel_id=1, source_target_pairs={{0,16},{8,24},{16,0},{24,8},{1,17},{9,25},{17,1},{25,9},{2,18},{10... | collective-permute-start | bytes 786440 | tf_op jit(solution)/shard_map/ppermute | solution.py:613
  7.3 26.5 %collective-permute-start = (s32[8,8,1024]{2,1,0:T(8,128)S(1)}, s32[8,8,1024]{2,1,0:T(8,128)S(1)}, u32[]{:S(2)}, u32[]{:S(2)}) collective-permute-start(s32[8,8,1024]{2,1,0:T(8,128)S(1)} %shift-left_or_fusion), channel_id=1, source_target_pairs={{0,8},{8,0},{16,24},{24,16},{1,9},{9,1},{17,25},{25,17},{2,10},{10... | collective-permute-start | bytes 786440 | tf_op jit(solution)/shard_map/ppermute | solution.py:613
  33.8 11.7 %copy-start.3 = (f32[128]{0:T(128)S(1)}, f32[128]{0:T(128)}, u32[]{:S(2)}) copy-start(f32[128]{0:T(128)} %param.14) | copy-start | bytes 1540
  33.8 19.8 %copy-start.2 = (s32[16,8,128]{2,1,0:T(8,128)S(1)}, s32[16,8,128]{2,1,0:T(8,128)}, u32[]{:S(2)}) copy-start(s32[16,8,128]{2,1,0:T(8,128)} %get-tuple-element.50.words_ref) | copy-start | bytes 196612
  33.9 11.6 %all-to-all-start = ((bf16[8,160,128]{2,1,0:T(8,128)(2,1)}), bf16[8,160,128]{2,1,0:T(8,128)(2,1)S(1)}, u32[]{:S(2)}, u32[]{:S(2)}) async-start(bf16[8,160,128]{2,1,0:T(8,128)(2,1)} %get-tuple-element.36), calls=%async_computation | async-start | bytes 655360 | tf_op jit(solution)/shard_map/all_to_all | solution.py:645
  38.0 0.8 copy-start.1
  45.5 2.2 %copy-start = (bf16[128,128,128]{2,1,0:T(8,128)(2,1)S(1)}, bf16[128,128,128]{2,1,0:T(8,128)(2,1)}, u32[]{:S(2)}) copy-start(bf16[128,128,128]{2,1,0:T(8,128)(2,1)} %w_ref.5) | copy-start | bytes 12582916
  49.2 9.8 %collective-permute-start.5 = (bf16[128,128]{1,0:T(8,128)(2,1)S(1)}, bf16[128,128]{1,0:T(8,128)(2,1)S(1)}, u32[]{:S(2)}, u32[]{:S(2)}) collective-permute-start(bf16[128,128]{1,0:T(8,128)(2,1)S(1)} %clip.1), channel_id=1, source_target_pairs={{0,24},{8,16},{16,8},{24,0},{1,25},{9,17},{17,9},{25,1},{2,26},{10... | collective-permute-start | bytes 98312 | tf_op jit(solution)/shard_map/ppermute | solution.py:613
  52.8 6.2 %collective-permute-start.4 = (bf16[128,128]{1,0:T(8,128)(2,1)S(1)}, bf16[128,128]{1,0:T(8,128)(2,1)S(1)}, u32[]{:S(2)}, u32[]{:S(2)}) collective-permute-start(bf16[128,128]{1,0:T(8,128)(2,1)S(1)} %clip.1), channel_id=1, source_target_pairs={{0,16},{8,24},{16,0},{24,8},{1,17},{9,25},{17,1},{25,9},{2,18},{10... | collective-permute-start | bytes 98312 | tf_op jit(solution)/shard_map/ppermute | solution.py:613
  52.8 6.2 %collective-permute-start.3 = (bf16[128,128]{1,0:T(8,128)(2,1)S(1)}, bf16[128,128]{1,0:T(8,128)(2,1)S(1)}, u32[]{:S(2)}, u32[]{:S(2)}) collective-permute-start(bf16[128,128]{1,0:T(8,128)(2,1)S(1)} %clip.1), channel_id=1, source_target_pairs={{0,8},{8,0},{16,24},{24,16},{1,9},{9,1},{17,25},{25,17},{2,10},{10... | collective-permute-start | bytes 98312 | tf_op jit(solution)/shard_map/ppermute | solution.py:613
  59.0 8.9 %collective-permute-start.8 = (bf16[4,128,128]{2,1,0:T(8,128)(2,1)S(1)}, bf16[4,128,128]{2,1,0:T(8,128)(2,1)S(1)}, u32[]{:S(2)}, u32[]{:S(2)}) collective-permute-start(bf16[4,128,128]{2,1,0:T(8,128)(2,1)S(1)} %pad_maximum_fusion.1), channel_id=1, source_target_pairs={{0,6},{1,7},{2,4},{3,5},{4,2},{5,3},{6,0},{7,1},{8,14},{9,15},{10,... | collective-permute-start | bytes 393224 | tf_op jit(solution)/shard_map/ppermute | solution.py:613
  60.6 7.3 %collective-permute-start.7 = (bf16[4,128,128]{2,1,0:T(8,128)(2,1)S(1)}, bf16[4,128,128]{2,1,0:T(8,128)(2,1)S(1)}, u32[]{:S(2)}, u32[]{:S(2)}) collective-permute-start(bf16[4,128,128]{2,1,0:T(8,128)(2,1)S(1)} %pad_maximum_fusion.1), channel_id=1, source_target_pairs={{0,4},{1,5},{2,6},{3,7},{4,0},{5,1},{6,2},{7,3},{8,12},{9,13},{10,... | collective-permute-start | bytes 393224 | tf_op jit(solution)/shard_map/ppermute | solution.py:613
  61.2 6.7 %collective-permute-start.6 = (bf16[4,128,128]{2,1,0:T(8,128)(2,1)S(1)}, bf16[4,128,128]{2,1,0:T(8,128)(2,1)S(1)}, u32[]{:S(2)}, u32[]{:S(2)}) collective-permute-start(bf16[4,128,128]{2,1,0:T(8,128)(2,1)S(1)} %pad_maximum_fusion.1), channel_id=1, source_target_pairs={{0,2},{1,3},{2,0},{3,1},{4,6},{5,7},{6,4},{7,5},{8,10},{9,11},{10,... | collective-permute-start | bytes 393224 | tf_op jit(solution)/shard_map/ppermute | solution.py:613
  68.0 5.4 %copy-start.4 = (bf16[4,4,128,128]{3,2,1,0:T(8,128)(2,1)}, bf16[4,4,128,128]{3,2,1,0:T(8,128)(2,1)S(1)}, u32[]{:S(2)}) copy-start(bf16[4,4,128,128]{3,2,1,0:T(8,128)(2,1)S(1)} %pad_maximum_fusion.near_ref) | copy-start | bytes 1572868
  68.0 5.4 %collective-permute-start.9 = (bf16[4,4,128,128]{3,2,1,0:T(8,128)(2,1)S(1)}, bf16[4,4,128,128]{3,2,1,0:T(8,128)(2,1)S(1)}, u32[]{:S(2)}, u32[]{:S(2)}) collective-permute-start(bf16[4,4,128,128]{3,2,1,0:T(8,128)(2,1)S(1)} %pad_maximum_fusion.near_ref), channel_id=1, source_target_pairs={{0,1},{1,0},{2,3},{3,2},{4,5},{5,4},{6,7},{7,6},{8,9},{9,8},{10,11... | collective-permute-start | bytes 1572872 | tf_op jit(solution)/shard_map/ppermute | solution.py:613
  73.4 0.8 copy-start.5

commit v8 on v7

--- a/solution.py
+++ b/solution.py
@@ -10,14 +10,14 @@
 CLIP = 1.0
 LEARN = 0.05
 LANES = 128
-DIGITS = 4
+DIGITS = 8
 HALF = 16
 BLOCK = 1024
 BATCH = 32
 ROWS = 512
 OWN, GROUP = range(2)
 PAIR = 2
-LISTED = 16
+LISTED = 32
 MIB = 1 << 20
 
 NT = (((1,), (1,)), ((), ()))
@@ -64,36 +64,36 @@
     word = pick_lanes(lines, ids >> 7, ids & (LANES - 1))
     upper = ids >= len(lines) * LANES
     word = jnp.where(upper, lax.shift_right_logical(word, HALF), word) & 0xFFFF
-    slots[0, :, where] = word & 0xFF
-    slots[1, :, where] = jnp.left_shift(jnp.ones_like(word), (word >> 8) & (LISTED - 1))
-
-
-def places(low):
-    shape = (low // HALF, HALF, LANES)
-    return (iota(shape, 0) * HALF + iota(shape, 1)).astype(jnp.int16)
-
-
-def tally(place, slots, where):
-    total = None
-    nothing = jnp.zeros(place.shape, jnp.int16)
-    wide = (HALF, LANES)
+    slots[0, :, where] = (word >> 3) & 7
+    slots[1, :, where] = word & 7
+    slots[2, :, where] = jnp.left_shift(jnp.ones_like(word), (word >> 8) & (LISTED - 1))
+
+
+def tally(slots, codes, where):
+    shape = (8, LANES)
+    row = iota(shape, 0)
     for hot in range(slots.shape[1]):
-        one_group = jnp.broadcast_to(slots[0, hot : hot + 1, where], wide).astype(jnp.int16)
-        one_code = jnp.broadcast_to(slots[1, hot : hot + 1, where], wide).astype(jnp.int16)
-        hit = place == jnp.broadcast_to(one_group[None], place.shape)
-        part = jnp.where(hit, jnp.broadcast_to(one_code[None], place.shape), nothing)
-        total = part if total is None else total + part
-    return total.reshape(-1, LANES)
+        high, code = (
+            jnp.broadcast_to(slots[part, hot : hot + 1, where], shape) for part in (0, 2)
+        )
+        codes[hot, :, where] = jnp.where(row == high, code, 0)
+    totals = [None] * 8
+    for hot in range(slots.shape[1]):
+        mask = jnp.where(row == jnp.broadcast_to(slots[1, hot : hot + 1, where], shape), -1, 0)
+        for high in range(8):
+            part = jnp.broadcast_to(codes[hot, high : high + 1, where], shape) & mask
+            totals[high] = part if hot == 0 else totals[high] + part
+    return jnp.concatenate(totals, axis=0)
 
 
 def spread(codes):
     parts = []
     for digit in range(DIGITS):
         if digit < DIGITS - 1:
-            part = codes & jnp.full(codes.shape, 15 << (4 * digit), jnp.int16)
+            part = codes & (15 << (4 * digit))
         else:
-            part = lax.shift_right_logical(codes, jnp.full(codes.shape, 4 * digit, jnp.int16))
-        parts.append(part.astype(jnp.bfloat16))
+            part = lax.shift_right_logical(codes, 4 * digit)
+        parts.append(part.astype(jnp.float32).astype(jnp.bfloat16))
     return jnp.concatenate(parts, axis=0)
 
 
@@ -114,6 +114,7 @@
     sums,
     same,
     slots,
+    codes,
 ):
     step = pl.program_id(0)
     rows_f, width = table_ref.shape[1:]
@@ -123,7 +124,6 @@
     hidden = w_ref.shape[2]
     blocks, tall, chunk = sums.shape
     block = min(b_group, BLOCK)
-    place = places(low)
 
     @pl.when(step == 0)
     def _():
@@ -182,9 +182,8 @@
             for side in features:
                 parts = []
                 for start in (inner, inner + chunk):
-                    parts.append(
-                        spread(tally(place, slots.at[side], slice(start, start + chunk)))
-                    )
+                    where = slice(start, start + chunk)
+                    parts.append(spread(tally(slots.at[side], codes.at[side], where)))
                 counts = jnp.concatenate(parts, axis=1)
                 where = pl.ds(pl.multiple_of(number * block + inner, 2 * chunk), 2 * chunk)
                 counts_ref[side, :, where] = counts
@@ -251,7 +250,8 @@
             scratch_shapes=[
                 pltpu.VMEM((blocks, tall, chunk), jnp.float32),
                 pltpu.VMEM((blocks, repeat_rows, chunk), jnp.float32),
-                pltpu.VMEM((PAIR, 2, hots, min(b_group, BLOCK)), jnp.int32),
+                pltpu.VMEM((PAIR, 3, hots, min(b_group, BLOCK)), jnp.int32),
+                pltpu.VMEM((PAIR, hots, 8, min(b_group, BLOCK)), jnp.int32),
             ],
         ),
         out_shape=[
@@ -271,10 +271,9 @@
 
 
 def code_kernel(words_ref, ids_ref, *rest):
-    codes_ref, slots = rest[-2:]
-    low, b_group = codes_ref.shape[1:]
+    codes_ref, slots, codes = rest[-3:]
+    b_group = codes_ref.shape[2]
     block = min(b_group, BLOCK)
-    place = places(low)
     lines = [
         [words_ref[side, number : number + 1] for number in range(words_ref.shape[1])]
         for side in range(PAIR)
@@ -290,7 +289,7 @@
             where = pl.ds(pl.multiple_of(number * block + inner, LANES), LANES)
             for side in range(PAIR):
                 codes_ref[side, :, where] = tally(
-                    place, slots.at[side], slice(inner, inner + LANES)
+                    slots.at[side], codes.at[side], slice(inner, inner + LANES)
                 )
 
     each(b_group // block, one_block)
@@ -309,12 +308,15 @@
         ]
         + [pl.BlockSpec(memory_space=pl.ANY)] * len(kept),
         out_specs=pl.BlockSpec((PAIR, low, b_group), lambda f, g: (f + start, 0, g)),
-        scratch_shapes=[pltpu.VMEM((PAIR, 2, hots, min(b_group, BLOCK)), jnp.int32)],
-        out_shape=jax.ShapeDtypeStruct((pairs * PAIR, low, others * b_group), jnp.int16),
+        scratch_shapes=[
+            pltpu.VMEM((PAIR, 3, hots, min(b_group, BLOCK)), jnp.int32),
+            pltpu.VMEM((PAIR, hots, 8, min(b_group, BLOCK)), jnp.int32),
+        ],
+        out_shape=jax.ShapeDtypeStruct((pairs * PAIR, low, others * b_group), jnp.int32),
         input_output_aliases={2: 0} if kept else {},
         compiler_params=pltpu.CompilerParams(vmem_limit_bytes=48 * MIB),
         cost_estimate=pl.CostEstimate(
-            flops=size * 400, bytes_accessed=size * 2, transcendentals=0
+            flops=size * 800, bytes_accessed=size * 4, transcendentals=0
         ),
         name="code",
     )(words, packed, *kept)
@@ -486,7 +488,8 @@
         ]
         words = words_ref[side]
         for half, word in enumerate((words & 0xFFFF, lax.shift_right_logical(words, HALF))):
-            gain = pick_lanes(extra, (word >> 10) & (DIGITS - 1), word & (LANES - 1))
+            digit = (word >> 10) & (DIGITS - 1)
+            gain = pick_lanes(extra, digit >> 1, (word & 63) + ((digit & 1) << 6))
             gain = jnp.where((word >> 8) >= LISTED, gain, 0.0)
             for number in range(words.shape[0]):
                 place = half * words.shape[0] + number

time: 119 us -> 117 us (0.983)
  Pallas kernels: 92.9 us -> 90.3 us
    pallas_call x4, Pallas kernels: 21.3 us -> 18.7 us  [code_counts(): pl.pallas_call(code_kernel, grid=(stop - start, others), in_specs=[pl.Blo...]
  transfers between devices with their start and end apart: 11 -> 11, of which waited for: 1 -> 1; matrix products, arithmetic and copies ran while one was open for 0% -> 0% of each run, Pallas kernels for 40% -> 38%
where the time goes in v8:
time: 117 us
  Pallas kernels  90.3 us (77%)
  starting transfers between devices  17.7 us (15%)
  local copies, waits for them, and re-layouts  3.97 us (3%)
  waiting for transfers between devices  2.04 us (2%)
  other arithmetic  1.78 us (2%)
    pallas_call x1, Pallas kernels, update_rows(): pl.pallas_call(update_kernel, grid_spec=pltpu.PrefetchScalarGridSpec(num_...  44 us
    pallas_call x1, Pallas kernels, pool(): pl.pallas_call(pool_kernel, grid_spec=pltpu.PrefetchScalarGridSpec(num_sc...  26.1 us
    pallas_call x4, Pallas kernels, code_counts(): pl.pallas_call(code_kernel, grid=(stop - start, others), in_specs=[pl.Blo...  18.7 us
    ppermute x10, starting transfers between devices, swap(): return lax.ppermute(array, axis, [(i, i ^ apart) for i in range(size)])  13.7 us
    all_to_all x1, starting transfers between devices, body(): lax.all_to_all(sent, 'table', split_axis=0, concat_axis=0, tiled=True)  3.96 us
    unnamed x14, local copies, waits for them, and re-layouts  3.85 us
  transfers between devices with their start and end apart: 11, of which 1 were waited for; matrix products, arithmetic and copies ran while one was open for 0% of the time, Pallas kernels for 38%

profile of v8, /device:TPU:0, one launch (start us, length us, event | category | flops | bytes accessed | tf_op | source)
XLA Modules:
  0.0 116.7 jit_solution(5137576713435955472)
XLA Ops:
  0.6 1.1 shift-left_or_fusion
  1.7 0.6 pad_add_fusion.1.place_ref
  2.3 5.0 %collective-permute-start.2 = (s32[8,8,1024]{2,1,0:T(8,128)S(1)}, s32[8,8,1024]{2,1,0:T(8,128)S(1)}, u32[]{:S(2)}, u32[]{:S(2)}) collective-permute-start(s32[8,8,1024]{2,1,0:T(8,128)S(1)} %shift-left_or_fusion), channel_id=1, source_target_pairs={{0,24},{8,16},{16,8},{24,0},{1,25},{9,17},{17,9},{25,1},{2,26},{10... | collective-permute-start | bytes 786440 | tf_op jit(solution)/shard_map/ppermute | solution.py:616
  7.3 0.6 collective-permute-start
  7.9 26.1 %pool.1 = (bf16[8,160,128]{2,1,0:T(8,128)(2,1)}, bf16[16,128,512]{2,1,0:T(8,128)(2,1)}, s32[16,8,128]{2,1,0:T(8,128)}, bf16[16,512,1024]{2,1,0:T(8,128)(2,1)}) custom-call(s32[2]{0:T(128)} %pad_add_fusion.1.place_ref, f32[16,2048,128]{2,1,0:T(8,128)} %table_ref.3, s32[16,512]{1,0:T(8,128)} %touched_ref.3, s32[16,8,1024]{2,1,0:T(8,128)} %ids_ref, ...), custom_call_target="tpu_custom_call" | custom-call | flops 17179869184 | bytes 16777216 | tf_op jit(solution)/shard_map/pool/pallas_call | solution.py:233
  34.1 4.0 %all-to-all-start = ((bf16[8,160,128]{2,1,0:T(8,128)(2,1)}), bf16[8,160,128]{2,1,0:T(8,128)(2,1)S(1)}, u32[]{:S(2)}, u32[]{:S(2)}) async-start(bf16[8,160,128]{2,1,0:T(8,128)(2,1)} %get-tuple-element.36), calls=%async_computation | async-start | bytes 655360 | tf_op jit(solution)/shard_map/all_to_all | solution.py:648
  38.1 0.1 copy.15.w_out_ref
  38.2 0.8 copy-done.1
  39.0 4.7 %code.4.rest_0_ = s32[16,64,3072]{2,1,0:T(8,128)} custom-call(s32[16,8,128]{2,1,0:T(8,128)S(1)} %copy-done.1, s32[3,8,8,1024]{3,2,1,0:T(8,128)S(1)} %pad_add_fusion.ids_ref), custom_call_target="tpu_custom_call" | custom-call | flops 629145600 | bytes 3145728 | tf_op jit(solution)/shard_map/code/pallas_call | solution.py:302
  43.7 2.0 %all-to-all-done.sent_ref = bf16[8,160,128]{2,1,0:T(8,128)(2,1)S(1)} async-done(((bf16[8,160,128]{2,1,0:T(8,128)(2,1)}), bf16[8,160,128]{2,1,0:T(8,128)(2,1)S(1)}, u32[]{:S(2)}, u32[]{:S(2)}) %all-to-all-start) | async-done | bytes 327712 | tf_op jit(solution)/shard_map/all_to_all | solution.py:648
  45.7 2.2 %copy-done = bf16[128,128,128]{2,1,0:T(8,128)(2,1)S(1)} copy-done((bf16[128,128,128]{2,1,0:T(8,128)(2,1)S(1)}, bf16[128,128,128]{2,1,0:T(8,128)(2,1)}, u32[]{:S(2)}) %copy-start) | copy-done | bytes 4194328
  47.9 1.5 %clip.1 = bf16[128,128]{1,0:T(8,128)(2,1)S(1)} custom-call(f32[128,1]{1,0:T(8,128)S(1)} %copy.15.w_out_ref, f32[1,128]{1,0:T(1,128)S(1)} %bitcast.16, bf16[128,128,128]{2,1,0:T(8,128)(2,1)S(1)} %copy-done, bf16[8,160,128]{2,1,0:T(8,128)(2,1)S(1)} %all-to-all-done.sent_ref), custom_call_target="tpu_custom_call" | custom-call | flops 536870912 | bytes 4194304 | tf_op jit(solution)/shard_map/clip/pallas_call | solution.py:361
  49.4 3.7 %collective-permute-start.5 = (bf16[128,128]{1,0:T(8,128)(2,1)S(1)}, bf16[128,128]{1,0:T(8,128)(2,1)S(1)}, u32[]{:S(2)}, u32[]{:S(2)}) collective-permute-start(bf16[128,128]{1,0:T(8,128)(2,1)S(1)} %clip.1), channel_id=1, source_target_pairs={{0,24},{8,16},{16,8},{24,0},{1,25},{9,17},{17,9},{25,1},{2,26},{10... | collective-permute-start | bytes 98312 | tf_op jit(solution)/shard_map/ppermute | solution.py:616
  53.0 0.8 collective-permute-start.3
  53.8 4.7 %code.5.rest_0_ = s32[16,64,3072]{2,1,0:T(8,128)} custom-call(s32[16,8,128]{2,1,0:T(8,128)S(1)} %copy-done.2, s32[3,8,8,1024]{3,2,1,0:T(8,128)S(1)} %pad_add_fusion.ids_ref, s32[16,64,3072]{2,1,0:T(8,128)} %code.4.rest_0_), custom_call_target="tpu_custom_call", output_to_operand_aliasing={{}: (2, {})} | custom-call | flops 629145600 | bytes 3145728 | tf_op jit(solution)/shard_map/code/pallas_call | solution.py:302
  58.5 1.0 collective-permute-start.8
  59.5 1.1 collective-permute-start.7
  60.6 1.5 %collective-permute-start.6 = (bf16[4,128,128]{2,1,0:T(8,128)(2,1)S(1)}, bf16[4,128,128]{2,1,0:T(8,128)(2,1)S(1)}, u32[]{:S(2)}, u32[]{:S(2)}) collective-permute-start(bf16[4,128,128]{2,1,0:T(8,128)(2,1)S(1)} %pad_maximum_fusion.1), channel_id=1, source_target_pairs={{0,2},{1,3},{2,0},{3,1},{4,6},{5,7},{6,4},{7,5},{8,10},{9,11},{10,... | collective-permute-start | bytes 393224 | tf_op jit(solution)/shard_map/ppermute | solution.py:616
  62.1 4.7 %code.6.rest_0_ = s32[16,64,3072]{2,1,0:T(8,128)} custom-call(s32[16,8,128]{2,1,0:T(8,128)S(1)} %copy-done.2, s32[3,8,8,1024]{3,2,1,0:T(8,128)S(1)} %pad_add_fusion.ids_ref, s32[16,64,3072]{2,1,0:T(8,128)} %code.5.rest_0_), custom_call_target="tpu_custom_call", output_to_operand_aliasing={{}: (2, {})} | custom-call | flops 629145600 | bytes 3145728 | tf_op jit(solution)/shard_map/code/pallas_call | solution.py:302
  66.8 0.1 pad_maximum_fusion.near_ref
  66.9 0.1 collective-permute-start.9
  67.0 4.7 %code.7.codes_ref = s32[16,64,3072]{2,1,0:T(8,128)} custom-call(s32[16,8,128]{2,1,0:T(8,128)S(1)} %copy-done.2, s32[3,8,8,1024]{3,2,1,0:T(8,128)S(1)} %pad_add_fusion.ids_ref, s32[16,64,3072]{2,1,0:T(8,128)} %code.6.rest_0_), custom_call_target="tpu_custom_call", output_to_operand_aliasing={{}: (2, {})} | custom-call | flops 629145600 | bytes 3145728 | tf_op jit(solution)/shard_map/code/pallas_call | solution.py:302
  71.7 0.8 copy-done.5
  72.5 44.0 %update.1 = (f32[16,2048,128]{2,1,0:T(8,128)}, f32[16,2048]{1,0:T(8,128)}, f32[16,32,128]{2,1,0:T(8,128)}) custom-call(s32[2]{0:T(128)} %pad_add_fusion.1.place_ref, s32[16,512]{1,0:T(8,128)} %touched_ref.3, bf16[16,512,1024]{2,1,0:T(8,128)(2,1)} %get-tuple-element.31.own_counts_ref, s32[16,64,3072]{2,1,0:T(8,128)} %code.7.codes_ref, ...), custom_call_target="tpu_custom_call" | custom-call | flops 8589934592 | bytes 39845888 | tf_op jit(solution)/shard_map/update/pallas_call | solution.py:557
  (25 shorter events, 0.1 us)
Async XLA Ops:
  2.3 35.8 %copy-start.6 = (f32[128]{0:T(128)S(1)}, f32[128]{0:T(128)}, u32[]{:S(2)}) copy-start(f32[128]{0:T(128)} %param.12) | copy-start | bytes 1540
  2.3 31.7 %collective-permute-start.2 = (s32[8,8,1024]{2,1,0:T(8,128)S(1)}, s32[8,8,1024]{2,1,0:T(8,128)S(1)}, u32[]{:S(2)}, u32[]{:S(2)}) collective-permute-start(s32[8,8,1024]{2,1,0:T(8,128)S(1)} %shift-left_or_fusion), channel_id=1, source_target_pairs={{0,24},{8,16},{16,8},{24,0},{1,25},{9,17},{17,9},{25,1},{2,26},{10... | collective-permute-start | bytes 786440 | tf_op jit(solution)/shard_map/ppermute | solution.py:616
  7.3 26.7 %collective-permute-start.1 = (s32[8,8,1024]{2,1,0:T(8,128)S(1)}, s32[8,8,1024]{2,1,0:T(8,128)S(1)}, u32[]{:S(2)}, u32[]{:S(2)}) collective-permute-start(s32[8,8,1024]{2,1,0:T(8,128)S(1)} %shift-left_or_fusion), channel_id=1, source_target_pairs={{0,16},{8,24},{16,0},{24,8},{1,17},{9,25},{17,1},{25,9},{2,18},{10... | collective-permute-start | bytes 786440 | tf_op jit(solution)/shard_map/ppermute | solution.py:616
  7.3 26.7 %collective-permute-start = (s32[8,8,1024]{2,1,0:T(8,128)S(1)}, s32[8,8,1024]{2,1,0:T(8,128)S(1)}, u32[]{:S(2)}, u32[]{:S(2)}) collective-permute-start(s32[8,8,1024]{2,1,0:T(8,128)S(1)} %shift-left_or_fusion), channel_id=1, source_target_pairs={{0,8},{8,0},{16,24},{24,16},{1,9},{9,1},{17,25},{25,17},{2,10},{10... | collective-permute-start | bytes 786440 | tf_op jit(solution)/shard_map/ppermute | solution.py:616
  34.0 11.7 %copy-start.3 = (f32[128]{0:T(128)S(1)}, f32[128]{0:T(128)}, u32[]{:S(2)}) copy-start(f32[128]{0:T(128)} %param.14) | copy-start | bytes 1540
  34.0 19.8 %copy-start.2 = (s32[16,8,128]{2,1,0:T(8,128)S(1)}, s32[16,8,128]{2,1,0:T(8,128)}, u32[]{:S(2)}) copy-start(s32[16,8,128]{2,1,0:T(8,128)} %get-tuple-element.50.words_ref) | copy-start | bytes 196612
  34.1 11.6 %all-to-all-start = ((bf16[8,160,128]{2,1,0:T(8,128)(2,1)}), bf16[8,160,128]{2,1,0:T(8,128)(2,1)S(1)}, u32[]{:S(2)}, u32[]{:S(2)}) async-start(bf16[8,160,128]{2,1,0:T(8,128)(2,1)} %get-tuple-element.36), calls=%async_computation | async-start | bytes 655360 | tf_op jit(solution)/shard_map/all_to_all | solution.py:648
  38.2 0.8 copy-start.1
  45.7 2.2 %copy-start = (bf16[128,128,128]{2,1,0:T(8,128)(2,1)S(1)}, bf16[128,128,128]{2,1,0:T(8,128)(2,1)}, u32[]{:S(2)}) copy-start(bf16[128,128,128]{2,1,0:T(8,128)(2,1)} %w_ref.5) | copy-start | bytes 12582916
  49.4 9.1 %collective-permute-start.5 = (bf16[128,128]{1,0:T(8,128)(2,1)S(1)}, bf16[128,128]{1,0:T(8,128)(2,1)S(1)}, u32[]{:S(2)}, u32[]{:S(2)}) collective-permute-start(bf16[128,128]{1,0:T(8,128)(2,1)S(1)} %clip.1), channel_id=1, source_target_pairs={{0,24},{8,16},{16,8},{24,0},{1,25},{9,17},{17,9},{25,1},{2,26},{10... | collective-permute-start | bytes 98312 | tf_op jit(solution)/shard_map/ppermute | solution.py:616
  53.0 5.5 %collective-permute-start.4 = (bf16[128,128]{1,0:T(8,128)(2,1)S(1)}, bf16[128,128]{1,0:T(8,128)(2,1)S(1)}, u32[]{:S(2)}, u32[]{:S(2)}) collective-permute-start(bf16[128,128]{1,0:T(8,128)(2,1)S(1)} %clip.1), channel_id=1, source_target_pairs={{0,16},{8,24},{16,0},{24,8},{1,17},{9,25},{17,1},{25,9},{2,18},{10... | collective-permute-start | bytes 98312 | tf_op jit(solution)/shard_map/ppermute | solution.py:616
  53.0 5.5 %collective-permute-start.3 = (bf16[128,128]{1,0:T(8,128)(2,1)S(1)}, bf16[128,128]{1,0:T(8,128)(2,1)S(1)}, u32[]{:S(2)}, u32[]{:S(2)}) collective-permute-start(bf16[128,128]{1,0:T(8,128)(2,1)S(1)} %clip.1), channel_id=1, source_target_pairs={{0,8},{8,0},{16,24},{24,16},{1,9},{9,1},{17,25},{25,17},{2,10},{10... | collective-permute-start | bytes 98312 | tf_op jit(solution)/shard_map/ppermute | solution.py:616
  58.5 8.3 %collective-permute-start.8 = (bf16[4,128,128]{2,1,0:T(8,128)(2,1)S(1)}, bf16[4,128,128]{2,1,0:T(8,128)(2,1)S(1)}, u32[]{:S(2)}, u32[]{:S(2)}) collective-permute-start(bf16[4,128,128]{2,1,0:T(8,128)(2,1)S(1)} %pad_maximum_fusion.1), channel_id=1, source_target_pairs={{0,6},{1,7},{2,4},{3,5},{4,2},{5,3},{6,0},{7,1},{8,14},{9,15},{10,... | collective-permute-start | bytes 393224 | tf_op jit(solution)/shard_map/ppermute | solution.py:616
  59.5 7.3 %collective-permute-start.7 = (bf16[4,128,128]{2,1,0:T(8,128)(2,1)S(1)}, bf16[4,128,128]{2,1,0:T(8,128)(2,1)S(1)}, u32[]{:S(2)}, u32[]{:S(2)}) collective-permute-start(bf16[4,128,128]{2,1,0:T(8,128)(2,1)S(1)} %pad_maximum_fusion.1), channel_id=1, source_target_pairs={{0,4},{1,5},{2,6},{3,7},{4,0},{5,1},{6,2},{7,3},{8,12},{9,13},{10,... | collective-permute-start | bytes 393224 | tf_op jit(solution)/shard_map/ppermute | solution.py:616
  60.6 6.2 %collective-permute-start.6 = (bf16[4,128,128]{2,1,0:T(8,128)(2,1)S(1)}, bf16[4,128,128]{2,1,0:T(8,128)(2,1)S(1)}, u32[]{:S(2)}, u32[]{:S(2)}) collective-permute-start(bf16[4,128,128]{2,1,0:T(8,128)(2,1)S(1)} %pad_maximum_fusion.1), channel_id=1, source_target_pairs={{0,2},{1,3},{2,0},{3,1},{4,6},{5,7},{6,4},{7,5},{8,10},{9,11},{10,... | collective-permute-start | bytes 393224 | tf_op jit(solution)/shard_map/ppermute | solution.py:616
  66.9 4.8 %copy-start.4 = (bf16[4,4,128,128]{3,2,1,0:T(8,128)(2,1)}, bf16[4,4,128,128]{3,2,1,0:T(8,128)(2,1)S(1)}, u32[]{:S(2)}) copy-start(bf16[4,4,128,128]{3,2,1,0:T(8,128)(2,1)S(1)} %pad_maximum_fusion.near_ref) | copy-start | bytes 1572868
  66.9 4.8 %collective-permute-start.9 = (bf16[4,4,128,128]{3,2,1,0:T(8,128)(2,1)S(1)}, bf16[4,4,128,128]{3,2,1,0:T(8,128)(2,1)S(1)}, u32[]{:S(2)}, u32[]{:S(2)}) collective-permute-start(bf16[4,4,128,128]{3,2,1,0:T(8,128)(2,1)S(1)} %pad_maximum_fusion.near_ref), channel_id=1, source_target_pairs={{0,1},{1,0},{2,3},{3,2},{4,5},{5,4},{6,7},{7,6},{8,9},{9,8},{10,11... | collective-permute-start | bytes 1572872 | tf_op jit(solution)/shard_map/ppermute | solution.py:616
  71.7 0.8 copy-start.5
